TPU v7x, 32 devices: a whole 2x2x4 slice. The times are simulated.
32 devices in a mesh: dp: 16 (over z, x, core), tensor: 2 (over y).
Axes of the slice: x: 2, y: 2, z: 4, core: 2. Of those that a mesh axis runs over, the one named last changes fastest.
Arguments:
- tokens: bfloat16 [32, 1024, 768], P(None, 'dp'), may hold values from -6 to 6
- cotangent: bfloat16 [32, 1024, 768], P(None, 'dp'), may hold values from -6 to 6
- landmark_ids: int32 [32, 1024], replicated, may hold values from 0 to 64, as said below
- w_query: bfloat16 [768, 768], P('dp', 'tensor')
- w_key: bfloat16 [768, 768], P('dp', 'tensor')
- w_value: bfloat16 [768, 768], P('dp', 'tensor'), may hold values from -0.21875 to 0.21875
- b_query: bfloat16 [768], P('tensor'), may hold values from -3 to 3
- b_value: bfloat16 [768], P('tensor'), may hold values from -3 to 3
- conv_taps: bfloat16 [12, 33], P('tensor'), may hold values from -1 to 1
- w_out: bfloat16 [768, 768], P('dp', 'tensor'), may hold values from -0.3125 to 0.3125
- b_out: bfloat16 [768], replicated, may hold values from -2 to 2
- first_gain: bfloat16 [768], replicated, may hold values from 0.5 to 1.5
- first_shift: bfloat16 [768], replicated, may hold values from -2 to 2
- w_inner: bfloat16 [768, 3072], P('dp', 'tensor'), may hold values from -0.21875 to 0.21875
- b_inner: bfloat16 [3072], P('tensor'), may hold values from -2 to 2
- w_outer: bfloat16 [768, 3072], P('dp', 'tensor'), may hold values from -0.109375 to 0.109375
- b_outer: bfloat16 [768], replicated, may hold values from -2 to 2
- second_gain: bfloat16 [768], replicated, may hold values from 0.5 to 1.5
- second_shift: bfloat16 [768], replicated, may hold values from -2 to 2
Outputs:
- layer_out: bfloat16 [32, 1024, 768], P(None, 'dp')
- grad_tokens: bfloat16 [32, 1024, 768], P(None, 'dp')
- grad_w_query: float32 [768, 768], P('dp', 'tensor')
- grad_w_key: float32 [768, 768], P('dp', 'tensor')
- grad_w_value: float32 [768, 768], P('dp', 'tensor')
- grad_b_query: float32 [768], P('tensor')
- grad_b_value: float32 [768], P('tensor')
- grad_conv_taps: float32 [12, 33], P('tensor')
- grad_w_out: float32 [768, 768], P('dp', 'tensor')
- grad_b_out: float32 [768], P('dp')
- grad_first_gain: float32 [768], P('dp')
- grad_first_shift: float32 [768], P('dp')
- grad_w_inner: float32 [768, 3072], P('dp', 'tensor')
- grad_b_inner: float32 [3072], P('tensor')
- grad_w_outer: float32 [768, 3072], P('dp', 'tensor')
- grad_b_outer: float32 [768], P('dp')
- grad_second_gain: float32 [768], P('dp')
- grad_second_shift: float32 [768], P('dp')
Inputs may be any that keep to these rules, and one draw needn't show every extreme that they name: `landmark_ids`: along a sequence the ids never fall, every id below 64 occurs in every sequence, and ids equal to 64 fill the end of a sequence; one sequence has none of them.
All inputs are finite; a program needn't handle non-finite values.
Results may differ from a plain program's by a relative error of at most 0.025.
Values may be sent and summed in bfloat16 or wider, within the bound.
A program may use at most 320 MiB of HBM per device.

v0:
```python
import jax
import jax.numpy as jnp
from jax import lax
from jax.sharding import PartitionSpec as P

LAND = 64
ITERS = 6


def contract_dims(spec, left, right):
    return jnp.einsum(spec, left, right, precision=lax.Precision.HIGHEST)


def partial_product(spec, left, right):
    return jnp.einsum(spec, left, right, preferred_element_type=jnp.float32)


def layer_norm(rows, gain, shift):
    center = rows - jnp.mean(rows, axis=-1, keepdims=True)
    spread = jnp.mean(center * center, axis=-1, keepdims=True)
    return center * lax.rsqrt(spread + 1e-05) * gain + shift


def exact_gelu(values):
    return jax.nn.gelu(values, approximate=False)


def depthwise(values, taps):
    width = taps.shape[1]
    reach = width // 2
    length = values.shape[0]
    padded = jnp.pad(values, ((reach, reach), (0, 0), (0, 0)))
    total = jnp.zeros_like(values)
    for offset in range(width):
        total = total + taps[:, offset][None, :, None] * padded[offset : offset + length]
    return total


def pseudo_inverse(kernel_matrix):
    extent = kernel_matrix.shape[-1]
    identity = jnp.eye(extent, dtype=jnp.float32)
    total = jnp.sum(kernel_matrix * kernel_matrix, axis=(1, 2), keepdims=True)
    approx = jnp.swapaxes(kernel_matrix, 1, 2) / total
    for step in range(ITERS):
        applied = contract_dims("hij,hjk->hik", kernel_matrix, approx)
        inner = 7.0 * identity - applied
        inner = 15.0 * identity - contract_dims("hij,hjk->hik", applied, inner)
        inner = 13.0 * identity - contract_dims("hij,hjk->hik", applied, inner)
        approx = 0.25 * contract_dims("hij,hjk->hik", approx, inner)
    return approx


def softmax_back(probs, grad, reduce_axis):
    return probs * (grad - jnp.sum(probs * grad, axis=reduce_axis, keepdims=True))


def sequence_step(rows, cot_rows, seg_ids, weights):
    (
        w_query,
        w_key,
        w_value,
        b_query,
        b_value,
        conv_taps,
        w_out,
        b_out,
        first_gain,
        first_shift,
        w_inner,
        b_inner,
        w_outer,
        b_outer,
        second_gain,
        second_shift,
    ) = weights
    single_float = jnp.float32
    reduced_dtype = jnp.bfloat16
    length = rows.shape[0]
    heads = conv_taps.shape[0]
    column_count = w_query.shape[1]
    head_dim = column_count // heads
    scale = head_dim ** (-0.25)
    rows_f = rows.astype(single_float)
    valid = seg_ids < LAND
    compare = seg_ids[None, :] == jnp.arange(LAND, dtype=jnp.int32)[:, None]
    member_mask = compare.astype(reduced_dtype)
    valid_count = jnp.sum(compare.astype(single_float), axis=1)[:, None, None]
    queries = (
        (jnp.dot(rows, w_query, preferred_element_type=single_float) + b_query.astype(single_float))
        * scale
    ).astype(reduced_dtype)
    keys_all = (jnp.dot(rows, w_key, preferred_element_type=single_float) * scale).astype(
        reduced_dtype
    )
    values_all = (
        jnp.dot(rows, w_value, preferred_element_type=single_float) + b_value.astype(single_float)
    ).astype(reduced_dtype)
    query_head_rows = queries.reshape(length, heads, head_dim)
    key_head_rows = keys_all.reshape(length, heads, head_dim)
    value_head_rows = values_all.reshape(length, heads, head_dim)
    landmark_queries_mean = (
        partial_product("gf,fwa->gwa", member_mask, query_head_rows) / valid_count
    ).astype(reduced_dtype)
    landmark_keys_mean = (
        partial_product("gf,fwa->gwa", member_mask, key_head_rows) / valid_count
    ).astype(reduced_dtype)
    near_block_float = jax.nn.softmax(
        partial_product("uow,qow->oqu", query_head_rows, landmark_keys_mean), axis=1
    )
    near_block = near_block_float.astype(reduced_dtype)
    kernel_matrix = jax.nn.softmax(
        partial_product("yoq,uoq->oyu", landmark_queries_mean, landmark_keys_mean), axis=2
    )
    inverse_matrix, inverse_back = jax.vjp(pseudo_inverse, kernel_matrix)
    third_factor = partial_product("zwp,owp->wzo", landmark_queries_mean, key_head_rows)
    third_factor = jnp.where(valid[None, None, :], third_factor, -1e30)
    far_f = jax.nn.softmax(third_factor, axis=2)
    far_block = far_f.astype(reduced_dtype)
    summary_matrix = partial_product("zyj,jzt->zyt", far_block, value_head_rows)
    mixed_heads = contract_dims("gfv,gvx->gfx", inverse_matrix, summary_matrix).astype(
        reduced_dtype
    )
    attended_rows = partial_product("azr,azs->ras", near_block, mixed_heads)
    masked = jnp.where(valid[:, None, None], value_head_rows.astype(single_float), 0.0)
    conv_out, conv_back = jax.vjp(depthwise, masked, conv_taps.astype(single_float))
    context = (attended_rows + conv_out).astype(reduced_dtype).reshape(length, column_count)
    attn_part = partial_product("nc,dc->nd", context, w_out)
    attn_out = lax.psum(attn_part.astype(jnp.bfloat16), "tensor").astype(
        jnp.float32
    ) + b_out.astype(single_float)
    hidden, first_norm_back = jax.vjp(
        layer_norm,
        rows_f + attn_out,
        first_gain.astype(single_float),
        first_shift.astype(single_float),
    )
    hidden_low = hidden.astype(reduced_dtype)
    inner = jnp.dot(hidden_low, w_inner, preferred_element_type=single_float) + b_inner.astype(
        single_float
    )
    active_f, gelu_back = jax.vjp(exact_gelu, inner)
    active = active_f.astype(reduced_dtype)
    ffn_part = partial_product("nf,df->nd", active, w_outer)
    ffn_out = lax.psum(ffn_part.astype(jnp.bfloat16), "tensor").astype(
        jnp.float32
    ) + b_outer.astype(single_float)
    result, second_norm_back = jax.vjp(
        layer_norm,
        hidden + ffn_out,
        second_gain.astype(single_float),
        second_shift.astype(single_float),
    )
    out_rows = result.astype(reduced_dtype)
    grad_second, grad_second_gain, grad_second_shift = second_norm_back(
        cot_rows.astype(single_float)
    )
    grad_b_outer = jnp.sum(grad_second, axis=0)
    grad_ffn = grad_second.astype(reduced_dtype)
    grad_w_outer = partial_product("nd,nf->df", grad_ffn, active)
    grad_active = partial_product("nd,df->nf", grad_ffn, w_outer)
    (grad_inner,) = gelu_back(grad_active)
    grad_b_inner = jnp.sum(grad_inner, axis=0)
    grad_inner_low = grad_inner.astype(reduced_dtype)
    grad_w_inner = partial_product("nd,nf->df", hidden_low, grad_inner_low)
    hidden_part = partial_product("nf,df->nd", grad_inner_low, w_inner)
    grad_hidden = grad_second + lax.psum(hidden_part.astype(jnp.bfloat16), "tensor").astype(
        jnp.float32
    )
    grad_first, grad_first_gain, grad_first_shift = first_norm_back(grad_hidden)
    grad_b_out = jnp.sum(grad_first, axis=0)
    grad_attn = grad_first.astype(reduced_dtype)
    grad_w_out = partial_product("nd,nc->dc", grad_attn, context)
    context_gradient = (
        partial_product("nd,dc->nc", grad_attn, w_out)
        .astype(reduced_dtype)
        .reshape(length, heads, head_dim)
    )
    grad_masked, grad_taps = conv_back(context_gradient.astype(single_float))
    values_gradient = jnp.where(valid[:, None, None], grad_masked, 0.0)
    near_block_gradient = partial_product("erl,ryl->rye", context_gradient, mixed_heads)
    mixed_gradient = partial_product("zyj,jzt->zyt", near_block, context_gradient)
    first_scores_gradient = softmax_back(near_block_float, near_block_gradient, 1).astype(
        reduced_dtype
    )
    queries_gradient = partial_product("uba,buo->auo", first_scores_gradient, landmark_keys_mean)
    landmark_key_gradient = partial_product("sjw,wsu->jsu", first_scores_gradient, query_head_rows)
    summary_gradient = contract_dims("sqe,sqg->seg", inverse_matrix, mixed_gradient).astype(
        reduced_dtype
    )
    inverse_gradient = contract_dims("lcp,lzp->lcz", mixed_gradient, summary_matrix)
    far_block_gradient = partial_product("byl,sbl->bys", summary_gradient, value_head_rows)
    values_gradient = values_gradient + partial_product("azr,azs->ras", far_block, summary_gradient)
    third_factor_gradient = softmax_back(far_f, far_block_gradient, 2).astype(reduced_dtype)
    landmark_query_gradient = partial_product("sjw,wsu->jsu", third_factor_gradient, key_head_rows)
    keys_gradient = partial_product("uba,buo->auo", third_factor_gradient, landmark_queries_mean)
    (grad_kernel,) = inverse_back(inverse_gradient)
    middle_gradient = softmax_back(kernel_matrix, grad_kernel, 2)
    landmark_query_gradient = landmark_query_gradient + contract_dims(
        "tiz,ztn->itn", middle_gradient, landmark_keys_mean.astype(single_float)
    )
    landmark_key_gradient = landmark_key_gradient + contract_dims(
        "xql,qxb->lxb", middle_gradient, landmark_queries_mean.astype(single_float)
    )
    queries_gradient = queries_gradient + partial_product(
        "wf,wqb->fqb", member_mask, (landmark_query_gradient / valid_count).astype(reduced_dtype)
    )
    keys_gradient = keys_gradient + partial_product(
        "wf,wqb->fqb", member_mask, (landmark_key_gradient / valid_count).astype(reduced_dtype)
    )
    queries_gradient = queries_gradient.reshape(length, column_count) * scale
    values_gradient = values_gradient.reshape(length, column_count)
    grad_b_query = jnp.sum(queries_gradient, axis=0)
    grad_b_value = jnp.sum(values_gradient, axis=0)
    pre_query = queries_gradient.astype(reduced_dtype)
    pre_key = (keys_gradient.reshape(length, column_count) * scale).astype(reduced_dtype)
    pre_value = values_gradient.astype(reduced_dtype)
    grad_w_query = partial_product("nd,nc->dc", rows, pre_query)
    grad_w_key = partial_product("nd,nc->dc", rows, pre_key)
    grad_w_value = partial_product("nd,nc->dc", rows, pre_value)
    token_part = (
        partial_product("nc,dc->nd", pre_query, w_query)
        + partial_product("nc,dc->nd", pre_key, w_key)
        + partial_product("nc,dc->nd", pre_value, w_value)
    )
    grad_rows = (
        grad_first + lax.psum(token_part.astype(jnp.bfloat16), "tensor").astype(jnp.float32)
    ).astype(reduced_dtype)
    grads = (
        grad_w_query,
        grad_w_key,
        grad_w_value,
        grad_b_query,
        grad_b_value,
        grad_taps,
        grad_w_out,
        grad_b_out,
        grad_first_gain,
        grad_first_shift,
        grad_w_inner,
        grad_b_inner,
        grad_w_outer,
        grad_b_outer,
        grad_second_gain,
        grad_second_shift,
    )
    return (out_rows, grad_rows, grads)


def dealing(landmark_ids, groups, seq_here):
    total_seqs = landmark_ids.shape[0]
    seq_lengths = jnp.sum((landmark_ids < LAND).astype(jnp.int32), axis=1)
    places = jnp.arange(total_seqs, dtype=jnp.int32)
    scores = seq_lengths * total_seqs + places
    ordered = jnp.argsort(-scores, stable=True)
    owners = places // seq_here
    within = places % seq_here
    ranked = within * groups + jnp.where(within % 2 == 0, owners, groups - 1 - owners)
    return jnp.take(ordered, ranked, axis=0)


def local(
    tokens,
    cotangent,
    landmark_ids,
    w_query,
    w_key,
    w_value,
    b_query,
    b_value,
    conv_taps,
    w_out,
    b_out,
    first_gain,
    first_shift,
    w_inner,
    b_inner,
    w_outer,
    b_outer,
    second_gain,
    second_shift,
):
    groups = lax.axis_size("dp")
    seq_here = tokens.shape[0] // groups
    deal_order = dealing(landmark_ids, groups, seq_here)
    arranged_rows = jnp.take(tokens, deal_order, axis=0)
    arranged_cot = jnp.take(cotangent, deal_order, axis=0)
    dealt_rows, dealt_cot = (
        lax.all_to_all(arranged_rows, "dp", split_axis=0, concat_axis=1, tiled=True),
        lax.all_to_all(arranged_cot, "dp", split_axis=0, concat_axis=1, tiled=True),
    )
    own_seqs = lax.dynamic_slice_in_dim(deal_order, lax.axis_index("dp") * seq_here, seq_here, 0)
    ids_here = jnp.take(landmark_ids, own_seqs, axis=0)

    def assemble(matrices):
        return (
            matrices[0],
            matrices[1],
            matrices[2],
            b_query,
            b_value,
            conv_taps,
            matrices[3],
            b_out,
            first_gain,
            first_shift,
            matrices[4],
            b_inner,
            matrices[5],
            b_outer,
            second_gain,
            second_shift,
        )

    def current_weights():
        return assemble(
            (
                lax.all_gather(w_query, "dp", axis=0, tiled=True),
                lax.all_gather(w_key, "dp", axis=0, tiled=True),
                lax.all_gather(w_value, "dp", axis=0, tiled=True),
                lax.all_gather(w_out, "dp", axis=0, tiled=True),
                lax.all_gather(w_inner, "dp", axis=0, tiled=True),
                lax.all_gather(w_outer, "dp", axis=0, tiled=True),
            )
        )

    def whole_rows(matrix):
        return (matrix.shape[0] * groups, matrix.shape[1])

    full_shapes = (
        whole_rows(w_query),
        whole_rows(w_key),
        whole_rows(w_value),
        b_query.shape,
        b_value.shape,
        conv_taps.shape,
        whole_rows(w_out),
        b_out.shape,
        first_gain.shape,
        first_shift.shape,
        whole_rows(w_inner),
        b_inner.shape,
        whole_rows(w_outer),
        b_outer.shape,
        second_gain.shape,
        second_shift.shape,
    )

    def after_step(totals, inputs):
        out_rows, grad_rows, grads = sequence_step(
            inputs[0], inputs[1], inputs[2], current_weights()
        )
        return (tuple((left + right for left, right in zip(totals, grads))), (out_rows, grad_rows))

    zeros = tuple((jnp.zeros(shape, jnp.float32) for shape in full_shapes))
    totals, (outs, grad_all) = lax.scan(after_step, zeros, (dealt_rows, dealt_cot, ids_here))
    wide = (
        lax.psum_scatter(totals[0], "dp", scatter_dimension=0, tiled=True),
        lax.psum_scatter(totals[1], "dp", scatter_dimension=0, tiled=True),
        lax.psum_scatter(totals[2], "dp", scatter_dimension=0, tiled=True),
        lax.psum_scatter(totals[6], "dp", scatter_dimension=0, tiled=True),
        lax.psum_scatter(totals[10], "dp", scatter_dimension=0, tiled=True),
        lax.psum_scatter(totals[12], "dp", scatter_dimension=0, tiled=True),
        lax.psum_scatter(totals[7], "dp", scatter_dimension=0, tiled=True),
        lax.psum_scatter(totals[8], "dp", scatter_dimension=0, tiled=True),
        lax.psum_scatter(totals[9], "dp", scatter_dimension=0, tiled=True),
        lax.psum_scatter(totals[13], "dp", scatter_dimension=0, tiled=True),
        lax.psum_scatter(totals[14], "dp", scatter_dimension=0, tiled=True),
        lax.psum_scatter(totals[15], "dp", scatter_dimension=0, tiled=True),
    )
    narrow = lax.psum((totals[3], totals[4], totals[5], totals[11]), "dp")
    back_out, back_grad = (
        lax.all_to_all(outs, "dp", split_axis=1, concat_axis=0, tiled=True),
        lax.all_to_all(grad_all, "dp", split_axis=1, concat_axis=0, tiled=True),
    )
    total_seqs = deal_order.shape[0]
    undo_order = (
        jnp.zeros((total_seqs,), jnp.int32)
        .at[deal_order]
        .set(jnp.arange(total_seqs, dtype=jnp.int32))
    )
    home_out = jnp.take(back_out, undo_order, axis=0)
    home_grad = jnp.take(back_grad, undo_order, axis=0)
    return (
        home_out,
        home_grad,
        wide[0],
        wide[1],
        wide[2],
        narrow[0],
        narrow[1],
        narrow[2],
        wide[3],
        wide[6],
        wide[7],
        wide[8],
        wide[4],
        narrow[3],
        wide[5],
        wide[9],
        wide[10],
        wide[11],
    )


def solution(mesh):
    return jax.shard_map(
        local,
        mesh=mesh,
        in_specs=(
            P(None, "dp", None),
            P(None, "dp", None),
            P(),
            P("dp", "tensor"),
            P("dp", "tensor"),
            P("dp", "tensor"),
            P("tensor"),
            P("tensor"),
            P("tensor", None),
            P("dp", "tensor"),
            P(),
            P(),
            P(),
            P("dp", "tensor"),
            P("tensor"),
            P("dp", "tensor"),
            P(),
            P(),
            P(),
        ),
        out_specs=(
            P(None, "dp", None),
            P(None, "dp", None),
            P("dp", "tensor"),
            P("dp", "tensor"),
            P("dp", "tensor"),
            P("tensor"),
            P("tensor"),
            P("tensor", None),
            P("dp", "tensor"),
            P("dp"),
            P("dp"),
            P("dp"),
            P("dp", "tensor"),
            P("tensor"),
            P("dp", "tensor"),
            P("dp"),
            P("dp"),
            P("dp"),
        ),
        check_vma=False,
    )
```

profile of v0, /device:TPU:0, one launch (start us, length us, event | category | flops | bytes accessed | tf_op | source)
XLA Modules:
  0.0 1732.2 jit_solution(10223171790938501074)
XLA Ops:
  22.7 77.0 %all_to_all.72 = bf16[32,64,768]{2,1,0:T(8,128)(2,1)} all-to-all(bf16[32,64,768]{2,1,0:T(8,128)(2,1)S(1)} %get-tuple-element.1059), channel_id=1, replica_groups=mesh['dp'=16,'tensor'=2] {'dp'}, dimensions={0} | all-to-all | bytes 6291456 | tf_op jit(solution)/shard_map/all_to_all | solution.py:289
  110.0 54.5 %all-to-all-done = bf16[32,64,768]{2,1,0:T(8,128)(2,1)S(1)} async-done(((bf16[32,64,768]{2,1,0:T(8,128)(2,1)}), bf16[32,64,768]{2,1,0:T(8,128)(2,1)S(1)}, u32[]{:S(2)}, u32[]{:S(2)}) %all-to-all-start) | async-done | bytes 3145760 | tf_op jit(solution)/shard_map/all_to_all | solution.py:288
  166.5 1101.2 %while.47 = (s32[]{:T(128)}, f32[768,384]{1,0:T(8,128)}, f32[768,384]{1,0:T(8,128)}, f32[768,384]{1,0:T(8,128)}, f32[384]{0:T(512)}, /*index=5*/f32[384]{0:T(512...) while((s32[]{:T(128)}, f32[768,384]{1,0:T(8,128)}, ...), condition=%wide.region_70.72_spmd.clone, body=%wide.region_2.71_spmd.clone.sunk | while | flops 24341413888 | bytes 777525184 | solution.py:355
  169.7 34.2 %all_gather.51 = bf16[768,384]{1,0:T(8,128)(2,1)} all-gather(bf16[48,384]{1,0:T(8,128)(2,1)S(1)} %get-tuple-element.1685), channel_id=1, replica_groups=mesh['dp'=16,'tensor'=2] {'dp'}, dimensions={0}, use_global_device_ids=true | all-gather | bytes 626688 | tf_op jit(solution)/shard_map/while/body/eval_jaxpr/all_gather | solution.py:320
  203.9 20.4 %all_gather.50 = bf16[768,384]{1,0:T(8,128)(2,1)} all-gather(bf16[48,384]{1,0:T(8,128)(2,1)S(1)} %get-tuple-element.1680), channel_id=1, replica_groups=mesh['dp'=16,'tensor'=2] {'dp'}, dimensions={0}, use_global_device_ids=true | all-gather | bytes 626688 | tf_op jit(solution)/shard_map/while/body/eval_jaxpr/all_gather | solution.py:319
  224.3 20.6 %all_gather.49 = bf16[768,384]{1,0:T(8,128)(2,1)S(1)} all-gather(bf16[48,384]{1,0:T(8,128)(2,1)S(1)} %get-tuple-element.1678), channel_id=1, replica_groups=mesh['dp'=16,'tensor'=2] {'dp'}, dimensions={0}, use_global_device_ids=true | all-gather | bytes 626688 | tf_op jit(solution)/shard_map/while/body/eval_jaxpr/all_gather | solution.py:317
  245.0 19.0 %all_gather.48 = bf16[768,384]{1,0:T(8,128)(2,1)S(1)} all-gather(bf16[48,384]{1,0:T(8,128)(2,1)S(1)} %get-tuple-element.1677), channel_id=1, replica_groups=mesh['dp'=16,'tensor'=2] {'dp'}, dimensions={0}, use_global_device_ids=true | all-gather | bytes 626688 | tf_op jit(solution)/shard_map/while/body/eval_jaxpr/all_gather | solution.py:318
  294.6 15.8 fusion.892
  314.0 48.8 %all-reduce.79.cloned.1.call-done = bf16[1024,768]{1,0:T(8,128)(2,1)} async-done(((bf16[1024,768]{1,0:T(8,128)(2,1)}), bf16[1024,768]{1,0:T(8,128)(2,1)}) %all-reduce.79.cloned.1.call-update) | async-done | bytes 1572880 | tf_op jit(solution)/shard_map/while/body/eval_jaxpr/psum | solution.py:128
  367.8 20.0 %multiply_convert_fusion.12 = (bf16[1024,1536]{1,0:T(8,128)(2,1)}, f32[1024,1536]{1,0:T(8,128)}, f32[1024,1536]{1,0:T(8,128)}) fusion(f32[1536]{0:T(1024)S(1)} %convert_element_type.836, bf16[768,1536]{1,0:T(8,128)(2,1)} %all-gather.3.cloned.1.call-done, f32[768]{0:T(1024)S(1)} %convert_element_type.837, f32[768]{0:T(1024)S(1)} %convert_element_type.838, ...), kind=kOutput, calls=%fused_computation.78.clone.1 | convolution fusion | flops 2526806016 | bytes 21257220 | tf_op jit(solution)/shard_map/while/body/eval_jaxpr/dot_general | solution.py:138
  387.8 12.5 all-gather.5.cloned.1.call-done
  412.6 44.4 %all-reduce.81.cloned.1.call-done = bf16[1024,768]{1,0:T(8,128)(2,1)} async-done(((bf16[1024,768]{1,0:T(8,128)(2,1)}), bf16[1024,768]{1,0:T(8,128)(2,1)}) %all-reduce.81.cloned.1.call-update) | async-done | bytes 1572880 | tf_op jit(solution)/shard_map/while/body/eval_jaxpr/psum | solution.py:144
  466.0 8.5 fusion.899
  484.5 7.0 select_add_fusion.27
  498.2 33.4 %all-reduce.83.cloned.1.call-done = bf16[1024,768]{1,0:T(8,128)(2,1)} async-done(((bf16[1024,768]{1,0:T(8,128)(2,1)}), bf16[1024,768]{1,0:T(8,128)(2,1)}) %all-reduce.83.cloned.1.call-update) | async-done | bytes 1572880 | tf_op jit(solution)/shard_map/while/body/eval_jaxpr/psum | solution.py:166
  573.5 8.8 fusion.940
  582.3 8.9 fusion.937
  591.1 6.9 convert_multiply_fusion.67
  598.1 10.8 convert_multiply_fusion.68
  630.6 20.8 %pad_add_fusion.8 = f32[1056,6,64]{0,2,1:T(8,128)} fusion(f32[1024,6,64]{0,2,1:T(8,128)} %get-tuple-element.1500, f32[1024,6,64]{0,2,1:T(8,128)} %get-tuple-element.1501, f32[1024,6,64]{0,2,1:T(8,128)} %get-tuple-element.1502, f32[1024,6,64]{0,2,1:T(8,128)} %get-tuple-element.1503, f32[1024,6,64]{0,2,1:T(8,128)} %get-tuple-element.1504, ...), kind=kLoop, calls=%fused_computation.122.clone.1 | loop fusion | flops 10543104 | bytes 44089344 | tf_op jit(solution)/shard_map/while/body/eval_jaxpr/transpose(jvp())/add_any | solution.py:35
  651.4 8.0 fusion.938
  678.9 35.8 %all-reduce.85.cloned.1.call-done = bf16[1024,768]{1,0:T(8,128)(2,1)} async-done(((bf16[1024,768]{1,0:T(8,128)(2,1)}), bf16[1024,768]{1,0:T(8,128)(2,1)}) %all-reduce.85.cloned.1.call-update) | async-done | bytes 1572880 | tf_op jit(solution)/shard_map/while/body/eval_jaxpr/psum | solution.py:226
  721.2 24.4 %all_gather.51 = bf16[768,384]{1,0:T(8,128)(2,1)} all-gather(bf16[48,384]{1,0:T(8,128)(2,1)S(1)} %get-tuple-element.1685), channel_id=1, replica_groups=mesh['dp'=16,'tensor'=2] {'dp'}, dimensions={0}, use_global_device_ids=true | all-gather | bytes 626688 | tf_op jit(solution)/shard_map/while/body/eval_jaxpr/all_gather | solution.py:320
  745.6 20.4 %all_gather.50 = bf16[768,384]{1,0:T(8,128)(2,1)} all-gather(bf16[48,384]{1,0:T(8,128)(2,1)S(1)} %get-tuple-element.1680), channel_id=1, replica_groups=mesh['dp'=16,'tensor'=2] {'dp'}, dimensions={0}, use_global_device_ids=true | all-gather | bytes 626688 | tf_op jit(solution)/shard_map/while/body/eval_jaxpr/all_gather | solution.py:319
  766.0 20.6 %all_gather.49 = bf16[768,384]{1,0:T(8,128)(2,1)S(1)} all-gather(bf16[48,384]{1,0:T(8,128)(2,1)S(1)} %get-tuple-element.1678), channel_id=1, replica_groups=mesh['dp'=16,'tensor'=2] {'dp'}, dimensions={0}, use_global_device_ids=true | all-gather | bytes 626688 | tf_op jit(solution)/shard_map/while/body/eval_jaxpr/all_gather | solution.py:317
  786.6 19.0 %all_gather.48 = bf16[768,384]{1,0:T(8,128)(2,1)S(1)} all-gather(bf16[48,384]{1,0:T(8,128)(2,1)S(1)} %get-tuple-element.1677), channel_id=1, replica_groups=mesh['dp'=16,'tensor'=2] {'dp'}, dimensions={0}, use_global_device_ids=true | all-gather | bytes 626688 | tf_op jit(solution)/shard_map/while/body/eval_jaxpr/all_gather | solution.py:318
  836.3 16.0 fusion.892
  856.1 47.7 %all-reduce.79.cloned.1.call-done = bf16[1024,768]{1,0:T(8,128)(2,1)} async-done(((bf16[1024,768]{1,0:T(8,128)(2,1)}), bf16[1024,768]{1,0:T(8,128)(2,1)}) %all-reduce.79.cloned.1.call-update) | async-done | bytes 1572880 | tf_op jit(solution)/shard_map/while/body/eval_jaxpr/psum | solution.py:128
  908.7 20.0 %multiply_convert_fusion.12 = (bf16[1024,1536]{1,0:T(8,128)(2,1)}, f32[1024,1536]{1,0:T(8,128)}, f32[1024,1536]{1,0:T(8,128)}) fusion(f32[1536]{0:T(1024)S(1)} %convert_element_type.836, bf16[768,1536]{1,0:T(8,128)(2,1)} %all-gather.3.cloned.1.call-done, f32[768]{0:T(1024)S(1)} %convert_element_type.837, f32[768]{0:T(1024)S(1)} %convert_element_type.838, ...), kind=kOutput, calls=%fused_computation.78.clone.1 | convolution fusion | flops 2526806016 | bytes 21257220 | tf_op jit(solution)/shard_map/while/body/eval_jaxpr/dot_general | solution.py:138
  928.7 12.9 all-gather.5.cloned.1.call-done
  954.4 44.0 %all-reduce.81.cloned.1.call-done = bf16[1024,768]{1,0:T(8,128)(2,1)} async-done(((bf16[1024,768]{1,0:T(8,128)(2,1)}), bf16[1024,768]{1,0:T(8,128)(2,1)}) %all-reduce.81.cloned.1.call-update) | async-done | bytes 1572880 | tf_op jit(solution)/shard_map/while/body/eval_jaxpr/psum | solution.py:144
  1007.4 8.5 fusion.899
  1025.9 7.7 select_add_fusion.27
  1033.6 8.1 select_add_fusion.25
  1041.8 31.2 %all-reduce.83.cloned.1.call-done = bf16[1024,768]{1,0:T(8,128)(2,1)} async-done(((bf16[1024,768]{1,0:T(8,128)(2,1)}), bf16[1024,768]{1,0:T(8,128)(2,1)}) %all-reduce.83.cloned.1.call-update) | async-done | bytes 1572880 | tf_op jit(solution)/shard_map/while/body/eval_jaxpr/psum | solution.py:166
  1115.1 8.8 fusion.940
  1123.9 8.6 fusion.937
  1132.5 6.9 convert_multiply_fusion.67
  1139.5 10.8 convert_multiply_fusion.68
  1172.0 21.0 %pad_add_fusion.8 = f32[1056,6,64]{0,2,1:T(8,128)} fusion(f32[1024,6,64]{0,2,1:T(8,128)} %get-tuple-element.1500, f32[1024,6,64]{0,2,1:T(8,128)} %get-tuple-element.1501, f32[1024,6,64]{0,2,1:T(8,128)} %get-tuple-element.1502, f32[1024,6,64]{0,2,1:T(8,128)} %get-tuple-element.1503, f32[1024,6,64]{0,2,1:T(8,128)} %get-tuple-element.1504, ...), kind=kLoop, calls=%fused_computation.122.clone.1 | loop fusion | flops 10543104 | bytes 44089344 | tf_op jit(solution)/shard_map/while/body/eval_jaxpr/transpose(jvp())/add_any | solution.py:35
  1193.0 8.0 fusion.938
  1222.2 34.2 %all-reduce.85.cloned.1.call-done = bf16[1024,768]{1,0:T(8,128)(2,1)} async-done(((bf16[1024,768]{1,0:T(8,128)(2,1)}), bf16[1024,768]{1,0:T(8,128)(2,1)}) %all-reduce.85.cloned.1.call-update) | async-done | bytes 1572880 | tf_op jit(solution)/shard_map/while/body/eval_jaxpr/psum | solution.py:226
  1290.3 56.8 %all-to-all-done.3 = bf16[2,1024,768]{2,0,1:T(2,128)(2,1)S(1)} async-done(((bf16[2,1024,768]{2,0,1:T(2,128)(2,1)}), bf16[2,1024,768]{2,0,1:T(2,128)(2,1)S(1)}, u32[]{:S(2)}, u32[]{:S(2)}) %all-to-all-start.3) | async-done | bytes 3145760 | tf_op jit(solution)/shard_map/all_to_all | solution.py:373
  1347.1 17.8 %all-to-all-start.2 = ((bf16[2,1024,768]{2,0,1:T(2,128)(2,1)}), bf16[2,1024,768]{2,0,1:T(2,128)(2,1)}, u32[]{:S(2)}, u32[]{:S(2)}) async-start(bf16[2,1024,768]{2,0,1:T(2,128)(2,1)} %copy.221), calls=%async_computation.2 | async-start | bytes 6291456 | tf_op jit(solution)/shard_map/all_to_all | solution.py:372
  1367.1 114.3 %all-reduce.73 = (f32[384]{0:T(512)}, f32[384]{0:T(512)}, f32[6,33]{1,0:T(8,128)}, f32[768]{0:T(1024)S(1)}, f32[768]{0:T(1024)S(1)}, /*index=5*/f32[768]{0:T(102...) all-reduce(f32[384]{0:T(512)S(1)} %copy-done.186, ...), channel_id=1, replica_groups=mesh['dp'=16,'tensor'=2] {'dp'}, use_global_device_ids=true, to_apply=%region_75.77 | all-reduce | flops 7110 | bytes 56880 | tf_op jit(solution)/shard_map/psum | solution.py:370
  1505.0 61.1 %reduce-scatter.13.cloned.1.call-done = f32[48,384]{1,0:T(8,128)} async-done(((f32[768,384]{1,0:T(8,128)}), f32[48,384]{1,0:T(8,128)}) %reduce-scatter.13.cloned.1.call-update) | async-done | bytes 73744 | tf_op jit(solution)/shard_map/reduce_scatter | solution.py:360
  1566.1 79.1 %reduce-scatter.15.cloned.1.call-done = f32[48,1536]{1,0:T(8,128)} async-done(((f32[768,1536]{1,0:T(8,128)}), f32[48,1536]{1,0:T(8,128)}) %reduce-scatter.15.cloned.1.call-update) | async-done | bytes 294928 | tf_op jit(solution)/shard_map/reduce_scatter | solution.py:361
  1645.2 79.4 %reduce-scatter.17.cloned.1.call-done = f32[48,1536]{1,0:T(8,128)} async-done(((f32[768,1536]{1,0:T(8,128)}), f32[48,1536]{1,0:T(8,128)}) %reduce-scatter.17.cloned.1.call-update) | async-done | bytes 294928 | tf_op jit(solution)/shard_map/reduce_scatter | solution.py:362
  (1360 shorter events, 396.0 us)
Async XLA Ops:
  99.7 64.7 %all-to-all-start = ((bf16[32,64,768]{2,1,0:T(8,128)(2,1)}), bf16[32,64,768]{2,1,0:T(8,128)(2,1)S(1)}, u32[]{:S(2)}, u32[]{:S(2)}) async-start(bf16[32,64,768]{2,1,0:T(8,128)(2,1)} %get-tuple-element.1060), calls=%async_computation | async-start | bytes 6291456 | tf_op jit(solution)/shard_map/all_to_all | solution.py:288
  166.8 100.3 %copy-start.155 = (bf16[6,33]{0,1:T(8,128)(2,1)}, bf16[6,33]{0,1:T(8,128)(2,1)S(1)}, u32[]{:S(2)}) copy-start(bf16[6,33]{0,1:T(8,128)(2,1)S(1)} %get-tuple-element.1684) | copy-start | bytes 1192 | tf_op jit(solution)/shard_map/while
  166.8 100.3 %copy-start.179 = (s32[2,1024]{1,0:T(2,128)}, s32[2,1024]{1,0:T(2,128)S(1)}, u32[]{:S(2)}) copy-start(s32[2,1024]{1,0:T(2,128)S(1)} %get-tuple-element.1676) | copy-start | bytes 24580 | tf_op jit(solution)/shard_map/while
  166.9 195.9 %all-reduce.79.cloned.1.call-start = ((), (), s32[]{:S(2)}) async-start(), calls=%async_computation.16 | async-start | bytes 3145728 | tf_op jit(solution)/shard_map/while/body/eval_jaxpr/psum | solution.py:128
  166.9 103.3 %copy-start.112 = (s32[1,1024]{1,0:T(1,128)}, s32[1,1024]{1,0:T(1,128)S(1)}, u32[]{:S(2)}) copy-start(s32[1,1024]{1,0:T(1,128)S(1)} %constant_dynamic-slice_fusion.2) | copy-start | bytes 12292 | tf_op jit(solution)/shard_map/while
  167.1 103.2 %copy-start.231 = (f32[64]{0:T(128)}, f32[64]{0:T(128)S(1)}, u32[]{:S(2)}) copy-start(f32[64]{0:T(128)S(1)} %convert_reduce_fusion.5) | copy-start | bytes 772 | tf_op jit(solution)/shard_map/while
  167.1 121.9 %copy-start.147 = (pred[1024]{0:T(1024)(128)(4,1)}, pred[1024]{0:T(1024)(128)(4,1)S(1)}, u32[]{:S(2)}) copy-start(pred[1024]{0:T(1024)(128)(4,1)S(1)} %broadcast_compare_fusion.2) | copy-start | bytes 3076 | tf_op jit(solution)/shard_map/while
  168.4 113.5 %copy-start.32 = (f32[64,64]{1,0:T(8,128)}, f32[64,64]{1,0:T(8,128)S(1)}, u32[]{:S(2)}) copy-start(f32[64,64]{1,0:T(8,128)S(1)} %fusion.881) | copy-start | bytes 49156 | tf_op jit(solution)/shard_map/while
  312.7 55.1 %all-gather.3.cloned.1.call-start = ((), (), s32[]{:S(2)}) async-start(), calls=%async_computation.17 | async-start | bytes 2506752 | tf_op jit(solution)/shard_map/while/body/eval_jaxpr/all_gather | solution.py:321
  313.3 87.0 %all-gather.5.cloned.1.call-start = ((), (), s32[]{:S(2)}) async-start(), calls=%async_computation.18 | async-start | bytes 2506752 | tf_op jit(solution)/shard_map/while/body/eval_jaxpr/all_gather | solution.py:322
  313.9 143.2 %all-reduce.81.cloned.1.call-start = ((), (), s32[]{:S(2)}) async-start(), calls=%async_computation.19 | async-start | bytes 3145728 | tf_op jit(solution)/shard_map/while/body/eval_jaxpr/psum | solution.py:144
  313.9 143.1 %copy-start.116 = (f32[768]{0:T(1024)}, f32[768]{0:T(1024)S(1)}, u32[]{:S(2)}) copy-start(f32[768]{0:T(1024)S(1)} %convert_element_type.838) | copy-start | bytes 9220 | tf_op jit(solution)/shard_map/while
  314.0 53.8 %copy-start.150 = (f32[768]{0:T(1024)}, f32[768]{0:T(1024)S(1)}, u32[]{:S(2)}) copy-start(f32[768]{0:T(1024)S(1)} %convert_element_type.837) | copy-start | bytes 9220 | tf_op jit(solution)/shard_map/while
  406.9 124.7 %all-reduce.83.cloned.1.call-start = ((), (), s32[]{:S(2)}) async-start(), calls=%async_computation.20 | async-start | bytes 3145728 | tf_op jit(solution)/shard_map/while/body/eval_jaxpr/psum | solution.py:166
  480.0 234.8 %all-reduce.85.cloned.1.call-start = ((), (), s32[]{:S(2)}) async-start(), calls=%async_computation.21 | async-start | bytes 3145728 | tf_op jit(solution)/shard_map/while/body/eval_jaxpr/psum | solution.py:226
  718.3 90.5 %copy-start.155 = (bf16[6,33]{0,1:T(8,128)(2,1)}, bf16[6,33]{0,1:T(8,128)(2,1)S(1)}, u32[]{:S(2)}) copy-start(bf16[6,33]{0,1:T(8,128)(2,1)S(1)} %get-tuple-element.1684) | copy-start | bytes 1192 | tf_op jit(solution)/shard_map/while
  718.3 90.5 %copy-start.179 = (s32[2,1024]{1,0:T(2,128)}, s32[2,1024]{1,0:T(2,128)S(1)}, u32[]{:S(2)}) copy-start(s32[2,1024]{1,0:T(2,128)S(1)} %get-tuple-element.1676) | copy-start | bytes 24580 | tf_op jit(solution)/shard_map/while
  718.3 185.4 %all-reduce.79.cloned.1.call-start = ((), (), s32[]{:S(2)}) async-start(), calls=%async_computation.16 | async-start | bytes 3145728 | tf_op jit(solution)/shard_map/while/body/eval_jaxpr/psum | solution.py:128
  718.4 93.5 %copy-start.112 = (s32[1,1024]{1,0:T(1,128)}, s32[1,1024]{1,0:T(1,128)S(1)}, u32[]{:S(2)}) copy-start(s32[1,1024]{1,0:T(1,128)S(1)} %constant_dynamic-slice_fusion.2) | copy-start | bytes 12292 | tf_op jit(solution)/shard_map/while
  718.6 93.3 %copy-start.231 = (f32[64]{0:T(128)}, f32[64]{0:T(128)S(1)}, u32[]{:S(2)}) copy-start(f32[64]{0:T(128)S(1)} %convert_reduce_fusion.5) | copy-start | bytes 772 | tf_op jit(solution)/shard_map/while
  718.6 112.1 %copy-start.147 = (pred[1024]{0:T(1024)(128)(4,1)}, pred[1024]{0:T(1024)(128)(4,1)S(1)}, u32[]{:S(2)}) copy-start(pred[1024]{0:T(1024)(128)(4,1)S(1)} %broadcast_compare_fusion.2) | copy-start | bytes 3076 | tf_op jit(solution)/shard_map/while
  719.9 103.6 %copy-start.32 = (f32[64,64]{1,0:T(8,128)}, f32[64,64]{1,0:T(8,128)S(1)}, u32[]{:S(2)}) copy-start(f32[64,64]{1,0:T(8,128)S(1)} %fusion.881) | copy-start | bytes 49156 | tf_op jit(solution)/shard_map/while
  854.6 54.1 %all-gather.3.cloned.1.call-start = ((), (), s32[]{:S(2)}) async-start(), calls=%async_computation.17 | async-start | bytes 2506752 | tf_op jit(solution)/shard_map/while/body/eval_jaxpr/all_gather | solution.py:321
  855.2 86.5 %all-gather.5.cloned.1.call-start = ((), (), s32[]{:S(2)}) async-start(), calls=%async_computation.18 | async-start | bytes 2506752 | tf_op jit(solution)/shard_map/while/body/eval_jaxpr/all_gather | solution.py:322
  855.9 142.5 %all-reduce.81.cloned.1.call-start = ((), (), s32[]{:S(2)}) async-start(), calls=%async_computation.19 | async-start | bytes 3145728 | tf_op jit(solution)/shard_map/while/body/eval_jaxpr/psum | solution.py:144
  856.0 142.4 %copy-start.116 = (f32[768]{0:T(1024)}, f32[768]{0:T(1024)S(1)}, u32[]{:S(2)}) copy-start(f32[768]{0:T(1024)S(1)} %convert_element_type.838) | copy-start | bytes 9220 | tf_op jit(solution)/shard_map/while
  948.3 124.7 %all-reduce.83.cloned.1.call-start = ((), (), s32[]{:S(2)}) async-start(), calls=%async_computation.20 | async-start | bytes 3145728 | tf_op jit(solution)/shard_map/while/body/eval_jaxpr/psum | solution.py:166
  1021.3 235.0 %all-reduce.85.cloned.1.call-start = ((), (), s32[]{:S(2)}) async-start(), calls=%async_computation.21 | async-start | bytes 3145728 | tf_op jit(solution)/shard_map/while/body/eval_jaxpr/psum | solution.py:226
  1267.7 235.3 %reduce-scatter.7.cloned.1.call-start = ((), (), s32[]{:S(2)}) async-start(), calls=%async_computation.10 | async-start | bytes 1253376 | tf_op jit(solution)/shard_map/reduce_scatter | solution.py:357
  1268.5 234.5 %reduce-scatter.9.cloned.1.call-start = ((), (), s32[]{:S(2)}) async-start(), calls=%async_computation.11 | async-start | bytes 1253376 | tf_op jit(solution)/shard_map/reduce_scatter | solution.py:358
  1269.1 236.0 %reduce-scatter.11.cloned.1.call-start = ((), (), s32[]{:S(2)}) async-start(), calls=%async_computation.12 | async-start | bytes 1253376 | tf_op jit(solution)/shard_map/reduce_scatter | solution.py:359
  1269.8 296.3 %reduce-scatter.13.cloned.1.call-start = ((), (), s32[]{:S(2)}) async-start(), calls=%async_computation.13 | async-start | bytes 1253376 | tf_op jit(solution)/shard_map/reduce_scatter | solution.py:360
  1270.4 374.8 %reduce-scatter.15.cloned.1.call-start = ((), (), s32[]{:S(2)}) async-start(), calls=%async_computation.14 | async-start | bytes 5013504 | tf_op jit(solution)/shard_map/reduce_scatter | solution.py:361
  1277.2 69.9 %all-to-all-start.3 = ((bf16[2,1024,768]{2,0,1:T(2,128)(2,1)}), bf16[2,1024,768]{2,0,1:T(2,128)(2,1)S(1)}, u32[]{:S(2)}, u32[]{:S(2)}) async-start(bf16[2,1024,768]{2,0,1:T(2,128)(2,1)} %copy.224), calls=%async_computation.3 | async-start | bytes 6291456 | tf_op jit(solution)/shard_map/all_to_all | solution.py:373
  1282.8 441.8 %reduce-scatter.17.cloned.1.call-start = ((), (), s32[]{:S(2)}) async-start(), calls=%async_computation.15 | async-start | bytes 5013504 | tf_op jit(solution)/shard_map/reduce_scatter | solution.py:362
  1290.3 74.7 %copy-start.238 = (u32[32]{0:T(128)S(1)}, u32[32]{0:T(128)}, u32[]{:S(2)}) copy-start(u32[32]{0:T(128)} %constant.503) | copy-start | bytes 388
  1290.3 75.9 %copy-start.235 = (s32[32]{0:T(128)S(1)}, s32[32]{0:T(128)}, u32[]{:S(2)}) copy-start(s32[32]{0:T(128)} %copy-done.234) | copy-start | bytes 388
  1290.3 76.7 %copy-start.143 = (f32[6,33]{0,1:T(8,128)S(1)}, f32[6,33]{0,1:T(8,128)}, u32[]{:S(2)}) copy-start(f32[6,33]{0,1:T(8,128)} %get-tuple-element.1967) | copy-start | bytes 2380
  1290.3 76.8 %copy-start.159 = (f32[1536]{0:T(1024)S(1)}, f32[1536]{0:T(1024)}, u32[]{:S(2)}) copy-start(f32[1536]{0:T(1024)} %get-tuple-element.1973) | copy-start | bytes 18436
  1290.3 76.8 %copy-start.165 = (f32[768]{0:T(1024)S(1)}, f32[768]{0:T(1024)}, u32[]{:S(2)}) copy-start(f32[768]{0:T(1024)} %get-tuple-element.1976) | copy-start | bytes 9220
  1290.3 76.8 %copy-start.168 = (f32[768]{0:T(1024)S(1)}, f32[768]{0:T(1024)}, u32[]{:S(2)}) copy-start(f32[768]{0:T(1024)} %get-tuple-element.1975) | copy-start | bytes 9220
  1290.3 76.7 %copy-start.171 = (f32[768]{0:T(1024)S(1)}, f32[768]{0:T(1024)}, u32[]{:S(2)}) copy-start(f32[768]{0:T(1024)} %get-tuple-element.1971) | copy-start | bytes 9220
  1290.3 76.7 %copy-start.174 = (f32[768]{0:T(1024)S(1)}, f32[768]{0:T(1024)}, u32[]{:S(2)}) copy-start(f32[768]{0:T(1024)} %get-tuple-element.1970) | copy-start | bytes 9220
  1290.3 76.7 %copy-start.177 = (f32[768]{0:T(1024)S(1)}, f32[768]{0:T(1024)}, u32[]{:S(2)}) copy-start(f32[768]{0:T(1024)} %get-tuple-element.1969) | copy-start | bytes 9220
  1290.3 76.7 %copy-start.183 = (f32[384]{0:T(512)S(1)}, f32[384]{0:T(512)}, u32[]{:S(2)}) copy-start(f32[384]{0:T(512)} %get-tuple-element.1966) | copy-start | bytes 4612
  1290.3 76.7 %copy-start.186 = (f32[384]{0:T(512)S(1)}, f32[384]{0:T(512)}, u32[]{:S(2)}) copy-start(f32[384]{0:T(512)} %get-tuple-element.1965) | copy-start | bytes 4612
  1347.1 138.5 %all-to-all-start.2 = ((bf16[2,1024,768]{2,0,1:T(2,128)(2,1)}), bf16[2,1024,768]{2,0,1:T(2,128)(2,1)}, u32[]{:S(2)}, u32[]{:S(2)}) async-start(bf16[2,1024,768]{2,0,1:T(2,128)(2,1)} %copy.221), calls=%async_computation.2 | async-start | bytes 6291456 | tf_op jit(solution)/shard_map/all_to_all | solution.py:372
  1496.7 227.9 %copy-start.1 = (bf16[32,64,768]{2,1,0:T(8,128)(2,1)S(1)}, bf16[32,64,768]{2,1,0:T(8,128)(2,1)}, u32[]{:S(2)}) copy-start(bf16[32,64,768]{2,1,0:T(8,128)(2,1)} %param.24) | copy-start | bytes 9437188
  (437 other events, 1736.4 us)
Sparse Core Ops, SparseCore 0:
  312.8 49.9 all-reduce.78
  407.0 49.9 all-reduce.80
  480.1 51.4 all-reduce.82
  663.2 51.4 all-reduce.84
  854.7 48.9 all-reduce.78
  948.4 49.9 all-reduce.80
  1021.5 51.4 all-reduce.82
  1204.8 51.4 all-reduce.84
  1272.8 83.4 reduce-scatter.6
  1360.3 80.6 reduce-scatter.8
  1445.2 59.7 reduce-scatter.10
  1509.1 56.9 reduce-scatter.12
  1570.5 74.5 reduce-scatter.14
  1650.0 74.5 reduce-scatter.16
Sparse Core Ops, SparseCore 1:
  315.7 40.9 all-gather.2
  359.1 41.1 all-gather.4
  857.6 40.2 all-gather.2
  900.4 41.2 all-gather.4
where the time goes:
time: 1740 us; the launch traced here: 1730 us
  waiting for transfers between devices  684 us (39%)
  blocking collectives  370 us (21%)
  matrix products  327 us (19%)
  other arithmetic  205 us (12%)
  local copies, waits for them, and re-layouts  82.9 us (5%)
  starting transfers between devices  30 us (2%)
    dot_general x54, matrix products, partial_product(): return jnp.einsum(spec, left, right, preferred_element_type=jnp.float32)  182 us
    psum x1, blocking collectives, local(): narrow = lax.psum((totals[3], totals[4], totals[5], totals[11]), 'dp')  114 us
    psum x2, waiting for transfers between devices, sequence_step(): lax.psum(attn_part.astype(jnp.bfloat16), 'tensor').astype(jnp.float32)  96.4 us
    psum x2, waiting for transfers between devices, sequence_step(): lax.psum(ffn_part.astype(jnp.bfloat16), 'tensor').astype(jnp.float32)  88.4 us
    dot_general x154, matrix products, contract_dims(): return jnp.einsum(spec, left, right, precision=lax.Precision.HIGHEST)  84.4 us
    reduce_scatter x1, waiting for transfers between devices, local(): lax.psum_scatter(totals[12], 'dp', scatter_dimension=0, tiled=True)  79.4 us
    reduce_scatter x1, waiting for transfers between devices, local(): lax.psum_scatter(totals[10], 'dp', scatter_dimension=0, tiled=True)  79.1 us
    all_to_all x1, blocking collectives, local(): lax.all_to_all(arranged_cot, 'dp', split_axis=0, concat_axis=1, tiled=True)  77 us
  transfers between devices with their start and end apart: 21, of which 16 were waited for; matrix products, arithmetic and copies ran while one was open for 10% of the time, Pallas kernels for 0%

commit v1 on v0

--- a/solution.py
+++ b/solution.py
@@ -125,9 +125,7 @@
     conv_out, conv_back = jax.vjp(depthwise, masked, conv_taps.astype(single_float))
     context = (attended_rows + conv_out).astype(reduced_dtype).reshape(length, column_count)
     attn_part = partial_product("nc,dc->nd", context, w_out)
-    attn_out = lax.psum(attn_part.astype(jnp.bfloat16), "tensor").astype(
-        jnp.float32
-    ) + b_out.astype(single_float)
+    attn_out = attn_part + b_out.astype(single_float)
     hidden, first_norm_back = jax.vjp(
         layer_norm,
         rows_f + attn_out,
@@ -141,9 +139,7 @@
     active_f, gelu_back = jax.vjp(exact_gelu, inner)
     active = active_f.astype(reduced_dtype)
     ffn_part = partial_product("nf,df->nd", active, w_outer)
-    ffn_out = lax.psum(ffn_part.astype(jnp.bfloat16), "tensor").astype(
-        jnp.float32
-    ) + b_outer.astype(single_float)
+    ffn_out = ffn_part + b_outer.astype(single_float)
     result, second_norm_back = jax.vjp(
         layer_norm,
         hidden + ffn_out,
@@ -163,9 +159,7 @@
     grad_inner_low = grad_inner.astype(reduced_dtype)
     grad_w_inner = partial_product("nd,nf->df", hidden_low, grad_inner_low)
     hidden_part = partial_product("nf,df->nd", grad_inner_low, w_inner)
-    grad_hidden = grad_second + lax.psum(hidden_part.astype(jnp.bfloat16), "tensor").astype(
-        jnp.float32
-    )
+    grad_hidden = grad_second + hidden_part
     grad_first, grad_first_gain, grad_first_shift = first_norm_back(grad_hidden)
     grad_b_out = jnp.sum(grad_first, axis=0)
     grad_attn = grad_first.astype(reduced_dtype)
@@ -223,7 +217,7 @@
         + partial_product("nc,dc->nd", pre_value, w_value)
     )
     grad_rows = (
-        grad_first + lax.psum(token_part.astype(jnp.bfloat16), "tensor").astype(jnp.float32)
+        grad_first + token_part
     ).astype(reduced_dtype)
     grads = (
         grad_w_query,
@@ -246,160 +240,77 @@
     return (out_rows, grad_rows, grads)
 
 
-def dealing(landmark_ids, groups, seq_here):
-    total_seqs = landmark_ids.shape[0]
-    seq_lengths = jnp.sum((landmark_ids < LAND).astype(jnp.int32), axis=1)
-    places = jnp.arange(total_seqs, dtype=jnp.int32)
-    scores = seq_lengths * total_seqs + places
-    ordered = jnp.argsort(-scores, stable=True)
-    owners = places // seq_here
-    within = places % seq_here
-    ranked = within * groups + jnp.where(within % 2 == 0, owners, groups - 1 - owners)
-    return jnp.take(ordered, ranked, axis=0)
-
-
-def local(
-    tokens,
-    cotangent,
-    landmark_ids,
-    w_query,
-    w_key,
-    w_value,
-    b_query,
-    b_value,
-    conv_taps,
-    w_out,
-    b_out,
-    first_gain,
-    first_shift,
-    w_inner,
-    b_inner,
-    w_outer,
-    b_outer,
-    second_gain,
-    second_shift,
-):
+def local(tokens, cotangent, landmark_ids, w_query, w_key, w_value, b_query, b_value, conv_taps, w_out, b_out,
+          first_gain, first_shift, w_inner, b_inner, w_outer, b_outer, second_gain, second_shift):
     groups = lax.axis_size("dp")
-    seq_here = tokens.shape[0] // groups
-    deal_order = dealing(landmark_ids, groups, seq_here)
-    arranged_rows = jnp.take(tokens, deal_order, axis=0)
-    arranged_cot = jnp.take(cotangent, deal_order, axis=0)
-    dealt_rows, dealt_cot = (
-        lax.all_to_all(arranged_rows, "dp", split_axis=0, concat_axis=1, tiled=True),
-        lax.all_to_all(arranged_cot, "dp", split_axis=0, concat_axis=1, tiled=True),
-    )
-    own_seqs = lax.dynamic_slice_in_dim(deal_order, lax.axis_index("dp") * seq_here, seq_here, 0)
-    ids_here = jnp.take(landmark_ids, own_seqs, axis=0)
-
-    def assemble(matrices):
-        return (
-            matrices[0],
-            matrices[1],
-            matrices[2],
-            b_query,
-            b_value,
-            conv_taps,
-            matrices[3],
-            b_out,
-            first_gain,
-            first_shift,
-            matrices[4],
-            b_inner,
-            matrices[5],
-            b_outer,
-            second_gain,
-            second_shift,
-        )
-
-    def current_weights():
-        return assemble(
-            (
-                lax.all_gather(w_query, "dp", axis=0, tiled=True),
-                lax.all_gather(w_key, "dp", axis=0, tiled=True),
-                lax.all_gather(w_value, "dp", axis=0, tiled=True),
-                lax.all_gather(w_out, "dp", axis=0, tiled=True),
-                lax.all_gather(w_inner, "dp", axis=0, tiled=True),
-                lax.all_gather(w_outer, "dp", axis=0, tiled=True),
-            )
-        )
-
-    def whole_rows(matrix):
-        return (matrix.shape[0] * groups, matrix.shape[1])
-
-    full_shapes = (
-        whole_rows(w_query),
-        whole_rows(w_key),
-        whole_rows(w_value),
-        b_query.shape,
-        b_value.shape,
-        conv_taps.shape,
-        whole_rows(w_out),
-        b_out.shape,
-        first_gain.shape,
-        first_shift.shape,
-        whole_rows(w_inner),
-        b_inner.shape,
-        whole_rows(w_outer),
-        b_outer.shape,
-        second_gain.shape,
-        second_shift.shape,
-    )
-
-    def after_step(totals, inputs):
-        out_rows, grad_rows, grads = sequence_step(
-            inputs[0], inputs[1], inputs[2], current_weights()
-        )
-        return (tuple((left + right for left, right in zip(totals, grads))), (out_rows, grad_rows))
-
-    zeros = tuple((jnp.zeros(shape, jnp.float32) for shape in full_shapes))
-    totals, (outs, grad_all) = lax.scan(after_step, zeros, (dealt_rows, dealt_cot, ids_here))
-    wide = (
-        lax.psum_scatter(totals[0], "dp", scatter_dimension=0, tiled=True),
-        lax.psum_scatter(totals[1], "dp", scatter_dimension=0, tiled=True),
-        lax.psum_scatter(totals[2], "dp", scatter_dimension=0, tiled=True),
-        lax.psum_scatter(totals[6], "dp", scatter_dimension=0, tiled=True),
-        lax.psum_scatter(totals[10], "dp", scatter_dimension=0, tiled=True),
-        lax.psum_scatter(totals[12], "dp", scatter_dimension=0, tiled=True),
-        lax.psum_scatter(totals[7], "dp", scatter_dimension=0, tiled=True),
-        lax.psum_scatter(totals[8], "dp", scatter_dimension=0, tiled=True),
-        lax.psum_scatter(totals[9], "dp", scatter_dimension=0, tiled=True),
-        lax.psum_scatter(totals[13], "dp", scatter_dimension=0, tiled=True),
-        lax.psum_scatter(totals[14], "dp", scatter_dimension=0, tiled=True),
-        lax.psum_scatter(totals[15], "dp", scatter_dimension=0, tiled=True),
-    )
-    narrow = lax.psum((totals[3], totals[4], totals[5], totals[11]), "dp")
-    back_out, back_grad = (
-        lax.all_to_all(outs, "dp", split_axis=1, concat_axis=0, tiled=True),
-        lax.all_to_all(grad_all, "dp", split_axis=1, concat_axis=0, tiled=True),
-    )
-    total_seqs = deal_order.shape[0]
-    undo_order = (
-        jnp.zeros((total_seqs,), jnp.int32)
-        .at[deal_order]
-        .set(jnp.arange(total_seqs, dtype=jnp.int32))
-    )
-    home_out = jnp.take(back_out, undo_order, axis=0)
-    home_grad = jnp.take(back_grad, undo_order, axis=0)
-    return (
-        home_out,
-        home_grad,
-        wide[0],
-        wide[1],
-        wide[2],
-        narrow[0],
-        narrow[1],
-        narrow[2],
-        wide[3],
-        wide[6],
-        wide[7],
-        wide[8],
-        wide[4],
-        narrow[3],
-        wide[5],
-        wide[9],
-        wide[10],
-        wide[11],
-    )
+    tens = lax.axis_index("tensor")
+    here = lax.axis_index("dp")
+    half = tokens.shape[1]
+
+    def to_owner(array):
+        mine = lax.dynamic_slice_in_dim(array, tens * groups, groups, 0)
+        moved = lax.all_to_all(mine, "dp", split_axis=0, concat_axis=0, tiled=True)
+        return moved.reshape(groups * half, array.shape[2])
+
+    def to_home(rows):
+        moved = lax.all_to_all(rows.reshape(groups, half, rows.shape[1]), "dp", split_axis=0, concat_axis=0, tiled=True)
+        return lax.all_gather(moved, "tensor", axis=0, tiled=True)
+
+    rows = to_owner(tokens)
+    cot = to_owner(cotangent)
+    ids = lax.dynamic_index_in_dim(landmark_ids, tens * groups + here, 0, keepdims=False)
+    packed = jnp.concatenate([w_query, w_key, w_value, w_out, w_inner, w_outer], axis=1)
+    widths = [w.shape[1] for w in (w_query, w_key, w_value, w_out, w_inner, w_outer)]
+    whole = lax.all_gather(packed, ("tensor", "dp"), axis=0, tiled=True)
+    tn = lax.axis_size("tensor")
+    depth = groups * packed.shape[0]
+    whole = whole.reshape(tn, depth, packed.shape[1])
+    mats = []
+    at = 0
+    for w in widths:
+        mats.append(jnp.concatenate([whole[t, :, at : at + w] for t in range(tn)], axis=1))
+        at += w
+    small = lax.all_gather(
+        jnp.concatenate([b_query, b_value, b_inner, conv_taps.reshape(-1)]), "tensor", axis=0
+    )
+    bq = small[:, : b_query.shape[0]].reshape(-1)
+    at = b_query.shape[0]
+    bv = small[:, at : at + b_value.shape[0]].reshape(-1)
+    at += b_value.shape[0]
+    bi = small[:, at : at + b_inner.shape[0]].reshape(-1)
+    at += b_inner.shape[0]
+    taps = small[:, at:].reshape(-1, conv_taps.shape[1])
+    weights = (mats[0], mats[1], mats[2], bq, bv, taps, mats[3], b_out, first_gain, first_shift,
+               mats[4], bi, mats[5], b_outer, second_gain, second_shift)
+    out_rows, grad_rows, g = sequence_step(rows, cot, ids, weights)
+    wide = [g[0], g[1], g[2], g[6], g[10], g[12]]
+    parts = []
+    for t in range(tn):
+        parts.append(jnp.concatenate([m[:, t * w : (t + 1) * w] for m, w in zip(wide, widths)], axis=1))
+    scat = lax.psum_scatter(
+        jnp.concatenate(parts, axis=0).astype(jnp.bfloat16), ("tensor", "dp"), scatter_dimension=0, tiled=True
+    ).astype(jnp.float32)
+    wgrads = []
+    at = 0
+    for w in widths:
+        wgrads.append(scat[:, at : at + w])
+        at += w
+    vec = jnp.concatenate([g[7], g[8], g[9], g[13], g[14], g[15], g[3], g[4], g[11], g[5].reshape(-1)])
+    vec = lax.psum(vec, ("tensor", "dp"))
+    d = g[7].shape[0]
+    share = d // groups
+    norms = [lax.dynamic_slice_in_dim(vec, k * d + here * share, share, 0) for k in range(6)]
+    at = 6 * d
+    gbq = lax.dynamic_slice_in_dim(vec, at + tens * b_query.shape[0], b_query.shape[0], 0)
+    at += d
+    gbv = lax.dynamic_slice_in_dim(vec, at + tens * b_value.shape[0], b_value.shape[0], 0)
+    at += d
+    gbi = lax.dynamic_slice_in_dim(vec, at + tens * b_inner.shape[0], b_inner.shape[0], 0)
+    at += bi.shape[0]
+    n = conv_taps.size
+    gt = lax.dynamic_slice_in_dim(vec, at + tens * n, n, 0).reshape(conv_taps.shape)
+    return (to_home(out_rows), to_home(grad_rows), wgrads[0], wgrads[1], wgrads[2], gbq, gbv, gt, wgrads[3],
+            norms[0], norms[1], norms[2], wgrads[4], gbi, wgrads[5], norms[3], norms[4], norms[5])
 
 
 def solution(mesh):

time: 1740 us -> 838 us (0.48)
  waiting for transfers between devices: 684 us -> 232 us
  blocking collectives: 370 us -> 53.6 us
  matrix products: 327 us -> 253 us
  other arithmetic: 205 us -> 155 us
    psum x8 -> x0, waiting for transfers between devices: 319 us -> none  [the longest x2 96.4 us: sequence_step(): lax.psum(attn_part.astype(jnp.bfloat16), 'tensor').astype(jnp.float32)]
    all_gather x8 -> x0, blocking collectives: 179 us -> none  [the longest x2 58.6 us: current_weights(): lax.all_gather(w_out, 'dp', axis=0, tiled=True)]
    all_to_all x3 -> x4, waiting for transfers between devices: 111 us -> 10.7 us  [the longest x2 10.7 us: to_home(): lax.all_to_all(rows.reshape(groups, half, rows.shape[1]), 'dp', split_axi...]
    reduce_scatter x6 -> x1, waiting for transfers between devices: 222 us -> 121 us  [local(): lax.psum_scatter(jnp.concatenate(parts, axis=0).astype(jnp.bfloat16), ('t...]
    all_to_all x1 -> x0, blocking collectives: 77 us -> none  [local(): lax.all_to_all(arranged_cot, 'dp', split_axis=0, concat_axis=1, tiled=True)]
    all_gather x4 -> x3, waiting for transfers between devices: 25.4 us -> 99.5 us  [the longest x1 99.5 us: local(): whole = lax.all_gather(packed, ('tensor', 'dp'), axis=0, tiled=True)]
    psum x1, blocking collectives: 114 us -> 45.3 us  [local(): vec = lax.psum(vec, ('tensor', 'dp'))]
    while x883 -> x0, local copies, waits for them, and re-layouts: 46.5 us -> none
  transfers between devices with their start and end apart: 21 -> 8, of which waited for: 16 -> 3; matrix products, arithmetic and copies ran while one was open for 10% -> 32% of each run, Pallas kernels for 0% -> 0%
where the time goes in v1:
time: 838 us; the launch traced here: 833 us
  matrix products  253 us (30%)
  waiting for transfers between devices  232 us (28%)
  other arithmetic  155 us (18%)
  local copies, waits for them, and re-layouts  97 us (12%)
  blocking collectives  53.6 us (6%)
  starting transfers between devices  24.9 us (3%)
  between operations  17.9 us (2%)
    dot_general x27, matrix products, partial_product(): return jnp.einsum(spec, left, right, preferred_element_type=jnp.float32)  142 us
    reduce_scatter x1, waiting for transfers between devices, local(): lax.psum_scatter(jnp.concatenate(parts, axis=0).astype(jnp.bfloat16), ('t...  121 us
    all_gather x1, waiting for transfers between devices, local(): whole = lax.all_gather(packed, ('tensor', 'dp'), axis=0, tiled=True)  99.5 us
    dot_general x77, matrix products, contract_dims(): return jnp.einsum(spec, left, right, precision=lax.Precision.HIGHEST)  61.6 us
    reduce_sum x3, other arithmetic, depthwise(): taps[:, offset][None, :, None] * padded[offset:offset + length]  51.9 us
    psum x1, blocking collectives, local(): vec = lax.psum(vec, ('tensor', 'dp'))  45.3 us
    unnamed x422, local copies, waits for them, and re-layouts  44.6 us
    dot_general x1, matrix products, sequence_step(): jnp.dot(hidden_low, w_inner, preferred_element_type=single_float)  37.7 us
  transfers between devices with their start and end apart: 8, of which 3 were waited for; matrix products, arithmetic and copies ran while one was open for 32% of the time, Pallas kernels for 0%

profile of v1, /device:TPU:0, one launch (start us, length us, event | category | flops | bytes accessed | tf_op | source)
XLA Modules:
  0.0 833.2 jit_solution(7931473851270329907)
XLA Ops:
  17.6 7.4 all-to-all-start
  26.7 8.2 all-reduce.67
  41.7 2.7 constant_dynamic-slice_fusion
  44.4 99.5 %all-gather.5.cloned.1.call-done = bf16[1536,4608]{1,0:T(8,128)(2,1)} async-done(((bf16[48,4608]{1,0:T(8,128)(2,1)}), bf16[1536,4608]{1,0:T(8,128)(2,1)}) %all-gather.5.cloned.1.call-update) | async-done | bytes 14155792 | tf_op jit(solution)/shard_map/all_gather | solution.py:264
  143.9 4.4 slice_bitcast_fusion.5
  148.3 7.1 slice_bitcast_fusion.1
  155.4 4.7 all-to-all-start.2
  160.2 3.1 multiply_convert_fusion.4
  166.8 2.2 fusion.178
  186.0 4.2 fusion.171
  190.3 5.3 fusion.172
  199.8 3.1 copy-done.22
  205.0 29.3 %fusion.50 = bf16[1024,12,64]{0,2,1:T(8,128)(2,1)} fusion(f32[1024,12,64]{0,2,1:T(8,128)S(1)} %convert_select_fusion, bf16[12,64,64]{2,1,0:T(8,128)(2,1)} %convolution_convert_fusion.8, f32[12]{0:T(128)} %get-tuple-element.56, f32[12]{0:T(128)} %get-tuple-element.57, f32[12]{0:T(128)} %get-tuple-element.58, f32[12]{0:T(128)} %get-tuple-element.59, ...), kind=kOutput, calls=%fused_computation.146 | convolution fusion | flops 153354240 | bytes 6391344 | tf_op jit(solution)/shard_map/azr,azs->ras/dot_general | solution.py:15
  234.3 4.0 fusion.173
  241.1 37.7 %multiply_convert_fusion = (bf16[1024,3072]{1,0:T(8,128)(2,1)S(1)}, f32[1024,3072]{1,0:T(8,128)}, f32[1024,3072]{1,0:T(8,128)}) fusion(f32[3072]{0:T(1024)S(1)} %copy-done.148, bf16[768,1536]{1,0:T(8,128)(2,1)S(1)} %copy-done.87, bf16[768,1536]{1,0:T(8,128)(2,1)S(1)} %copy-done.88, f32[1024,768]{1,0:T(8,128)S(1)} %get-tuple-element.179, ...), kind=kOutput, calls=%fused_computation.72 | convolution fusion | flops 5052825600 | bytes 39348224 | tf_op jit(solution)/shard_map/dot_general | solution.py:136
  278.9 6.1 fusion.174
  285.8 3.3 fusion.49
  289.0 4.1 fusion.158
  293.2 18.2 %fusion.175 = (f32[3072]{0:T(1024)}, bf16[1024,3072]{1,0:T(8,128)(2,1)}) fusion(f32[1024,3072]{1,0:T(8,128)} %get-tuple-element.93, bf16[768,1536]{1,0:T(8,128)(2,1)} %get-tuple-element.95, bf16[768,1536]{1,0:T(8,128)(2,1)} %get-tuple-element.94, f32[1024,768]{1,0:T(8,128)} %get-tuple-element.91, f32[1024]{0:T(1024)S(1)} %negate_multiply_fusion.2, ...), kind=kOutput, calls=%fused_computation.491 | convolution fusion | flops 4893176832 | bytes 39350272 | tf_op jit(solution)/shard_map/nd,df->nf/dot_general | solution.py:15
  311.4 11.6 %multiply_reduce_fusion.1 = (f32[768]{0:T(1024)}, f32[1024]{0:T(1024)S(1)}, f32[768]{0:T(1024)}, f32[1024,768]{1,0:T(8,128)S(1)}) fusion(f32[1024,768]{1,0:T(8,128)} %copy-done.27, f32[1024]{0:T(1024)S(1)} %fusion.134, f32[1024]{0:T(1024)S(1)} %broadcast_multiply_fusion.1, f32[768]{0:T(1024)} %convert_element_type.203, ...), kind=kOutput, calls=%fused_computation.148 | convolution fusion | flops 4849136640 | bytes 20472832 | tf_op jit(solution)/shard_map/nf,df->nd/dot_general | solution.py:15
  323.1 2.3 fusion.157
  325.5 2.4 multiply_reduce_fusion
  329.0 15.6 %fusion.27 = (f32[12]{0:T(128)}, f32[12]{0:T(128)}, f32[12]{0:T(128)}, f32[12]{0:T(128)}, f32[12]{0:T(128)}, /*index=5*/f32[12]{0:T(128)}, f32[12]{0:T(128)}, f3...) fusion(bf16[1024,12,64]{0,2,1:T(8,128)(2,1)S(1)} %bitcast.307, ...), kind=kLoop, calls=%fused_computation.111 | loop fusion | flops 25952088 | bytes 17302368 | tf_op jit(solution)/shard_map/transpose(jvp())/reduce_sum | solution.py:35
  344.7 5.2 fusion.86
  389.5 19.3 %convert_multiply_fusion.64 = (f32[1024,12,64]{0,2,1:T(8,128)}, f32[1024,12,64]{0,2,1:T(8,128)}, f32[1024,12,64]{0,2,1:T(8,128)}, f32[1024,12,64]{0,2,1:T(8,128)...) fusion(bf16[1024,12,64]{0,2,1:T(8,128)(2,1)} %bitcast.309, ...), kind=kLoop, calls=%fused_computation.67 | loop fusion | flops 14942208 | bytes 58196832 | tf_op jit(solution)/shard_map/transpose(jvp())/mul | solution.py:35
  408.8 13.2 %convert_multiply_fusion.44 = (f32[1024,12,64]{0,2,1:T(8,128)}, f32[1024,12,64]{0,2,1:T(8,128)}, f32[1024,12,64]{0,2,1:T(8,128)}, f32[1024,12,64]{0,2,1:T(8,128)...) fusion(bf16[1024,12,64]{0,2,1:T(8,128)(2,1)} %bitcast.310, ...), kind=kLoop, calls=%fused_computation.47 | loop fusion | flops 9437184 | bytes 36176400 | tf_op jit(solution)/shard_map/transpose(jvp())/mul | solution.py:35
  437.1 2.6 convolution_convert_fusion.5
  439.7 3.2 fusion.92
  445.1 3.1 fusion.93
  448.3 33.5 %pad_add_fusion = f32[1056,12,64]{0,2,1:T(8,128)S(1)} fusion(f32[1024,12,64]{0,2,1:T(8,128)} %get-tuple-element.143, f32[1024,12,64]{0,2,1:T(8,128)} %get-tuple-element.142, f32[1024,12,64]{0,2,1:T(8,128)} %get-tuple-element.141, f32[1024,12,64]{0,2,1:T(8,128)} %get-tuple-element.140, f32[1024,12,64]{0,2,1:T(8,128)} %get-tuple-element.139, ...), kind=kLoop, calls=%fused_computation.92 | loop fusion | flops 21086208 | bytes 88178688 | tf_op jit(solution)/shard_map/transpose(jvp())/add_any | solution.py:35
  481.8 13.9 %fusion.160 = (f32[12,64]{1,0:T(8,128)S(1)}, bf16[1024,12,64]{0,2,1:T(8,128)(2,1)S(1)}) fusion(bf16[12,64,64]{2,1,0:T(8,128)(2,1)} %convolution_convert_fusion.7, f32[12,64,1024]{2,1,0:T(8,128)} %get-tuple-element.175, f32[12,64]{1,0:T(8,128)S(1)} %copy-done.140, f32[1024,12,64]{0,2,1:T(8,128)} %get-tuple-element.116, ...), kind=kOutput, calls=%fused_computation.476 | convolution fusion | flops 110099712 | bytes 26844160 | tf_op jit(solution)/shard_map/azr,azs->ras/dot_general | solution.py:15
  495.7 3.3 add_convert_fusion
  499.1 6.4 all-to-all-start.3
  505.4 2.3 fusion.164
  509.9 3.3 convolution_convert_fusion.6
  516.4 3.3 convolution_convert_fusion.4
  522.9 2.9 convolution_convert_fusion.3
  547.4 6.1 all-to-all-start.1
  554.4 9.9 %convolution_convert_fusion = bf16[768,3072]{1,0:T(8,128)(2,1)} fusion(bf16[1024,3072]{1,0:T(8,128)(2,1)} %copy-done.194, f32[1024,768]{1,0:T(8,128)} %get-tuple-element.91, f32[1024]{0:T(1024)S(1)} %copy-done.142), kind=kOutput, calls=%fused_computation.86 | convolution fusion | flops 4835770368 | bytes 14159872 | tf_op jit(solution)/shard_map/nd,nf->df/dot_general | solution.py:15
  564.4 10.6 %convolution_convert_fusion.1 = bf16[768,3072]{1,0:T(8,128)(2,1)} fusion(bf16[1024,3072]{1,0:T(8,128)(2,1)} %get-tuple-element.195, f32[1024,768]{1,0:T(8,128)S(1)} %copy-done.29, f32[768]{0:T(1024)S(1)} %copy-done.155, f32[768]{0:T(1024)} %convert_element_type.203, f32[1024]{0:T(1024)S(1)} %copy-done.144, f32[1024]{0:T(1024)S(1)} %broadcast_multiply_fusion.1), kind=kOutput, calls=%fused_computation.87 | convolution fusion | flops 4838129664 | bytes 14170112 | tf_op jit(solution)/shard_map/nd,nf->df/dot_general | solution.py:15
  575.0 10.7 %all-to-all-done.1 = bf16[16,64,768]{2,1,0:T(8,128)(2,1)} async-done(((bf16[16,64,768]{2,1,0:T(8,128)(2,1)}), bf16[16,64,768]{2,1,0:T(8,128)(2,1)}, u32[]{:S(2)}, u32[]{:S(2)}) %all-to-all-start.1) | async-done | bytes 1572896 | tf_op jit(solution)/shard_map/all_to_all | solution.py:256
  588.0 5.0 slice_dynamic-update-slice_fusion.3
  593.0 2.5 slice_dynamic-update-slice_fusion.2
  595.5 11.2 %pad_maximum_fusion = bf16[1536,4608]{1,0:T(8,128)(2,1)} fusion(bf16[768,4608]{1,0:T(8,128)(2,1)} %get-tuple-element.107, bf16[768,4608]{1,0:T(8,128)(2,1)} %get-tuple-element.106), kind=kLoop, calls=%fused_computation.69 | loop fusion | flops 28311552 | bytes 28311552 | tf_op jit(solution)/shard_map/concatenate | solution.py:291
  608.8 36.2 %fusion.9 = (f32[12]{0:T(128)S(1)}, f32[12]{0:T(128)S(1)}, f32[12]{0:T(128)S(1)}, f32[12]{0:T(128)S(1)}, f32[12]{0:T(128)S(1)}, /*index=5*/f32[12]{0:T(128)S(1)}...) fusion(bf16[1024,12,64]{0,2,1:T(8,128)(2,1)} %bitcast.311, ...), kind=kLoop, calls=%fused_computation.93 | loop fusion | flops 29097768 | bytes 4719456 | tf_op jit(solution)/shard_map/transpose(jvp())/reduce_sum | solution.py:35
  647.9 45.3 %psum.7 = f32[9612]{0:T(1024)S(1)} all-reduce(f32[9612]{0:T(1024)S(1)} %constant_dynamic-update-slice_fusion.18), channel_id=1, replica_groups=mesh['dp'=16,'tensor'=2] {'tensor','dp'}, use_global_device_ids=true, to_apply=%region_64.65 | all-reduce | flops 9612 | bytes 76896 | tf_op jit(solution)/shard_map/psum | solution.py:299
  695.9 121.4 %reduce-scatter.2.cloned.1.call-done = bf16[48,4608]{1,0:T(8,128)(2,1)} async-done(((bf16[1536,4608]{1,0:T(8,128)(2,1)}), bf16[48,4608]{1,0:T(8,128)(2,1)}) %reduce-scatter.2.cloned.1.call-update) | async-done | bytes 442384 | tf_op jit(solution)/shard_map/reduce_scatter | solution.py:290
  820.7 4.0 copy.299
  (596 shorter events, 150.2 us)
Async XLA Ops:
  7.2 136.7 %all-gather.5.cloned.1.call-start = ((), (), s32[]{:S(2)}) async-start(), calls=%async_computation.5 | async-start | bytes 14598144 | tf_op jit(solution)/shard_map/all_gather | solution.py:264
  16.2 18.9 %copy-start.178 = (bf16[768]{0:T(1024)(128)(2,1)S(1)}, bf16[768]{0:T(1024)(128)(2,1)}, u32[]{:S(2)}) copy-start(bf16[768]{0:T(1024)(128)(2,1)} %param.29) | copy-start | bytes 4612
  16.2 19.5 %copy-start.179 = (bf16[768]{0:T(1024)(128)(2,1)S(1)}, bf16[768]{0:T(1024)(128)(2,1)}, u32[]{:S(2)}) copy-start(bf16[768]{0:T(1024)(128)(2,1)} %param.30) | copy-start | bytes 4612
  16.2 20.1 %copy-start.180 = (bf16[768]{0:T(1024)(128)(2,1)S(1)}, bf16[768]{0:T(1024)(128)(2,1)}, u32[]{:S(2)}) copy-start(bf16[768]{0:T(1024)(128)(2,1)} %param.31) | copy-start | bytes 4612
  16.3 20.7 %copy-start.181 = (bf16[768]{0:T(1024)(128)(2,1)S(1)}, bf16[768]{0:T(1024)(128)(2,1)}, u32[]{:S(2)}) copy-start(bf16[768]{0:T(1024)(128)(2,1)} %param.35) | copy-start | bytes 4612
  16.3 21.3 %copy-start.182 = (bf16[768]{0:T(1024)(128)(2,1)S(1)}, bf16[768]{0:T(1024)(128)(2,1)}, u32[]{:S(2)}) copy-start(bf16[768]{0:T(1024)(128)(2,1)} %param.36) | copy-start | bytes 4612
  16.3 21.8 %copy-start.183 = (bf16[768]{0:T(1024)(128)(2,1)S(1)}, bf16[768]{0:T(1024)(128)(2,1)}, u32[]{:S(2)}) copy-start(bf16[768]{0:T(1024)(128)(2,1)} %param.37) | copy-start | bytes 4612
  17.6 137.8 %all-to-all-start = ((bf16[16,64,768]{2,1,0:T(8,128)(2,1)}), bf16[16,64,768]{2,1,0:T(8,128)(2,1)S(1)}, u32[]{:S(2)}, u32[]{:S(2)}) async-start(bf16[16,64,768]{2,1,0:T(8,128)(2,1)} %constant_dynamic-slice_fusion.2), calls=%async_computation | async-start | bytes 3145728 | tf_op jit(solution)/shard_map/all_to_all | solution.py:252
  39.5 126.2 %copy-start.135 = (s32[1,1024]{1,0:T(1,128)}, s32[1,1024]{1,0:T(1,128)S(1)}, u32[]{:S(2)}) copy-start(s32[1,1024]{1,0:T(1,128)S(1)} %constant_dynamic-slice_fusion.1) | copy-start | bytes 12292
  40.5 143.9 %copy-start.45 = (f32[64,64]{1,0:T(8,128)}, f32[64,64]{1,0:T(8,128)S(1)}, u32[]{:S(2)}) copy-start(f32[64,64]{1,0:T(8,128)S(1)} %get-tuple-element.198) | copy-start | bytes 49156
  41.7 124.0 %copy-start.190 = (f32[64]{0:T(128)}, f32[64]{0:T(128)S(1)}, u32[]{:S(2)}) copy-start(f32[64]{0:T(128)S(1)} %convert_reduce_fusion.1) | copy-start | bytes 772
  44.4 154.9 %copy-start.149 = (pred[1024]{0:T(1024)(128)(4,1)}, pred[1024]{0:T(1024)(128)(4,1)S(1)}, u32[]{:S(2)}) copy-start(pred[1024]{0:T(1024)(128)(4,1)S(1)} %broadcast_compare_fusion) | copy-start | bytes 3076
  155.4 130.2 %all-to-all-start.2 = ((bf16[16,64,768]{2,1,0:T(8,128)(2,1)}), bf16[16,64,768]{2,1,0:T(8,128)(2,1)}, u32[]{:S(2)}, u32[]{:S(2)}) async-start(bf16[16,64,768]{2,1,0:T(8,128)(2,1)} %constant_dynamic-slice_fusion), calls=%async_computation.2 | async-start | bytes 3145728 | tf_op jit(solution)/shard_map/all_to_all | solution.py:252
  164.2 21.8 %copy-start.118 = (bf16[64,12,64]{2,0,1:T(8,128)(2,1)}, bf16[64,12,64]{2,0,1:T(8,128)(2,1)S(1)}, u32[]{:S(2)}) copy-start(bf16[64,12,64]{2,0,1:T(8,128)(2,1)S(1)} %fusion.82) | copy-start | bytes 294916
  169.3 14.2 %copy-start.6 = (f32[12,64,64]{1,2,0:T(8,128)}, f32[12,64,64]{1,2,0:T(8,128)S(1)}, u32[]{:S(2)}) copy-start(f32[12,64,64]{1,2,0:T(8,128)S(1)} %get-tuple-element.173) | copy-start | bytes 589828
  169.3 14.2 %copy-start.129 = (f32[12,64]{1,0:T(8,128)}, f32[12,64]{1,0:T(8,128)S(1)}, u32[]{:S(2)}) copy-start(f32[12,64]{1,0:T(8,128)S(1)} %get-tuple-element.172) | copy-start | bytes 9220
  186.0 17.5 %copy-start.63 = (f32[12,64,64]{2,1,0:T(8,128)}, f32[12,64,64]{2,1,0:T(8,128)S(1)}, u32[]{:S(2)}) copy-start(f32[12,64,64]{2,1,0:T(8,128)S(1)} %convolution_multiply_fusion.1) | copy-start | bytes 589828
  238.3 40.6 %copy-start.27 = (f32[1024,768]{1,0:T(8,128)}, f32[1024,768]{1,0:T(8,128)S(1)}, u32[]{:S(2)}) copy-start(f32[1024,768]{1,0:T(8,128)S(1)} %get-tuple-element.179) | copy-start | bytes 9437188
  238.9 84.1 %copy-start.143 = (f32[1024]{0:T(1024)}, f32[1024]{0:T(1024)S(1)}, u32[]{:S(2)}) copy-start(f32[1024]{0:T(1024)S(1)} %fusion.134) | copy-start | bytes 12292
  241.1 37.8 %copy-start.89 = (bf16[768,1536]{1,0:T(8,128)(2,1)S(1)}, bf16[768,1536]{1,0:T(8,128)(2,1)}, u32[]{:S(2)}) copy-start(bf16[768,1536]{1,0:T(8,128)(2,1)} %get-tuple-element.94) | copy-start | bytes 7077892
  241.1 37.8 %copy-start.90 = (bf16[768,1536]{1,0:T(8,128)(2,1)S(1)}, bf16[768,1536]{1,0:T(8,128)(2,1)}, u32[]{:S(2)}) copy-start(bf16[768,1536]{1,0:T(8,128)(2,1)} %get-tuple-element.95) | copy-start | bytes 7077892
  241.1 37.8 %copy-start.156 = (f32[768]{0:T(1024)S(1)}, f32[768]{0:T(1024)}, u32[]{:S(2)}) copy-start(f32[768]{0:T(1024)} %convert_element_type.209) | copy-start | bytes 9220
  293.2 18.2 %copy-start.141 = (f32[1024]{0:T(1024)}, f32[1024]{0:T(1024)S(1)}, u32[]{:S(2)}) copy-start(f32[1024]{0:T(1024)S(1)} %negate_multiply_fusion.2) | copy-start | bytes 12292
  293.2 18.2 %copy-start.25 = (f32[1024,768]{1,0:T(8,128)S(1)}, f32[1024,768]{1,0:T(8,128)}, u32[]{:S(2)}) copy-start(f32[1024,768]{1,0:T(8,128)} %get-tuple-element.91) | copy-start | bytes 9437188
  448.3 33.5 %copy-start.140 = (f32[12,64]{1,0:T(8,128)S(1)}, f32[12,64]{1,0:T(8,128)}, u32[]{:S(2)}) copy-start(f32[12,64]{1,0:T(8,128)} %copy-done.138) | copy-start | bytes 9220
  448.3 33.5 %copy-start.151 = (pred[1024]{0:T(1024)(128)(4,1)S(1)}, pred[1024]{0:T(1024)(128)(4,1)}, u32[]{:S(2)}) copy-start(pred[1024]{0:T(1024)(128)(4,1)} %copy-done.149) | copy-start | bytes 3076
  481.7 14.0 %copy-start.85 = (f32[1024,768]{1,0:T(8,128)S(1)}, f32[1024,768]{1,0:T(8,128)}, u32[]{:S(2)}) copy-start(f32[1024,768]{1,0:T(8,128)} %fusion.92) | copy-start | bytes 9437188
  499.1 48.4 %all-to-all-start.3 = ((bf16[16,64,768]{2,1,0:T(8,128)(2,1)}), bf16[16,64,768]{2,1,0:T(8,128)(2,1)}, u32[]{:S(2)}, u32[]{:S(2)}) async-start(bf16[16,64,768]{2,1,0:T(8,128)(2,1)} %bitcast.322), calls=%async_computation.3 | async-start | bytes 3145728 | tf_op jit(solution)/shard_map/all_to_all | solution.py:256
  547.4 38.2 %all-to-all-start.1 = ((bf16[16,64,768]{2,1,0:T(8,128)(2,1)}), bf16[16,64,768]{2,1,0:T(8,128)(2,1)}, u32[]{:S(2)}, u32[]{:S(2)}) async-start(bf16[16,64,768]{2,1,0:T(8,128)(2,1)} %bitcast.323), calls=%async_computation.1 | async-start | bytes 3145728 | tf_op jit(solution)/shard_map/all_to_all | solution.py:256
  553.6 142.3 %all-gather.9.cloned.1.call-start = ((), (), s32[]{:S(2)}) async-start(), calls=%async_computation.7 | async-start | bytes 4718592 | tf_op jit(solution)/shard_map/all_gather | solution.py:257
  554.4 141.5 %all-gather.7.cloned.1.call-start = ((), (), s32[]{:S(2)}) async-start(), calls=%async_computation.6 | async-start | bytes 4718592 | tf_op jit(solution)/shard_map/all_gather | solution.py:257
  585.7 231.7 %reduce-scatter.2.cloned.1.call-start = ((), (), s32[]{:S(2)}) async-start(), calls=%async_computation.8 | async-start | bytes 14598144 | tf_op jit(solution)/shard_map/reduce_scatter | solution.py:290
  606.8 38.3 %copy-start.159 = (f32[12]{0:T(128)S(1)}, f32[12]{0:T(128)}, u32[]{:S(2)}) copy-start(f32[12]{0:T(128)} %get-tuple-element.40) | copy-start | bytes 148
  606.8 38.3 %copy-start.160 = (f32[12]{0:T(128)S(1)}, f32[12]{0:T(128)}, u32[]{:S(2)}) copy-start(f32[12]{0:T(128)} %get-tuple-element.41) | copy-start | bytes 148
  606.8 38.3 %copy-start.161 = (f32[12]{0:T(128)S(1)}, f32[12]{0:T(128)}, u32[]{:S(2)}) copy-start(f32[12]{0:T(128)} %get-tuple-element.42) | copy-start | bytes 148
  606.8 38.3 %copy-start.162 = (f32[12]{0:T(128)S(1)}, f32[12]{0:T(128)}, u32[]{:S(2)}) copy-start(f32[12]{0:T(128)} %get-tuple-element.43) | copy-start | bytes 148
  606.8 38.3 %copy-start.163 = (f32[12]{0:T(128)S(1)}, f32[12]{0:T(128)}, u32[]{:S(2)}) copy-start(f32[12]{0:T(128)} %get-tuple-element.44) | copy-start | bytes 148
  606.8 38.3 %copy-start.164 = (f32[12]{0:T(128)S(1)}, f32[12]{0:T(128)}, u32[]{:S(2)}) copy-start(f32[12]{0:T(128)} %get-tuple-element.45) | copy-start | bytes 148
  606.9 38.3 %copy-start.165 = (f32[12]{0:T(128)S(1)}, f32[12]{0:T(128)}, u32[]{:S(2)}) copy-start(f32[12]{0:T(128)} %get-tuple-element.46) | copy-start | bytes 148
  606.9 38.3 %copy-start.166 = (f32[12]{0:T(128)S(1)}, f32[12]{0:T(128)}, u32[]{:S(2)}) copy-start(f32[12]{0:T(128)} %get-tuple-element.47) | copy-start | bytes 148
  606.9 38.3 %copy-start.167 = (f32[12]{0:T(128)S(1)}, f32[12]{0:T(128)}, u32[]{:S(2)}) copy-start(f32[12]{0:T(128)} %get-tuple-element.48) | copy-start | bytes 148
  606.9 38.3 %copy-start.168 = (f32[12]{0:T(128)S(1)}, f32[12]{0:T(128)}, u32[]{:S(2)}) copy-start(f32[12]{0:T(128)} %get-tuple-element.49) | copy-start | bytes 148
  606.9 38.3 %copy-start.169 = (f32[12]{0:T(128)S(1)}, f32[12]{0:T(128)}, u32[]{:S(2)}) copy-start(f32[12]{0:T(128)} %get-tuple-element.50) | copy-start | bytes 148
  606.9 38.3 %copy-start.170 = (f32[12]{0:T(128)S(1)}, f32[12]{0:T(128)}, u32[]{:S(2)}) copy-start(f32[12]{0:T(128)} %get-tuple-element.51) | copy-start | bytes 148
  606.9 38.3 %copy-start.171 = (f32[12]{0:T(128)S(1)}, f32[12]{0:T(128)}, u32[]{:S(2)}) copy-start(f32[12]{0:T(128)} %get-tuple-element.52) | copy-start | bytes 148
  606.9 38.3 %copy-start.172 = (f32[12]{0:T(128)S(1)}, f32[12]{0:T(128)}, u32[]{:S(2)}) copy-start(f32[12]{0:T(128)} %get-tuple-element.53) | copy-start | bytes 148
  608.8 37.1 %copy-start.158 = (f32[768]{0:T(1024)S(1)}, f32[768]{0:T(1024)}, u32[]{:S(2)}) copy-start(f32[768]{0:T(1024)} %get-tuple-element.18) | copy-start | bytes 9220
  608.8 37.1 %copy-start.157 = (f32[768]{0:T(1024)S(1)}, f32[768]{0:T(1024)}, u32[]{:S(2)}) copy-start(f32[768]{0:T(1024)} %get-tuple-element.54) | copy-start | bytes 9220
  (157 other events, 689.5 us)
Sparse Core Ops, SparseCore 0:
  16.3 127.5 all-gather.4
  556.0 46.1 all-gather.8
  603.8 44.9 all-gather.6
  654.6 162.7 reduce-scatter.1

commit v2 on v1

v2 whole, which is shorter than its diff:
```python
import functools
import jax
import jax.numpy as jnp
from jax import lax
from jax.experimental import pallas as pl
from jax.experimental.pallas import tpu as pltpu

from jax.sharding import PartitionSpec as P

F32 = jnp.float32
BF = jnp.bfloat16
LAND = 64
ITERS = 6
HEADS_HERE = 6
ROWS_BQ, ROWS_BV, ROWS_BI, ROWS_TAPS, ROWS_FLIP = 0, 3, 6, 18, 24
EDGE = 112


def nn(a, b):
    return lax.dot_general(a, b, (((1,), (0,)), ((), ())), preferred_element_type=F32)


def nt(a, b):
    return lax.dot_general(a, b, (((1,), (1,)), ((), ())), preferred_element_type=F32)


def turn(a):
    return jnp.transpose(a, (1, 0))


def same_head(rows, columns):
    left = lax.broadcasted_iota(jnp.int32, (rows, columns), 0) // LAND
    right = lax.broadcasted_iota(jnp.int32, (rows, columns), 1) // LAND
    return left == right


def spread(small):
    n = small.shape[1] // LAND
    tall = jnp.concatenate([small] * n, axis=0)
    return jnp.where(same_head(n * LAND, n * LAND), tall, jnp.zeros_like(tall))


def gather_diag(full):
    n = full.shape[1] // LAND
    lane = lax.broadcasted_iota(jnp.int32, (LAND, full.shape[1]), 1) // LAND
    out = full[:LAND]
    for h in range(1, n):
        out = jnp.where(lane == h, full[h * LAND : (h + 1) * LAND], out)
    return out


def halves(a):
    high = a.astype(BF)
    return high, (a - high.astype(F32)).astype(BF)


def pair_nn(a, b):
    ah, al = halves(a)
    bh, bl = halves(b)
    bh, bl = spread(bh), spread(bl)
    wide = jnp.concatenate([bh, bl], axis=1)
    r = nn(jnp.concatenate([ah, al], axis=1), jnp.concatenate([wide, wide], axis=0))
    return r[:, : 2 * LAND] + r[:, 2 * LAND :]


def pair_nt(a, b):
    ah, al = halves(a)
    bh, bl = halves(b)
    bh, bl = spread(bh), spread(bl)
    tall = jnp.concatenate([bh, bl], axis=0)
    r = nt(jnp.concatenate([ah, al], axis=1), jnp.concatenate([tall, tall], axis=1))
    return r[:, : 2 * LAND] + r[:, 2 * LAND :]


def pair_turn(a):
    t = turn(a)
    return jnp.concatenate([t[:LAND], t[LAND:]], axis=1)


def pair_sum(a):
    left = lax.broadcasted_iota(jnp.int32, a.shape, 1) < LAND
    low = jnp.sum(jnp.where(left, a, 0.0), axis=1, keepdims=True)
    high = jnp.sum(jnp.where(left, 0.0, a), axis=1, keepdims=True)
    return jnp.where(left, low, high)


def pair_softmax(a):
    left = lax.broadcasted_iota(jnp.int32, a.shape, 1) < LAND
    low = jnp.max(jnp.where(left, a, -1e30), axis=1, keepdims=True)
    high = jnp.max(jnp.where(left, -1e30, a), axis=1, keepdims=True)
    e = jnp.exp(a - jnp.where(left, low, high))
    return e / pair_sum(e)


def pair_eye():
    r = lax.broadcasted_iota(jnp.int32, (LAND, 2 * LAND), 0)
    c = lax.broadcasted_iota(jnp.int32, (LAND, 2 * LAND), 1) % LAND
    return jnp.where(r == c, 1.0, 0.0).astype(F32)


def toeplitz(row, size, width):
    return pltpu.roll(jnp.broadcast_to(row, (size, width)), 0, 1, stride=1, stride_axis=0)


def blocks_of(ref, lower, block):
    length = ref.shape[1] - 256
    return jnp.concatenate(
        [ref[lower : lower + LAND, at : at + block + 256] for at in range(0, length, block)], axis=0
    )


def unblock(stacked, block):
    n = stacked.shape[0] // LAND
    return jnp.concatenate([stacked[i * LAND : (i + 1) * LAND] for i in range(n)], axis=1)


def own_sequence():
    return lax.axis_index("tensor") * lax.axis_size("dp") + lax.axis_index("dp")


def side_row(small_ref, t, first, count):
    return jnp.concatenate([small_ref[t, r : r + 1, :] for r in range(first, first + count)], axis=1)


def band_of(small_ref, head, first):
    t, h = head // HEADS_HERE, head % HEADS_HERE
    row = small_ref[t, first + h : first + h + 1, :]
    row = jnp.concatenate([row, jnp.zeros((1, 384), F32)], axis=1)
    return toeplitz(pltpu.roll(row, EDGE, 1), 256, 512).astype(BF)


def attend_forward(x_ref, w_ref, small_ref, ids_ref,
                   q_ref, k_ref, v_ref, near_ref, far_ref, ctx_ref, lq_ref, lk_ref, mix_ref, sum_ref, ker_ref,
                   z_ref, a_ref, v2_ref, w2_ref, pad_ref):
    length, width = x_ref.shape
    tn = w_ref.shape[0]
    cols = width // tn
    scale = LAND ** -0.25
    rows_at = 256
    pairs = width // 128
    groups = width // 256
    bq = [side_row(small_ref, t, ROWS_BQ, 3) for t in range(tn)]
    bv = [side_row(small_ref, t, ROWS_BV, 3) for t in range(tn)]

    def project(i, carry):
        at = pl.ds(pl.multiple_of(i * rows_at, rows_at), rows_at)
        for t in range(tn):
            out = nn(x_ref[at, :], w_ref[t])
            own = slice(t * cols, (t + 1) * cols)
            q_ref[at, own] = ((out[:, :cols] + bq[t]) * scale).astype(BF)
            k_ref[at, own] = (out[:, cols : 2 * cols] * scale).astype(BF)
            v_ref[at, own] = (out[:, 2 * cols :] + bv[t]).astype(BF)
        return carry

    lax.fori_loop(0, length // rows_at, project, 0)

    ids = ids_ref[pl.ds(own_sequence(), 1), :]
    member = jnp.where(lax.broadcasted_iota(jnp.int32, (LAND, length), 0) == ids, 1.0, 0.0).astype(F32)
    count = jnp.sum(member, axis=1, keepdims=True)
    member = member.astype(BF)
    valid = ids < LAND
    lq_ref[...] = (nn(member, q_ref[...]) / count).astype(BF)
    lk_ref[...] = (nn(member, k_ref[...]) / count).astype(BF)

    eye = pair_eye()
    for p in range(pairs):
        own = slice(p * 128, (p + 1) * 128)
        scores = nt(lq_ref[:, own], spread(lk_ref[:, own]))
        kernel = pair_softmax(scores)
        ker_ref[:, own] = kernel
        left = lax.broadcasted_iota(jnp.int32, kernel.shape, 1) < LAND
        total = jnp.sum(pair_sum(kernel * kernel), axis=0, keepdims=True)
        z_ref[0, :, own] = pair_turn(kernel) / total

    for g in range(groups):
        own = slice(g * 256, (g + 1) * 256)
        scores = nt(spread(lk_ref[:, own]), q_ref[:, own]).reshape(4, LAND, length)
        scores = jnp.exp(scores - jnp.max(scores, axis=1, keepdims=True))
        scores = scores / jnp.sum(scores, axis=1, keepdims=True)
        near_ref[own, :] = scores.reshape(256, length).astype(BF)
        scores = nt(spread(lq_ref[:, own]), k_ref[:, own])
        scores = jnp.where(valid, scores, -1e30)
        scores = jnp.exp(scores - jnp.max(scores, axis=1, keepdims=True))
        scores = scores / jnp.sum(scores, axis=1, keepdims=True)
        far_ref[own, :] = scores.astype(BF)
        sum_ref[:, own] = gather_diag(nn(far_ref[own, :], v_ref[:, own]))

    def iterate(n, carry):
        for p in range(pairs):
            own = slice(p * 128, (p + 1) * 128)
            z = z_ref[n, :, own]
            a = pair_nn(ker_ref[:, own], z)
            v2 = 15.0 * eye - pair_nn(a, 7.0 * eye - a)
            w2 = 13.0 * eye - pair_nn(a, v2)
            a_ref[n, :, own] = a
            v2_ref[n, :, own] = v2
            w2_ref[n, :, own] = w2
            z_ref[n + 1, :, own] = 0.25 * pair_nn(z, w2)
        return carry

    lax.fori_loop(0, ITERS, iterate, 0)

    for p in range(pairs):
        own = slice(p * 128, (p + 1) * 128)
        mix_ref[:, own] = pair_nn(z_ref[ITERS, :, own], sum_ref[:, own]).astype(BF)

    pad_ref[...] = jnp.zeros_like(pad_ref)
    for g in range(groups):
        own = slice(g * 256, (g + 1) * 256)
        att = nn(turn(spread(mix_ref[:, own])), near_ref[own, :])
        vt = turn(v_ref[:, own])
        pad_ref[:, 128 : 128 + length] = jnp.where(valid, vt, jnp.zeros_like(vt))
        parts = []
        for h in range(4):
            band = band_of(small_ref, 4 * g + h, ROWS_TAPS)
            parts.append(unblock(nt(blocks_of(pad_ref, h * LAND, 256), band), 256))
        att = (att + jnp.concatenate(parts, axis=0)).astype(BF)
        ctx_ref[:, own] = turn(att)


def call_attend_forward(x, w, small, ids):
    length, width = x.shape
    s = jax.ShapeDtypeStruct
    big = s((length, width), BF)
    tall = s((width, length), BF)
    low = s((LAND, width), BF)
    wide = s((LAND, width), F32)
    steps = s((ITERS, LAND, width), F32)
    vm = pl.BlockSpec(memory_space=pltpu.VMEM)
    tn = w.shape[0]
    cols = width // tn
    wspec = pl.BlockSpec((tn, width, 3 * cols), lambda i: (0, 0, 0))
    full = lambda a: pl.BlockSpec(a.shape, lambda i: (0,) * len(a.shape))
    outs = (big, big, big, tall, tall, big, low, low, low, wide, wide, s((ITERS + 1, LAND, width), F32), steps, steps, steps)
    return pl.pallas_call(
        attend_forward,
        grid=(1,),
        out_shape=outs,
        in_specs=[full(x), wspec, full(small), full(ids)],
        out_specs=tuple(full(o) for o in outs),
        scratch_shapes=[pltpu.VMEM((256, length + 256), BF)],
        compiler_params=pltpu.CompilerParams(vmem_limit_bytes=60 * 2**20),
        name="attend_forward",
    )(x, w, small, ids)


ROOT_HALF = 0.7071067811865476
P_ERF = 0.3275911
C_ERF = (0.254829592, -0.284496736, 1.421413741, -1.453152027, 1.061405429)


def gelu_both(u):
    x = jnp.abs(u) * ROOT_HALF
    e = jnp.exp(-0.5 * u * u)
    t = 1.0 / (1.0 + P_ERF * x)
    poly = C_ERF[4]
    for c in (C_ERF[3], C_ERF[2], C_ERF[1], C_ERF[0]):
        poly = poly * t + c
    tail = 0.5 * poly * t * e
    phi = jnp.where(u < 0.0, tail, 1.0 - tail)
    return u * phi, phi + u * e * 0.3989422804014327


def norm_parts(r):
    n = r.shape[1]
    center = r - jnp.sum(r, axis=1, keepdims=True) * (1.0 / n)
    spread_ = jnp.sum(center * center, axis=1, keepdims=True) * (1.0 / n)
    rstd = lax.rsqrt(spread_ + 1e-05)
    return center * rstd, rstd


def norm_back(e, normed, rstd):
    n = e.shape[1]
    mean_e = jnp.sum(e, axis=1, keepdims=True) * (1.0 / n)
    mean_en = jnp.sum(e * normed, axis=1, keepdims=True) * (1.0 / n)
    return rstd * (e - mean_e - normed * mean_en)


def fold(a):
    return jnp.sum(a.reshape(a.shape[0] // 8, 8, a.shape[1]), axis=0)


def feed(x_ref, cot_ref, ctx_ref, wo_ref, wi_ref, wf_ref, vec_in_ref, small_ref,
         out_ref, gr1_ref, dc_ref, dwo_ref, dwi_ref, dwf_ref, vec_ref, bsum_ref,
         act_ref, gi_ref, hid_ref, gr2_ref, hidf_ref, turn_ref, gp_ref):
    length, width = x_ref.shape
    tn = wo_ref.shape[0]
    cols = width // tn
    units = wi_ref.shape[2]
    size = 256
    chunk = 512
    bo, g1, s1, bf, g2, s2 = [vec_in_ref[k : k + 1, :].astype(F32) for k in range(6)]
    bi = [side_row(small_ref, t, ROWS_BI, 12) for t in range(tn)]
    vec_ref[...] = jnp.zeros_like(vec_ref)
    bsum_ref[...] = jnp.zeros_like(bsum_ref)

    def step(i, carry):
        at = pl.ds(pl.multiple_of(i * size, size), size)
        attn = bo + x_ref[at, :].astype(F32)
        for t in range(tn):
            attn = attn + nt(ctx_ref[at, t * cols : (t + 1) * cols], wo_ref[t])
        n1, rstd1 = norm_parts(attn)
        hidden = n1 * g1 + s1
        hid = hidden.astype(BF)
        hid_ref[at, :] = hid
        r2 = hidden + bf
        for t in range(tn):
            for c in range(0, units, chunk):
                own = slice(t * units + c, t * units + c + chunk)
                u = nn(hid, wi_ref[t, :, c : c + chunk]) + bi[t][:, c : c + chunk]
                act, gp = gelu_both(u)
                act_ref[at, own] = act.astype(BF)
                gp_ref[:, own] = gp
        for t in range(tn):
            r2 = r2 + nt(act_ref[at, t * units : (t + 1) * units], wf_ref[t])
        n2, rstd2 = norm_parts(r2)
        out_ref[at, :] = (n2 * g2 + s2).astype(BF)
        cot = cot_ref[at, :].astype(F32)
        gr2 = norm_back(cot * g2, n2, rstd2)
        vec_ref[5] += fold(cot)
        vec_ref[4] += fold(cot * n2)
        vec_ref[3] += fold(gr2)
        low = gr2.astype(BF)
        gr2_ref[at, :] = low
        for t in range(tn):
            for c in range(0, units, chunk):
                own = slice(t * units + c, t * units + c + chunk)
                gi = nn(low, wf_ref[t, :, c : c + chunk]) * gp_ref[:, own]
                bsum_ref[:, own] += fold(gi)
                gi_ref[at, own] = gi.astype(BF)
        gh = gr2
        for t in range(tn):
            gh = gh + nt(gi_ref[at, t * units : (t + 1) * units], wi_ref[t])
        gr1 = norm_back(gh * g1, n1, rstd1)
        vec_ref[2] += fold(gh)
        vec_ref[1] += fold(gh * n1)
        vec_ref[0] += fold(gr1)
        low1 = gr1.astype(BF)
        gr1_ref[at, :] = low1
        for t in range(tn):
            dc_ref[at, t * cols : (t + 1) * cols] = nn(low1, wo_ref[t]).astype(BF)
        return carry

    lax.fori_loop(0, length // size, step, 0)

    turn_ref[...] = turn(gr2_ref[...])
    for t in range(tn):
        for c in range(0, units, chunk):
            own = slice(t * units + c, t * units + c + chunk)
            dwf_ref[t, :, c : c + chunk] = nn(turn_ref[...], act_ref[:, own]).astype(BF)
    turn_ref[...] = turn(hid_ref[...])
    for t in range(tn):
        for c in range(0, units, chunk):
            own = slice(t * units + c, t * units + c + chunk)
            dwi_ref[t, :, c : c + chunk] = nn(turn_ref[...], gi_ref[:, own]).astype(BF)
    turn_ref[...] = turn(gr1_ref[...])
    for t in range(tn):
        dwo_ref[t] = nn(turn_ref[...], ctx_ref[:, t * cols : (t + 1) * cols]).astype(BF)


def call_feed(x, cot, ctx, w, vec_in, small):
    length, width = x.shape
    tn = w.shape[0]
    cols = width // tn
    units = (w.shape[2] - 4 * cols) // 2
    s = jax.ShapeDtypeStruct
    big = s((length, width), BF)
    full = lambda a: pl.BlockSpec(a.shape, lambda i: (0,) * len(a.shape))
    outs = (big, big, big, s((tn, width, cols), BF), s((tn, width, units), BF), s((tn, width, units), BF),
            s((6, 8, width), F32), s((8, tn * units), F32))
    return pl.pallas_call(
        feed,
        grid=(1,),
        out_shape=outs,
        in_specs=[full(x), full(cot), full(ctx),
                  pl.BlockSpec((tn, width, cols), lambda i: (0, 0, 3)),
                  pl.BlockSpec((tn, width, units), lambda i: (0, 0, 1)),
                  pl.BlockSpec((tn, width, units), lambda i: (0, 0, 2)),
                  full(vec_in), full(small)],
        out_specs=tuple(full(o) for o in outs),
        scratch_shapes=[pltpu.VMEM((length, tn * units), BF), pltpu.VMEM((length, tn * units), BF),
                        pltpu.VMEM((length, width), BF), pltpu.VMEM((length, width), BF),
                        pltpu.VMEM((8, 128), F32), pltpu.VMEM((width, length), BF),
                        pltpu.VMEM((256, tn * units), F32)],
        compiler_params=pltpu.CompilerParams(vmem_limit_bytes=62 * 2**20),
        name="feed_forward",
    )(x, cot, ctx, w, w, w, vec_in, small)


def attend_backward(x_ref, w_ref, ids_ref, small_ref, q_ref, k_ref, v_ref, near_ref, far_ref, lq_ref, lk_ref, mix_ref,
                    sum_ref, ker_ref, z_ref, a_ref, v2_ref, w2_ref, dc_ref, gr1_ref,
                    gtok_ref, dw_ref, vecq_ref, vecv_ref, gtap_ref,
                    pre_ref, glq_ref, glk_ref, gsum_ref, gz_ref, gk_ref, padv_ref, padc_ref, xt_ref):
    length, width = x_ref.shape
    tn = w_ref.shape[0]
    cols = width // tn
    scale = LAND ** -0.25
    pairs = width // 128
    groups = width // 256
    ids = ids_ref[pl.ds(own_sequence(), 1), :]
    member = jnp.where(lax.broadcasted_iota(jnp.int32, (LAND, length), 0) == ids, 1.0, 0.0).astype(F32)
    count = jnp.sum(member, axis=1, keepdims=True)
    member = member.astype(BF)
    valid = ids < LAND
    eye = pair_eye()

    for g in range(groups):
        own = slice(g * 256, (g + 1) * 256)
        gsum_ref[:, own] = gather_diag(nn(near_ref[own, :], dc_ref[:, own]))
    for p in range(pairs):
        own = slice(p * 128, (p + 1) * 128)
        gmix = gsum_ref[:, own]
        gz_ref[:, own] = pair_nt(gmix, sum_ref[:, own])
        gsum_ref[:, own] = pair_nn(pair_turn(z_ref[ITERS, :, own]), gmix)

    gk_ref[...] = jnp.zeros_like(gk_ref)

    def iterate(m, carry):
        n = ITERS - 1 - m
        for p in range(pairs):
            own = slice(p * 128, (p + 1) * 128)
            grad = 0.25 * gz_ref[:, own]
            kernel = ker_ref[:, own]
            z = z_ref[n, :, own]
            a = a_ref[n, :, own]
            v2 = v2_ref[n, :, own]
            w2 = w2_ref[n, :, own]
            dw2 = pair_nn(pair_turn(z), grad)
            at = pair_turn(a)
            dv2 = -pair_nn(at, dw2)
            da = -pair_nt(dw2, v2) - pair_nt(dv2, 7.0 * eye - a) + pair_nn(at, dv2)
            gk_ref[:, own] += pair_nt(da, z)
            gz_ref[:, own] = pair_nt(grad, w2) + pair_nn(pair_turn(kernel), da)
        return carry

    lax.fori_loop(0, ITERS, iterate, 0)

    for p in range(pairs):
        own = slice(p * 128, (p + 1) * 128)
        kernel = ker_ref[:, own]
        gz = gz_ref[:, own]
        total = jnp.sum(pair_sum(kernel * kernel), axis=0, keepdims=True)
        kt = pair_turn(kernel)
        back = jnp.sum(pair_sum(gz * kt), axis=0, keepdims=True)
        gk = gk_ref[:, own] + pair_turn(gz) / total - kernel * (2.0 * back / (total * total))
        mid = kernel * (gk - pair_sum(kernel * gk))
        glq_ref[:, own] = pair_nn(mid, lk_ref[:, own].astype(F32))
        glk_ref[:, own] = pair_nn(pair_turn(mid), lq_ref[:, own].astype(F32))

    flip = jnp.where(
        lax.broadcasted_iota(jnp.int32, (256, 256), 0) + lax.broadcasted_iota(jnp.int32, (256, 256), 1) == 255, 1.0, 0.0
    ).astype(BF)
    padv_ref[...] = jnp.zeros_like(padv_ref)
    padc_ref[...] = jnp.zeros_like(padc_ref)
    inner = slice(128, 128 + length)
    for g in range(groups):
        own = slice(g * 256, (g + 1) * 256)
        lk4 = spread(lk_ref[:, own])
        lq4 = spread(lq_ref[:, own])
        near = near_ref[own, :].astype(F32)
        gnear = nt(spread(mix_ref[:, own]), dc_ref[:, own])
        drop = jnp.sum((near * gnear).reshape(4, LAND, length), axis=1, keepdims=True)
        first = (near * (gnear.reshape(4, LAND, length) - drop).reshape(256, length)).astype(BF)
        glk_ref[:, own] += gather_diag(nn(first, q_ref[:, own]))
        gsum4 = spread(gsum_ref[:, own].astype(BF))
        far = far_ref[own, :].astype(F32)
        gfar = nt(gsum4, v_ref[:, own])
        drop = jnp.sum(far * gfar, axis=1, keepdims=True)
        third = (far * (gfar - drop)).astype(BF)
        glq_ref[:, own] += gather_diag(nn(third, k_ref[:, own]))
        glq = turn((glq_ref[:, own] / count).astype(BF))
        glk = turn((glk_ref[:, own] / count).astype(BF))
        dq = (nn(turn(lk4), first) + nn(glq, member)) * scale
        dk = (nn(turn(lq4), third) + nn(glk, member)) * scale
        dv = nn(turn(gsum4), far_ref[own, :])

        vt = turn(v_ref[:, own])
        padv_ref[:, inner] = jnp.where(valid, vt, jnp.zeros_like(vt))
        padc_ref[:, inner] = turn(dc_ref[:, own])
        parts = []
        for h in range(4):
            band = band_of(small_ref, 4 * g + h, ROWS_FLIP)
            parts.append(unblock(nt(blocks_of(padc_ref, h * LAND, 256), band), 256))
            plain = jnp.concatenate(
                [padc_ref[h * LAND : (h + 1) * LAND, 128 + at : 128 + at + 256] for at in range(0, length, 256)], axis=0
            )
            gram = nn(nt(flip, plain).astype(BF), blocks_of(padv_ref, h * LAND, 256))
            gram = pltpu.roll(gram, 0, 1, stride=1, stride_axis=0)
            gtap_ref[4 * g + h : 4 * g + h + 1, :] = jnp.sum(gram, axis=0, keepdims=True)
        dv = dv + jnp.where(valid, jnp.concatenate(parts, axis=0), 0.0)
        vecq_ref[own, :] = jnp.sum(dq, axis=1, keepdims=True)
        vecv_ref[own, :] = jnp.sum(dv, axis=1, keepdims=True)
        for lower in range(0, 256, 128):
            c = g * 256 + lower
            t, r = c // cols, c % cols
            pre_ref[t, r : r + 128, :] = dq[lower : lower + 128].astype(BF)
            pre_ref[t, cols + r : cols + r + 128, :] = dk[lower : lower + 128].astype(BF)
            pre_ref[t, 2 * cols + r : 2 * cols + r + 128, :] = dv[lower : lower + 128].astype(BF)

    xt_ref[...] = turn(x_ref[...])
    for t in range(tn):
        dw_ref[t] = nt(xt_ref[...], pre_ref[t]).astype(BF)
    for at in range(0, length, 256):
        part = nn(w_ref[0], pre_ref[0, :, at : at + 256])
        for t in range(1, tn):
            part = part + nn(w_ref[t], pre_ref[t, :, at : at + 256])
        gtok_ref[at : at + 256, :] = (gr1_ref[at : at + 256, :].astype(F32) + turn(part)).astype(BF)


def call_attend_backward(x, w, ids, small, saved, dc, gr1):
    (q, k, v, near, far, lq, lk, mix, summ, ker, z, a, v2, w2) = saved
    length, width = x.shape
    tn = w.shape[0]
    cols = width // tn
    s = jax.ShapeDtypeStruct
    full = lambda a: pl.BlockSpec(a.shape, lambda i: (0,) * len(a.shape))
    outs = (s((length, width), BF), s((tn, width, 3 * cols), BF), s((width, 1), F32), s((width, 1), F32),
            s((width // LAND, 512), F32))
    args = (x, w, ids, small, q, k, v, near, far, lq, lk, mix, summ, ker, z, a, v2, w2, dc, gr1)
    specs = [full(b) for b in args]
    specs[1] = pl.BlockSpec((tn, width, 3 * cols), lambda i: (0, 0, 0))
    small = pltpu.VMEM((LAND, width), F32)
    return pl.pallas_call(
        attend_backward,
        grid=(1,),
        out_shape=outs,
        in_specs=specs,
        out_specs=tuple(full(o) for o in outs),
        scratch_shapes=[pltpu.VMEM((tn, 3 * cols, length), BF), small, small, small, small, small,
                        pltpu.VMEM((256, length + 256), BF), pltpu.VMEM((256, length + 256), BF),
                        pltpu.VMEM((width, length), BF)],
        compiler_params=pltpu.CompilerParams(vmem_limit_bytes=60 * 2**20),
        name="attend_backward",
    )(*args)


FLIP_AT = 367
MESH = pl.DeviceIdType.MESH


class Place:
    def __init__(self, dp, tn):
        self.dp, self.tn = dp, tn
        self.nz = dp // 4
        i = lax.axis_index("dp")
        self.i = i
        self.t = lax.axis_index("tensor")
        self.c = lax.rem(i, 2)
        self.x = lax.rem(i // 2, 2)
        self.z = i // 4

    def at(self, z=None, x=None, c=None, t=None):
        z = self.z if z is None else z
        x = self.x if x is None else x
        c = self.c if c is None else c
        t = self.t if t is None else t
        return (z * 4 + x * 2 + c, t)


def greet(me):
    bar = pltpu.get_barrier_semaphore()
    for k in range(1, me.dp):
        pl.semaphore_signal(bar, 1, device_id=(lax.rem(me.i + k, me.dp), me.t), device_id_type=MESH)
    pl.semaphore_signal(bar, 1, device_id=(me.i, 1 - me.t), device_id_type=MESH)
    pl.semaphore_wait(bar, me.dp)


def remote(src, dst, ss, rs, to):
    return pltpu.make_async_remote_copy(
        src_ref=src, dst_ref=dst, send_sem=ss, recv_sem=rs, device_id=to, device_id_type=MESH
    )


class ToOwner:
    def __init__(self, me, src, out, ss, rs, local):
        self.copies = []
        for k in range(1, me.dp):
            j = lax.rem(me.i + k, me.dp)
            self.copies.append(remote(src.at[me.t * me.dp + j], out.at[me.i], ss.at[k], rs.at[k], (j, me.t)))
        self.own = pltpu.make_async_copy(src.at[me.t * me.dp + me.i], out.at[me.i], local)

    def start(self):
        for c in self.copies:
            c.start()
        self.own.start()

    def wait(self):
        for c in self.copies:
            c.wait()
        self.own.wait()


def gather_steps(me, src, out, ss, rs, local, cuts):
    t, z, x, c = me.t, me.z, me.x, me.c
    n = me.nz
    px, py, sib = me.at(x=1 - x), me.at(t=1 - t), me.at(c=1 - c)
    lanes = []
    for q, (lo, hi) in enumerate(cuts):
        w = pl.ds(lo, hi - lo)
        base = q * (n + 4)

        def move(ref, k, to):
            return remote(ref, ref, ss.at[base + k], rs.at[base + k], to)

        own = pltpu.make_async_copy(src.at[:, w], out.at[t, z, x, c, :, w], local.at[q])
        zs = []
        for k in range(1, n):
            to = me.at(z=lax.rem(z + k, n))
            zs.append(remote(src.at[:, w], out.at[t, z, x, c, :, w], ss.at[base + k], rs.at[base + k], to))
        if q % 2 == 0:
            first, second = move(out.at[t, :, x, c, :, w], n, px), move(out.at[t, :, :, c, :, w], n + 1, py)
            d2, d3 = move(out.at[t, :, :, c, :, w], n + 2, sib), move(out.at[1 - t, :, :, c, :, w], n + 3, sib)
        else:
            first, second = move(out.at[t, :, x, c, :, w], n, py), move(out.at[:, :, x, c, :, w], n + 1, px)
            d2, d3 = move(out.at[:, :, x, c, :, w], n + 2, sib), move(out.at[:, :, 1 - x, c, :, w], n + 3, sib)
        lanes.append([([], zs + [own]), (zs + [own], [first]), ([first], [second, d2]), ([second], [d3]), ([d2, d3], [])])
    depth = len(lanes[0])
    order = []
    for step in range(depth + len(lanes) // 2):
        for q in range(len(lanes)):
            if 0 <= step - q // 2 < depth:
                order.append(lanes[q][step - q // 2])
    return order


def run_stage(stage):
    for c in stage[0]:
        c.wait()
    for c in stage[1]:
        c.start()


def gather_sems(dp, chunks):
    n = (dp // 4 + 4) * chunks
    return [pltpu.SemaphoreType.DMA((n,)), pltpu.SemaphoreType.DMA((n,)), pltpu.SemaphoreType.DMA((chunks,))]


def even_cuts(width, n):
    return [(k * width // n, (k + 1) * width // n) for k in range(n)]


def owner_sems(dp):
    return [pltpu.SemaphoreType.DMA((dp,)), pltpu.SemaphoreType.DMA((dp,)), pltpu.SemaphoreType.DMA]


ANY = pl.BlockSpec(memory_space=pl.ANY)


def bring(dp, tn, order, chunks, *refs):
    n = len(order)
    ins, outs, sems = refs[:n], refs[n : 2 * n], refs[2 * n :]
    me = Place(dp, tn)
    greet(me)
    plans = []
    for k, kind in enumerate(order):
        s = sems[3 * k : 3 * k + 3]
        if kind == "pair":
            side = remote(ins[k], outs[k].at[me.t], s[0].at[0], s[1].at[0], (me.i, 1 - me.t))
            here = pltpu.make_async_copy(ins[k], outs[k].at[me.t], s[2])
            plans.append([([], [side, here]), ([side, here], [])])
        elif kind == "rows":
            plan = ToOwner(me, ins[k], outs[k], *s)
            plans.append([([], plan.copies + [plan.own]), (plan.copies + [plan.own], [])])
        else:
            w = ins[k].shape[1]
            plans.append(gather_steps(me, ins[k], outs[k], *s, even_cuts(w, chunks)))
    for p in plans:
        run_stage(p[0])
    for p, kind in zip(plans, order):
        if kind == "w":
            for st in p[1:]:
                run_stage(st)
    for p, kind in zip(plans, order):
        if kind != "w":
            for st in p[1:]:
                run_stage(st)


def call_bring(dp, tn, order, arrays, cid, chunks=4):
    outs, scratch = [], []
    for kind, a in zip(order, arrays):
        if kind == "pair":
            outs.append(jax.ShapeDtypeStruct((tn,) + a.shape, a.dtype))
            scratch += owner_sems(1)
        elif kind == "rows":
            outs.append(jax.ShapeDtypeStruct((dp,) + a.shape[1:], a.dtype))
            scratch += owner_sems(dp)
        else:
            outs.append(jax.ShapeDtypeStruct((tn, dp // 4, 2, 2) + a.shape, a.dtype))
            scratch += gather_sems(dp, chunks)
    return pl.pallas_call(
        functools.partial(bring, dp, tn, order, chunks),
        out_shape=tuple(outs),
        in_specs=[ANY] * len(arrays),
        out_specs=tuple([ANY] * len(outs)),
        scratch_shapes=scratch,
        compiler_params=pltpu.CompilerParams(collective_id=cid, has_side_effects=True),
        name="bring",
    )(*arrays)


def add_low(a, b):
    return (a.astype(F32) + b.astype(F32)).astype(BF)


def rows_home(me, src, out, ss, rs, local):
    mine = me.t * me.dp + me.i
    first, second = [], []
    for k in range(1, me.dp):
        j = lax.rem(me.i + k, me.dp)
        first.append(remote(src.at[j], out.at[mine], ss.at[k], rs.at[k], (j, me.t)))
    own = pltpu.make_async_copy(src.at[me.i], out.at[mine], local)
    partner = (me.i, 1 - me.t)
    n = me.dp
    second.append(remote(src.at[me.i], out.at[mine], ss.at[n], rs.at[n], partner))
    for k in range(1, me.dp):
        j = me.t * me.dp + lax.rem(me.i + me.dp - k, me.dp)
        second.append(remote(out.at[j], out.at[j], ss.at[n + k], rs.at[n + k], partner))
    return first, own, second


def reduce_lane(me, k, src, lo, w, bufs, ss, rs, puts):
    t, z, x, c = me.t, me.z, me.x, me.c
    n = me.nz
    base = k * (n + 2)
    rc, rx, ry, rz = bufs
    cols = pl.ds(0, w)
    own = pl.ds(lo, w)

    def move(a, b, q, to):
        return remote(a, b, ss.at[base + q], rs.at[base + q], to)

    core = move(src.at[:, :, :, 1 - c, :, own], rc.at[:, :, :, :, cols], 0, me.at(c=1 - c))
    east = move(rc.at[:, :, 1 - x, :, cols], rx.at[:, :, :, cols], 1, me.at(x=1 - x))
    north = move(rx.at[1 - t, :, :, cols], ry.at[:, :, cols], 2, me.at(t=1 - t))
    lines = []
    for q in range(1, n):
        to = lax.rem(z + q, n)
        lines.append(move(ry.at[to, :, cols], rz.at[q, :, cols], 2 + q, me.at(z=to)))

    def s0():
        core.start()

    def s1():
        core.wait()
        rc[:, :, :, :, :w] = add_low(rc[:, :, :, :, :w], src[:, :, :, c, :, own])
        east.start()

    def s2():
        east.wait()
        rx[:, :, :, :w] = add_low(rx[:, :, :, :w], rc[:, :, x, :, :w])
        north.start()

    def s3():
        north.wait()
        ry[:, :, :w] = add_low(ry[:, :, :w], rx[t, :, :, :w])
        for m in lines:
            m.start()

    def s4():
        total = ry[z, :, :w].astype(F32)
        for m in lines:
            m.wait()
        for q in range(1, n):
            total = total + rz[q, :, :w].astype(F32)
        for dst, at, first, width in puts:
            dst[:, at : at + width] = total[:, first : first + width]

    return [s0, s1, s2, s3, s4]


def carry_home(dp, tn, count, n_dst, chunks, *refs):
    n_in = 4 + count
    o_rows, g_rows = refs[:2]
    grads = refs[2 : 2 + count]
    norms, rest = refs[2 + count : n_in]
    o_home, g_home = refs[n_in : n_in + 2]
    douts = refs[n_in + 2 : n_in + 2 + n_dst]
    n_out, r_out = refs[n_in + 2 + n_dst : n_in + 4 + n_dst]
    sc = list(refs[n_in + 4 + n_dst :])
    me = Place(dp, tn)
    row_sems = [sc[0:3], sc[3:6]]
    v_ss, v_rs, nbuf, rbuf, nall, rall, nsum, rsum = sc[6:14]
    g_ss, g_rs = sc[14:16]
    bufs = [sc[16 + 4 * k : 20 + 4 * k] for k in range(len(chunks))]
    greet(me)
    plans = [rows_home(me, a, b, *s) for a, b, s in ((o_rows, o_home, row_sems[0]), (g_rows, g_home, row_sems[1]))]
    partner = (me.i, 1 - me.t)
    v1 = [remote(norms, nbuf, v_ss.at[0], v_rs.at[0], partner),
          remote(rest.at[1 - me.t], rbuf, v_ss.at[1], v_rs.at[1], partner)]
    lanes = [reduce_lane(me, k, grads[g], lo, w, bufs[k], g_ss, g_rs, [(douts[d],) + tuple(r) for d, *r in puts])
             for k, (g, lo, w, puts) in enumerate(chunks)]
    for lane in lanes:
        lane[0]()
    for c in v1:
        c.start()
    for first, own, second in plans:
        for c in first:
            c.start()
        own.start()
        second[0].start()
    for c in v1:
        c.wait()
    nsum[...] = norms[...] + nbuf[...]
    rsum[...] = rest[me.t] + rbuf[...]
    v2 = []
    for k in range(1, dp):
        j = lax.rem(me.i + k, dp)
        v2.append(remote(nsum.at[j], nall.at[k], v_ss.at[2 * k], v_rs.at[2 * k], (j, me.t)))
        v2.append(remote(rsum, rall.at[k], v_ss.at[2 * k + 1], v_rs.at[2 * k + 1], (j, me.t)))
    for c in v2:
        c.start()
    for s in (1, 2):
        for lane in lanes:
            lane[s]()
    for first, own, second in plans:
        for a, b in zip(first, second[1:]):
            a.wait()
            b.start()
    for s in (3, 4):
        for lane in lanes:
            lane[s]()
    for c in v2:
        c.wait()
    ntot = nsum[me.i]
    rtot = rsum[...]
    for k in range(1, dp):
        ntot = ntot + nall[k]
        rtot = rtot + rall[k]
    n_out[...] = ntot
    r_out[...] = rtot
    for first, own, second in plans:
        own.wait()
        for c in second:
            c.wait()


def call_carry_home(dp, tn, o_rows, g_rows, grads, chunks, widths, norms, rest, cid):
    s = jax.ShapeDtypeStruct
    count = len(grads)
    nz = dp // 4
    r, w = o_rows.shape[1:]
    depth = grads[0].shape[4]
    home = s((tn * dp, r, w), BF)
    douts = [s((depth, w2), F32) for w2 in widths]
    outs = [home, home] + douts + [s(norms.shape[1:], F32), s(rest.shape[1:], F32)]
    dma = pltpu.SemaphoreType.DMA
    scratch = [dma((2 * dp,)), dma((2 * dp,)), dma, dma((2 * dp,)), dma((2 * dp,)), dma,
               dma((2 * dp,)), dma((2 * dp,)),
               pltpu.VMEM(norms.shape, F32), pltpu.VMEM(rest.shape[1:], F32),
               pltpu.VMEM((dp,) + norms.shape[1:], F32), pltpu.VMEM((dp,) + rest.shape[1:], F32),
               pltpu.VMEM(norms.shape, F32), pltpu.VMEM(rest.shape[1:], F32),
               dma(((nz + 2) * len(chunks),)), dma(((nz + 2) * len(chunks),))]
    for _, _, gw, _ in chunks:
        scratch += [pltpu.VMEM((tn, nz, 2, depth, gw), BF), pltpu.VMEM((tn, nz, depth, gw), BF),
                    pltpu.VMEM((nz, depth, gw), BF), pltpu.VMEM((nz, depth, gw), BF)]
    vm = pl.BlockSpec(memory_space=pltpu.VMEM)
    return pl.pallas_call(
        functools.partial(carry_home, dp, tn, count, len(widths), chunks),
        out_shape=tuple(outs),
        in_specs=[ANY, ANY] + [vm] * (count + 2),
        out_specs=tuple([ANY, ANY] + [vm] * (len(widths) + 2)),
        scratch_shapes=scratch,
        compiler_params=pltpu.CompilerParams(
            collective_id=cid, has_side_effects=True, vmem_limit_bytes=60 * 2**20
        ),
        name="carry_home",
    )(o_rows, g_rows, *grads, norms, rest)


def local(tokens, cotangent, landmark_ids, w_query, w_key, w_value, b_query, b_value, conv_taps, w_out, b_out,
          first_gain, first_shift, w_inner, b_inner, w_outer, b_outer, second_gain, second_shift):
    dp = lax.axis_size("dp")
    tn = lax.axis_size("tensor")
    here = lax.axis_index("dp")
    tens = lax.axis_index("tensor")
    part, width = tokens.shape[1:]
    length = dp * part
    cols = w_query.shape[1]
    units = w_inner.shape[1]
    heads, taps = conv_taps.shape
    packed = jnp.concatenate([w_query, w_key, w_value, w_out, w_inner, w_outer], axis=1)
    tap_rows = jnp.pad(conv_taps.astype(F32), ((0, 0), (0, 128 - taps)))
    flip_rows = jnp.pad(conv_taps[:, ::-1].astype(F32), ((0, 0), (0, 128 - taps)))
    flat = jnp.concatenate([b_query, b_value, b_inner]).astype(F32).reshape(-1, 128)
    small = jnp.concatenate([flat, tap_rows, flip_rows, jnp.zeros((2, 128), F32)], axis=0)
    vec_in = jnp.stack([b_out, first_gain, first_shift, b_outer, second_gain, second_shift])

    rows, cot, whole, small = call_bring(
        dp, tn, ("rows", "rows", "w", "pair"), (tokens, cotangent, packed, small), 0, 6
    )
    rows = rows.reshape(length, width)
    cot = cot.reshape(length, width)
    whole = whole.reshape(tn, width, packed.shape[1])
    q, k, v, near, far, ctx, *rest_saved = call_attend_forward(rows, whole, small, landmark_ids)
    out_rows, gr1, dc, dwo, dwi, dwf, vec, bsum = call_feed(rows, cot, ctx, whole, vec_in, small)
    grad_rows, dwqkv, gbq, gbv, gtap = call_attend_backward(
        rows, whole, landmark_ids, small, (q, k, v, near, far, *rest_saved), dc, gr1
    )
    share = width // dp
    norms = jnp.sum(vec, axis=1).reshape(6, dp, share).transpose(1, 0, 2).reshape(dp, 6 * share)
    norms = jnp.pad(norms, ((0, 0), (0, 1024 - 6 * share))).reshape(dp, 8, 128)
    rest = jnp.concatenate(
        [gbq.reshape(tn, cols), gbv.reshape(tn, cols), jnp.sum(bsum, axis=0).reshape(tn, units),
         gtap[:, FLIP_AT : FLIP_AT + taps].reshape(tn, heads * taps)], axis=1)
    rest = jnp.pad(rest, ((0, 0), (0, 24 * 128 - rest.shape[1]))).reshape(tn, 24, 128)

    def cut(g):
        return g.reshape(tn, dp // 4, 2, 2, width // dp, g.shape[2])

    half = units // 2
    chunks = (
        (2, 0, half, ((5, 0, 0, half),)), (2, half, half, ((5, half, 0, half),)),
        (1, 0, half, ((4, 0, 0, half),)), (1, half, half, ((4, half, 0, half),)),
        (0, 0, cols, ((3, 0, 0, cols),)),
        (3, 0, 3 * cols, ((0, 0, 0, cols), (1, 0, cols, cols), (2, 0, 2 * cols, cols))),
    )
    out_home, grad_home, gq, gk, gv, go, gi, gf, nsum, rsum = call_carry_home(
        dp, tn, out_rows.reshape(dp, part, width), grad_rows.reshape(dp, part, width),
        [cut(dwo), cut(dwi), cut(dwf), cut(dwqkv)], chunks, (cols, cols, cols, cols, units, units), norms, rest, 1
    )
    n = nsum.reshape(-1)[: 6 * share].reshape(6, share)
    r = rsum.reshape(-1)
    at = 2 * cols + units
    return (out_home, grad_home, gq, gk, gv, r[:cols], r[cols : 2 * cols],
            r[at : at + heads * taps].reshape(heads, taps), go, n[0], n[1], n[2], gi, r[2 * cols : at], gf,
            n[3], n[4], n[5])


def solution(mesh):
    return jax.shard_map(
        local,
        mesh=mesh,
        in_specs=(
            P(None, "dp", None),
            P(None, "dp", None),
            P(),
            P("dp", "tensor"),
            P("dp", "tensor"),
            P("dp", "tensor"),
            P("tensor"),
            P("tensor"),
            P("tensor", None),
            P("dp", "tensor"),
            P(),
            P(),
            P(),
            P("dp", "tensor"),
            P("tensor"),
            P("dp", "tensor"),
            P(),
            P(),
            P(),
        ),
        out_specs=(
            P(None, "dp", None),
            P(None, "dp", None),
            P("dp", "tensor"),
            P("dp", "tensor"),
            P("dp", "tensor"),
            P("tensor"),
            P("tensor"),
            P("tensor", None),
            P("dp", "tensor"),
            P("dp"),
            P("dp"),
            P("dp"),
            P("dp", "tensor"),
            P("tensor"),
            P("dp", "tensor"),
            P("dp"),
            P("dp"),
            P("dp"),
        ),
        check_vma=False,
    )
```

time: 838 us -> 534 us (0.64)
  Pallas kernels: 0 us -> 492 us
  matrix products: 253 us -> 0 us
  waiting for transfers between devices: 232 us -> 0 us
  other arithmetic: 155 us -> 4.5 us
  local copies, waits for them, and re-layouts: 97 us -> 28.8 us
  blocking collectives: 53.6 us -> 0 us
  starting transfers between devices: 24.9 us -> 0 us
  between operations: 17.9 us -> 1.27 us
    pallas_call x0 -> x5, Pallas kernels: none -> 492 us  [the longest x1 201 us: call_carry_home(): pl.pallas_call(functools.partial(carry_home, dp, tn, count, len(widths),...]
    dot_general x108 -> x0, matrix products: 247 us -> none  [the longest x27 142 us: partial_product(): return jnp.einsum(spec, left, right, preferred_element_type=jnp.float32)]
    reduce_scatter x1 -> x0, waiting for transfers between devices: 121 us -> none  [local(): lax.psum_scatter(jnp.concatenate(parts, axis=0).astype(jnp.bfloat16), ('t...]
    all_gather x3 -> x0, waiting for transfers between devices: 99.5 us -> none  [the longest x1 99.5 us: local(): whole = lax.all_gather(packed, ('tensor', 'dp'), axis=0, tiled=True)]
    reduce_sum x13 -> x2, other arithmetic: 65.2 us -> 0.07 us  [the longest x1 0.04 us: local(): jnp.sum(vec, axis=1).reshape(6, dp, share).transpose(1, 0, 2)]
    psum x1 -> x0, blocking collectives: 45.3 us -> none  [local(): vec = lax.psum(vec, ('tensor', 'dp'))]
    add_any x2 -> x0, other arithmetic: 33.5 us -> none  [the longest x1 33.5 us: depthwise(): padded[offset:offset + length]]
    mul x4 -> x0, other arithmetic: 32.5 us -> none  [the longest x2 32.5 us: depthwise(): taps[:, offset][None, :, None] * padded[offset:offset + length]]
  transfers between devices with their start and end apart: 8 -> 0, of which waited for: 3 -> 0; matrix products, arithmetic and copies ran while one was open for 32% -> 0% of each run, Pallas kernels for 0% -> 0%
where the time goes in v2:
time: 534 us; the launch traced here: 527 us
  Pallas kernels  492 us (92%)
  local copies, waits for them, and re-layouts  28.8 us (5%)
    pallas_call x1, Pallas kernels, call_carry_home(): pl.pallas_call(functools.partial(carry_home, dp, tn, count, len(widths),...  201 us
    pallas_call x1, Pallas kernels, call_bring(): pl.pallas_call(functools.partial(bring, dp, tn, order, chunks), out_shape...  152 us
    pallas_call x1, Pallas kernels, call_feed(): pl.pallas_call(feed, grid=(1,), out_shape=outs, in_specs=[full(x), full(c...  58.3 us
    pallas_call x1, Pallas kernels, call_attend_backward(): pl.pallas_call(attend_backward, grid=(1,), out_shape=outs, in_specs=specs...  47.4 us
    pallas_call x1, Pallas kernels, call_attend_forward(): pl.pallas_call(attend_forward, grid=(1,), out_shape=outs, in_specs=[full(...  33.3 us
    unnamed x36, local copies, waits for them, and re-layouts  15.7 us

profile of v2, /device:TPU:0, one launch (start us, length us, event | category | flops | bytes accessed | tf_op | source)
XLA Modules:
  0.0 526.8 jit_solution(13672642356109367476)
XLA Ops:
  0.7 0.1 pad.34.clone
  0.7 0.8 rev.3
  1.5 0.7 stack.21
  2.2 0.7 stack.22
  2.9 0.7 stack.23
  3.6 0.7 stack.24
  4.2 0.7 stack.25
  4.9 0.7 stack.26
  5.6 0.6 stack.27.vec_in_ref
  6.3 0.7 pad_convert_fusion
  6.9 0.7 fusion.1
  7.7 0.7 maximum_maximum_fusion.refs_3_
  8.3 0.8 constant_dynamic-update-slice_fusion.5
  9.1 0.8 constant_dynamic-update-slice_fusion.4
  9.9 0.8 constant_dynamic-update-slice_fusion.3
  10.7 0.8 constant_dynamic-update-slice_fusion.2
  11.4 0.9 constant_dynamic-update-slice_fusion.1
  12.4 0.9 constant_dynamic-update-slice_fusion.refs_2_
  13.3 0.0 copy-start.1
  13.3 0.8 copy-done.1
  14.1 151.9 %bring.1 = (bf16[16,64,768]{2,1,0:T(8,128)(2,1)}, bf16[16,64,768]{2,1,0:T(8,128)(2,1)}, bf16[2,4,2,2,48,4608]{5,4,3,2,1,0:T(8,128)(2,1)}, f32[2,32,128]{2,1,0:T(8,128)}) custom-call(bf16[32,64,768]{2,1,0:T(8,128)(2,1)} %refs_0_.1, bf16[32,64,768]{2,1,0:T(8,128)(2,1)} %refs_1_.1, bf16[48,4608]{1,0:T(8,128)(2,1)} %copy-done.1, ...), custom_call_target="tpu_custom_call" | custom-call | tf_op jit(solution)/shard_map/bring/pallas_call | solution.py:691
  166.0 33.3 %attend_forward.1 = (bf16[1024,768]{1,0:T(8,128)(2,1)}, bf16[1024,768]{1,0:T(8,128)(2,1)}, bf16[1024,768]{1,0:T(8,128)(2,1)}, bf16[768,1024]{1,0:T(8,128)(2,1)},...) custom-call(bf16[1024,768]{1,0:T(8,128)(2,1)} %bitcast.36, ...), custom_call_target="tpu_custom_call" | custom-call | tf_op jit(solution)/shard_map/attend_forward/pallas_call | solution.py:235
  199.2 58.3 %feed_forward.1 = (bf16[1024,768]{1,0:T(8,128)(2,1)}, bf16[1024,768]{1,0:T(8,128)(2,1)}, bf16[1024,768]{1,0:T(8,128)(2,1)}, bf16[2,768,384]{2,1,0:T(8,128)(2,1)}...) custom-call(bf16[1024,768]{1,0:T(8,128)(2,1)} %bitcast.37, ...), custom_call_target="tpu_custom_call" | custom-call | tf_op jit(solution)/shard_map/feed_forward/pallas_call | solution.py:371
  257.6 0.0 copy-start.4
  257.6 47.4 %attend_backward.1 = (bf16[1024,768]{1,0:T(8,128)(2,1)}, bf16[2,768,1152]{2,1,0:T(8,128)(2,1)}, f32[768,1]{1,0:T(8,128)}, f32[768,1]{1,0:T(8,128)}, f32[12,512]{1,0:T(8,128)}) custom-call(bf16[1024,768]{1,0:T(8,128)(2,1)} %bitcast.38, bf16[2,768,4608]{2,1,0:T(8,128)(2,1)} %bitcast.35, s32[32,1024]{1,0:T(8,128)} %ids_ref.3, ...), custom_call_target="tpu_custom_call" | custom-call | tf_op jit(solution)/shard_map/attend_backward/pallas_call | solution.py:523
  304.9 1.2 reduce
  306.1 1.2 reduce.1
  307.3 0.8 slice.55
  308.1 0.1 reshape.131
  308.2 0.0 copy-done.4
  308.3 0.6 copy.41
  308.9 0.1 reshape.125
  309.0 0.1 reshape.126
  309.1 0.6 copy.38
  309.8 201.3 %carry_home.1 = (bf16[32,64,768]{2,1,0:T(8,128)(2,1)}, bf16[32,64,768]{2,1,0:T(8,128)(2,1)}, f32[48,384]{1,0:T(8,128)}, f32[48,384]{1,0:T(8,128)}, f32[48,384]{1...) custom-call(bf16[16,64,768]{2,1,0:T(8,128)(2,1)} %bitcast.43, ...), custom_call_target="tpu_custom_call" | custom-call | tf_op jit(solution)/shard_map/carry_home/pallas_call | solution.py:858
  511.1 0.7 slice.69
  511.8 0.7 reshape.134
  512.5 1.5 fusion.2
  514.0 1.3 slice_bitcast_fusion.1
  515.3 1.3 slice_bitcast_fusion
  516.6 4.0 copy.55
  520.7 1.7 copy.56
  522.4 0.6 copy.57
  523.0 0.6 copy.58
  523.6 0.6 copy.59
  524.3 0.6 copy.60
  524.9 0.7 copy.61
  525.6 0.7 copy.62
  (25 shorter events, 0.2 us)
Async XLA Ops:
  13.3 0.8 copy-start.1
  257.6 50.6 %copy-start.5 = (f32[8,3072]{1,0:T(8,128)S(1)}, f32[8,3072]{1,0:T(8,128)}, u32[]{:S(2)}) copy-start(f32[8,3072]{1,0:T(8,128)} %get-tuple-element.90) | copy-start | bytes 294916
  257.6 50.7 %copy-start.4 = (f32[6,8,768]{2,1,0:T(8,128)S(1)}, f32[6,8,768]{2,1,0:T(8,128)}, u32[]{:S(2)}) copy-start(f32[6,8,768]{2,1,0:T(8,128)} %get-tuple-element.87) | copy-start | bytes 442372
  516.6 4.0 copy-start
  520.7 1.7 copy-start.9
  520.7 2.3 copy-start.8
  520.7 3.0 copy-start.7
  520.7 3.6 copy-start.6
  520.7 4.2 copy-start.3
  520.7 4.9 copy-start.2

commit v3 on v2

v3 whole, which is shorter than its diff:
```python
import functools

import jax
import jax.numpy as jnp
from jax import lax
from jax.experimental import pallas as pl
from jax.experimental.pallas import tpu as pltpu
from jax.sharding import PartitionSpec as P

F32 = jnp.float32
BF = jnp.bfloat16
MESH = pl.DeviceIdType.MESH
ANY = pl.BlockSpec(memory_space=pl.ANY)
VM = pl.BlockSpec(memory_space=pltpu.VMEM)
DMA = pltpu.SemaphoreType.DMA
SMALL_ROWS = 32


class Place:
    def __init__(self, dp, tn):
        self.dp, self.tn = dp, tn
        self.nz = dp // 4
        i = lax.axis_index("dp")
        self.i = i
        self.t = lax.axis_index("tensor")
        self.c = lax.rem(i, 2)
        self.x = lax.rem(i // 2, 2)
        self.z = i // 4

    def at(self, z=None, x=None, c=None, t=None):
        z = self.z if z is None else z
        x = self.x if x is None else x
        c = self.c if c is None else c
        t = self.t if t is None else t
        return (z * 4 + x * 2 + c, t)


def greet(me, rows=True):
    bar = pltpu.get_barrier_semaphore()
    if rows:
        peers = [(lax.rem(me.i + k, me.dp), me.t) for k in range(1, me.dp)]
    else:
        peers = [me.at(z=lax.rem(me.z + k, me.nz)) for k in range(1, me.nz)] + [me.at(x=1 - me.x), me.at(c=1 - me.c)]
    peers.append((me.i, 1 - me.t))
    for p in peers:
        pl.semaphore_signal(bar, 1, device_id=p, device_id_type=MESH)
    pl.semaphore_wait(bar, len(peers))


def remote(src, dst, ss, rs, to):
    return pltpu.make_async_remote_copy(
        src_ref=src, dst_ref=dst, send_sem=ss, recv_sem=rs, device_id=to, device_id_type=MESH
    )


def start_all(copies):
    for c in copies:
        c.start()


def wait_all(copies):
    for c in copies:
        c.wait()


def to_owner(me, src, out, ss, rs, local):
    copies = []
    for k in range(1, me.dp):
        j = lax.rem(me.i + k, me.dp)
        copies.append(remote(src.at[me.t * me.dp + j], out.at[me.i], ss.at[k], rs.at[k], (j, me.t)))
    copies.append(pltpu.make_async_copy(src.at[me.t * me.dp + me.i], out.at[me.i], local))
    return copies


def to_home(me, src, out, ss, rs, local):
    copies = []
    for k in range(1, me.dp):
        j = lax.rem(me.i + k, me.dp)
        copies.append(remote(src.at[j], out.at[me.i], ss.at[k], rs.at[k], (j, me.t)))
    copies.append(pltpu.make_async_copy(src.at[me.i], out.at[me.i], local))
    return copies


def gather_lane(me, src, own, out, cols, north_first, ss, rs, local):
    t, z, x, c, n = me.t, me.z, me.x, me.c, me.nz
    px, py, sib = me.at(x=1 - x), me.at(t=1 - t), me.at(c=1 - c)

    def move(ref, k, to):
        return remote(ref, ref, ss.at[k], rs.at[k], to)

    zs = [pltpu.make_async_copy(src.at[:, own], out.at[t, z, x, c, :, cols], local)]
    for k in range(1, n):
        to = me.at(z=lax.rem(z + k, n))
        zs.append(remote(src.at[:, own], out.at[t, z, x, c, :, cols], ss.at[k], rs.at[k], to))
    if north_first:
        first, second = move(out.at[t, :, x, c, :, cols], n, py), move(out.at[:, :, x, c, :, cols], n + 1, px)
        d2, d3 = move(out.at[:, :, x, c, :, cols], n + 2, sib), move(out.at[:, :, 1 - x, c, :, cols], n + 3, sib)
    else:
        first, second = move(out.at[t, :, x, c, :, cols], n, px), move(out.at[t, :, :, c, :, cols], n + 1, py)
        d2, d3 = move(out.at[t, :, :, c, :, cols], n + 2, sib), move(out.at[1 - t, :, :, c, :, cols], n + 3, sib)

    def s0():
        start_all(zs)

    def s1():
        wait_all(zs)
        first.start()

    def s2():
        first.wait()
        second.start()
        d2.start()

    def s3():
        second.wait()
        d3.start()

    def s4():
        d2.wait()
        d3.wait()

    return [s0, s1, s2, s3, s4]


def gather_count(dp):
    return dp // 4 + 4


def add_low(a, b):
    return (a.astype(F32) + b.astype(F32)).astype(BF)


def reduce_lane(me, src, lo, w, bufs, ss, rs, local, puts):
    t, z, x, c, n = me.t, me.z, me.x, me.c, me.nz
    mine, rc, rx, ry, rz = bufs
    cols = pl.ds(lo, w)

    def move(a, b, q, to):
        return remote(a, b, ss.at[q], rs.at[q], to)

    keep = pltpu.make_async_copy(src.at[:, :, :, c, :, cols], mine, local)
    core = move(src.at[:, :, :, 1 - c, :, cols], rc, 0, me.at(c=1 - c))
    east = move(rc.at[:, :, 1 - x], rx, 1, me.at(x=1 - x))
    north = move(rx.at[1 - t], ry, 2, me.at(t=1 - t))
    lines = []
    for q in range(1, n):
        to = lax.rem(z + q, n)
        lines.append(move(ry.at[to], rz.at[q], 2 + q, me.at(z=to)))

    def s0():
        keep.start()
        core.start()

    def s1():
        keep.wait()
        core.wait()
        rc[...] = add_low(rc[...], mine[...])
        east.start()

    def s2():
        east.wait()
        rx[...] = add_low(rx[...], rc[:, :, x])
        north.start()

    def s3():
        north.wait()
        ry[...] = add_low(ry[...], rx[t])
        start_all(lines)

    def s4():
        total = ry[z].astype(F32)
        wait_all(lines)
        for q in range(1, n):
            total = total + rz[q].astype(F32)
        for dst, at, first, width in puts:
            dst[:, at : at + width] = total[:, first : first + width]

    return [s0, s1, s2, s3, s4]


def reduce_bufs(dp, tn, depth, w):
    nz = dp // 4
    return [pltpu.VMEM((tn, nz, 2, depth, w), BF), pltpu.VMEM((tn, nz, 2, depth, w), BF),
            pltpu.VMEM((tn, nz, depth, w), BF), pltpu.VMEM((nz, depth, w), BF), pltpu.VMEM((nz, depth, w), BF)]


def reduce_count(dp):
    return dp // 4 + 2


class Sub:
    def __init__(self, ref, base):
        self.ref, self.base = ref, base

    @property
    def at(self):
        return self

    def __getitem__(self, k):
        return self.ref.at[self.base + k]


class Ticks:
    def __init__(self, stages):
        self.stages = list(stages)

    def __call__(self, count=1):
        for _ in range(min(count, len(self.stages))):
            self.stages.pop(0)()

    def rest(self):
        self(len(self.stages))


def sems(n):
    return [DMA((n,)), DMA((n,))]


def params(cid, mib):
    return pltpu.CompilerParams(collective_id=cid, has_side_effects=True, vmem_limit_bytes=mib * 2**20)


def bring(dp, tn, tok, wq, wk, wv, wo, bq, bv, bi, taps, rows, wqkv, wout, small,
          r_ss, r_rs, g_ss, g_rs, local, piece):
    me = Place(dp, tn)
    cols = wq.shape[1]
    n = gather_count(dp)
    lanes = []
    for k, (src, dst, lo) in enumerate(((wq, wqkv, 0), (wk, wqkv, cols), (wv, wqkv, 2 * cols), (wo, wout, 0))):
        lanes.append(gather_lane(me, src, pl.ds(0, cols), dst, pl.ds(lo, cols), k % 2 == 1,
                                 Sub(g_ss, k * n), Sub(g_rs, k * n), local.at[k]))
    piece[...] = jnp.zeros_like(piece)
    for ref, first in ((bq, ROWS_BQ), (bv, ROWS_BV), (bi, ROWS_BI)):
        for r in range(ref.shape[1] // 128):
            piece[first + r : first + r + 1, :] = ref[:, r * 128 : (r + 1) * 128].astype(F32)
    heads, width = taps.shape
    tap = taps[...].astype(F32)
    piece[ROWS_TAPS : ROWS_TAPS + heads, :width] = tap
    greet(me)
    for s in (0, 1):
        for lane in lanes[2 * s : 2 * s + 2]:
            lane[0]()
    moved = to_owner(me, tok, rows, r_ss, r_rs, local.at[4])
    start_all(moved)
    side = [remote(piece, small.at[me.t], r_ss.at[0], r_rs.at[0], (me.i, 1 - me.t)),
            pltpu.make_async_copy(piece, small.at[me.t], local.at[5])]
    start_all(side)
    for pair, stage in ((0, 1), (0, 2), (1, 1), (0, 3), (1, 2), (1, 3), (0, 4), (1, 4)):
        for lane in lanes[2 * pair : 2 * pair + 2]:
            lane[stage]()
    wait_all(side)
    wait_all(moved)


def call_bring(dp, tn, tok, wq, wk, wv, wo, bq, bv, bi, taps):
    s = jax.ShapeDtypeStruct
    depth, cols = wq.shape
    lead = (tn, dp // 4, 2, 2, depth)
    outs = (s((dp,) + tok.shape[1:], BF), s(lead + (3 * cols,), BF), s(lead + (cols,), BF), s((tn, SMALL_ROWS, 128), F32))
    return pl.pallas_call(
        functools.partial(bring, dp, tn),
        out_shape=outs,
        in_specs=[ANY] * 5 + [VM] * 4,
        out_specs=(ANY, ANY, ANY, ANY),
        scratch_shapes=sems(dp) + sems(4 * gather_count(dp)) + [DMA((6,)), pltpu.VMEM((SMALL_ROWS, 128), F32)],
        compiler_params=params(0, 16),
        name="bring",
    )(tok, wq, wk, wv, wo, bq, bv, bi, taps)


def carry_home(dp, tn, g_rows, dwqkv, norms, rest, g_home, gq, gk, gv, n_out, r_out,
               r_ss, r_rs, v_ss, v_rs, g_ss, g_rs, local, nbuf, rbuf, nall, rall, nsum, rsum, *bufs):
    me = Place(dp, tn)
    cols = gq.shape[1]
    n = reduce_count(dp)
    lanes = []
    for k, dst in enumerate((gq, gk, gv)):
        lanes.append(reduce_lane(me, dwqkv, k * cols, cols, bufs[5 * k : 5 * k + 5], Sub(g_ss, k * n), Sub(g_rs, k * n),
                                 local.at[1 + k], [(dst, 0, 0, cols)]))
    greet(me)
    mine = me.t * dp
    first = []
    for k in range(1, dp):
        j = lax.rem(me.i + k, dp)
        first.append(remote(g_rows.at[j], g_home.at[mine + me.i], r_ss.at[k], r_rs.at[k], (j, me.t)))
    own = pltpu.make_async_copy(g_rows.at[me.i], g_home.at[mine + me.i], local.at[0])
    partner = (me.i, 1 - me.t)
    second = [remote(g_rows.at[me.i], g_home.at[mine + me.i], r_ss.at[dp], r_rs.at[dp], partner)]
    for k in range(1, dp):
        j = mine + lax.rem(me.i + dp - k, dp)
        second.append(remote(g_home.at[j], g_home.at[j], r_ss.at[dp + k], r_rs.at[dp + k], partner))
    v1 = [remote(norms, nbuf, v_ss.at[0], v_rs.at[0], partner),
          remote(rest.at[1 - me.t], rbuf, v_ss.at[1], v_rs.at[1], partner)]
    for lane in lanes:
        lane[0]()
    start_all(v1)
    start_all(first)
    own.start()
    second[0].start()
    for lane in lanes:
        lane[1]()
    wait_all(v1)
    nsum[...] = norms[...] + nbuf[...]
    rsum[...] = rest[me.t] + rbuf[...]
    v2 = []
    for k in range(1, dp):
        j = lax.rem(me.i + k, dp)
        v2.append(remote(nsum.at[j], nall.at[k], v_ss.at[2 * k], v_rs.at[2 * k], (j, me.t)))
        v2.append(remote(rsum, rall.at[k], v_ss.at[2 * k + 1], v_rs.at[2 * k + 1], (j, me.t)))
    start_all(v2)
    todo = list(zip(first, second[1:]))
    stages = [lane[s] for s in (2, 3) for lane in lanes]
    at = [2, 4, 6, 8, 10, 12]
    for k, (a, b) in enumerate(todo):
        while at and k == at[0]:
            at.pop(0)
            stages.pop(0)()
        a.wait()
        b.start()
    for st in stages:
        st()
    wait_all(v2)
    ntot = nsum[me.i]
    rtot = rsum[...]
    for k in range(1, dp):
        ntot = ntot + nall[k]
        rtot = rtot + rall[k]
    n_out[...] = ntot
    r_out[...] = rtot
    for lane in lanes:
        lane[4]()
    own.wait()
    wait_all(second)


def call_carry_home(dp, tn, g_rows, dwqkv, norms, rest):
    s = jax.ShapeDtypeStruct
    r, w = g_rows.shape[1:]
    depth, cols = dwqkv.shape[4], dwqkv.shape[5] // 3
    share = s((depth, cols), F32)
    outs = (s((tn * dp, r, w), BF), share, share, share, s(norms.shape[1:], F32), s(rest.shape[1:], F32))
    scratch = sems(2 * dp) + sems(2 * dp) + sems(3 * reduce_count(dp)) + [DMA((4,))]
    scratch += [pltpu.VMEM(norms.shape, F32), pltpu.VMEM(rest.shape[1:], F32),
                pltpu.VMEM((dp,) + norms.shape[1:], F32), pltpu.VMEM((dp,) + rest.shape[1:], F32),
                pltpu.VMEM(norms.shape, F32), pltpu.VMEM(rest.shape[1:], F32)]
    for _ in range(3):
        scratch += reduce_bufs(dp, tn, depth, cols)
    return pl.pallas_call(
        functools.partial(carry_home, dp, tn),
        out_shape=outs,
        in_specs=[ANY, ANY, VM, VM],
        out_specs=(ANY,) + (VM,) * 5,
        scratch_shapes=scratch,
        compiler_params=params(4, 48),
        name="carry_home",
    )(g_rows, dwqkv, norms, rest)


F32 = jnp.float32
BF = jnp.bfloat16
LAND = 64
ITERS = 6
HEADS_HERE = 6
ROWS_BQ, ROWS_BV, ROWS_BI, ROWS_TAPS = 0, 3, 6, 18
EDGE = 112
TAPS = 33
FLIP_AT = 367


def nn(a, b):
    return lax.dot_general(a, b, (((1,), (0,)), ((), ())), preferred_element_type=F32)


def nt(a, b):
    return lax.dot_general(a, b, (((1,), (1,)), ((), ())), preferred_element_type=F32)


def turn(a):
    return jnp.transpose(a, (1, 0))


def same_head(rows, columns):
    left = lax.broadcasted_iota(jnp.int32, (rows, columns), 0) // LAND
    right = lax.broadcasted_iota(jnp.int32, (rows, columns), 1) // LAND
    return left == right


def spread(small):
    n = small.shape[1] // LAND
    tall = jnp.concatenate([small] * n, axis=0)
    return jnp.where(same_head(n * LAND, n * LAND), tall, jnp.zeros_like(tall))


def gather_diag(full):
    n = full.shape[1] // LAND
    lane = lax.broadcasted_iota(jnp.int32, (LAND, full.shape[1]), 1) // LAND
    out = full[:LAND]
    for h in range(1, n):
        out = jnp.where(lane == h, full[h * LAND : (h + 1) * LAND], out)
    return out


def halves(a):
    high = a.astype(BF)
    return high, (a - high.astype(F32)).astype(BF)


def pair_nn(a, b):
    ah, al = halves(a)
    bh, bl = halves(b)
    bh, bl = spread(bh), spread(bl)
    wide = jnp.concatenate([bh, bl], axis=1)
    r = nn(jnp.concatenate([ah, al], axis=1), jnp.concatenate([wide, wide], axis=0))
    return r[:, : 2 * LAND] + r[:, 2 * LAND :]


def pair_nt(a, b):
    ah, al = halves(a)
    bh, bl = halves(b)
    bh, bl = spread(bh), spread(bl)
    tall = jnp.concatenate([bh, bl], axis=0)
    r = nt(jnp.concatenate([ah, al], axis=1), jnp.concatenate([tall, tall], axis=1))
    return r[:, : 2 * LAND] + r[:, 2 * LAND :]


def pair_turn(a):
    t = turn(a)
    return jnp.concatenate([t[:LAND], t[LAND:]], axis=1)


def pair_sum(a):
    left = lax.broadcasted_iota(jnp.int32, a.shape, 1) < LAND
    low = jnp.sum(jnp.where(left, a, 0.0), axis=1, keepdims=True)
    high = jnp.sum(jnp.where(left, 0.0, a), axis=1, keepdims=True)
    return jnp.where(left, low, high)


def pair_softmax(a):
    left = lax.broadcasted_iota(jnp.int32, a.shape, 1) < LAND
    low = jnp.max(jnp.where(left, a, -1e30), axis=1, keepdims=True)
    high = jnp.max(jnp.where(left, -1e30, a), axis=1, keepdims=True)
    e = jnp.exp(a - jnp.where(left, low, high))
    return e / pair_sum(e)


def pair_eye():
    r = lax.broadcasted_iota(jnp.int32, (LAND, 2 * LAND), 0)
    c = lax.broadcasted_iota(jnp.int32, (LAND, 2 * LAND), 1) % LAND
    return jnp.where(r == c, 1.0, 0.0).astype(F32)


def toeplitz(row, size, width):
    return pltpu.roll(jnp.broadcast_to(row, (size, width)), 0, 1, stride=1, stride_axis=0)


def blocks_of(ref, lower, block):
    length = ref.shape[1] - 256
    return jnp.concatenate(
        [ref[lower : lower + LAND, at : at + block + 256] for at in range(0, length, block)], axis=0
    )


def unblock(stacked, block):
    n = stacked.shape[0] // LAND
    return jnp.concatenate([stacked[i * LAND : (i + 1) * LAND] for i in range(n)], axis=1)


def own_sequence():
    return lax.axis_index("tensor") * lax.axis_size("dp") + lax.axis_index("dp")


def side_row(small_ref, t, first, count):
    return jnp.concatenate([small_ref[t, r : r + 1, :] for r in range(first, first + count)], axis=1)


def band_of(rows, head):
    h = head % HEADS_HERE
    row = jnp.concatenate([rows[head // HEADS_HERE][h : h + 1, :], jnp.zeros((1, 384), F32)], axis=1)
    return toeplitz(pltpu.roll(row, EDGE, 1), 256, 512).astype(BF)


def tap_rows(small_ref, t):
    return small_ref[t, ROWS_TAPS : ROWS_TAPS + 8, :]


def reversed_taps(rows):
    turned = jnp.where(
        lax.broadcasted_iota(jnp.int32, (128, 128), 0) + lax.broadcasted_iota(jnp.int32, (128, 128), 1) == TAPS - 1, 1.0, 0.0
    ).astype(BF)
    return nn(rows.astype(BF), turned)


def attend_forward(dp, x_ref, w_ref, small_ref, ids_ref, wi_ref, wf_ref,
                   q_ref, k_ref, v_ref, near_ref, far_ref, ctx_ref, lq_ref, lk_ref, mix_ref, sum_ref, ker_ref,
                   z_ref, a_ref, v2_ref, w2_ref, wi_all, wf_all, pad_ref, g_ss, g_rs, local):
    length, width = x_ref.shape
    tn = w_ref.shape[0]
    cols = width // tn
    scale = LAND ** -0.25
    rows_at = 256
    pairs = width // 128
    groups = width // 256
    me = Place(dp, tn)
    n = gather_count(dp)
    half = wi_ref.shape[1] // 2
    lanes = []
    for p, (src, dst) in enumerate(((wi_ref, wi_all), (wf_ref, wf_all))):
        for h in range(2):
            own, k = pl.ds(h * half, half), 2 * p + h
            lanes.append(gather_lane(me, src, own, dst, own, h == 1, Sub(g_ss, k * n), Sub(g_rs, k * n), local.at[k]))

    def stage(pair, s):
        def run():
            for lane in lanes[2 * pair : 2 * pair + 2]:
                lane[s]()
        return run

    greet(me, False)
    stage(0, 0)()
    stage(1, 0)()
    tick = Ticks([stage(0, 1), stage(0, 2), stage(1, 1), stage(0, 3), stage(1, 2), stage(1, 3), stage(0, 4), stage(1, 4)])
    bq = [side_row(small_ref, t, ROWS_BQ, 3) for t in range(tn)]
    bv = [side_row(small_ref, t, ROWS_BV, 3) for t in range(tn)]

    def project(i, carry):
        at = pl.ds(pl.multiple_of(i * rows_at, rows_at), rows_at)
        for t in range(tn):
            out = nn(x_ref[at, :], w_ref[t])
            own = slice(t * cols, (t + 1) * cols)
            q_ref[at, own] = ((out[:, :cols] + bq[t]) * scale).astype(BF)
            k_ref[at, own] = (out[:, cols : 2 * cols] * scale).astype(BF)
            v_ref[at, own] = (out[:, 2 * cols :] + bv[t]).astype(BF)
        return carry

    lax.fori_loop(0, length // rows_at, project, 0)

    ids = ids_ref[pl.ds(own_sequence(), 1), :]
    member = jnp.where(lax.broadcasted_iota(jnp.int32, (LAND, length), 0) == ids, 1.0, 0.0).astype(F32)
    count = jnp.sum(member, axis=1, keepdims=True)
    member = member.astype(BF)
    valid = ids < LAND
    lq_ref[...] = (nn(member, q_ref[...]) / count).astype(BF)
    lk_ref[...] = (nn(member, k_ref[...]) / count).astype(BF)

    eye = pair_eye()
    for p in range(pairs):
        own = slice(p * 128, (p + 1) * 128)
        scores = nt(lq_ref[:, own], spread(lk_ref[:, own]))
        kernel = pair_softmax(scores)
        ker_ref[:, own] = kernel
        left = lax.broadcasted_iota(jnp.int32, kernel.shape, 1) < LAND
        total = jnp.sum(pair_sum(kernel * kernel), axis=0, keepdims=True)
        z_ref[0, :, own] = pair_turn(kernel) / total

    for g in range(groups):
        own = slice(g * 256, (g + 1) * 256)
        scores = nt(spread(lk_ref[:, own]), q_ref[:, own]).reshape(4, LAND, length)
        scores = jnp.exp(scores - jnp.max(scores, axis=1, keepdims=True))
        scores = scores / jnp.sum(scores, axis=1, keepdims=True)
        near_ref[own, :] = scores.reshape(256, length).astype(BF)
        scores = nt(spread(lq_ref[:, own]), k_ref[:, own])
        scores = jnp.where(valid, scores, -1e30)
        scores = jnp.exp(scores - jnp.max(scores, axis=1, keepdims=True))
        scores = scores / jnp.sum(scores, axis=1, keepdims=True)
        far_ref[own, :] = scores.astype(BF)
        sum_ref[:, own] = gather_diag(nn(far_ref[own, :], v_ref[:, own]))
        if g == 1:
            tick()

    def iterate(n, carry):
        for p in range(pairs):
            own = slice(p * 128, (p + 1) * 128)
            z = z_ref[n, :, own]
            a = pair_nn(ker_ref[:, own], z)
            v2 = 15.0 * eye - pair_nn(a, 7.0 * eye - a)
            w2 = 13.0 * eye - pair_nn(a, v2)
            a_ref[n, :, own] = a
            v2_ref[n, :, own] = v2
            w2_ref[n, :, own] = w2
            z_ref[n + 1, :, own] = 0.25 * pair_nn(z, w2)
        return carry

    lax.fori_loop(0, ITERS // 2, iterate, 0)
    tick()
    lax.fori_loop(ITERS // 2, ITERS, iterate, 0)
    tick(2)

    for p in range(pairs):
        own = slice(p * 128, (p + 1) * 128)
        mix_ref[:, own] = pair_nn(z_ref[ITERS, :, own], sum_ref[:, own]).astype(BF)

    pad_ref[...] = jnp.zeros_like(pad_ref)
    taps = [tap_rows(small_ref, t) for t in range(tn)]
    for g in range(groups):
        own = slice(g * 256, (g + 1) * 256)
        att = nn(turn(spread(mix_ref[:, own])), near_ref[own, :])
        vt = turn(v_ref[:, own])
        pad_ref[:, 128 : 128 + length] = jnp.where(valid, vt, jnp.zeros_like(vt))
        parts = []
        for h in range(4):
            band = band_of(taps, 4 * g + h)
            parts.append(unblock(nt(blocks_of(pad_ref, h * LAND, 256), band), 256))
        att = (att + jnp.concatenate(parts, axis=0)).astype(BF)
        ctx_ref[:, own] = turn(att)
        if g == 0:
            tick()
    tick.rest()


def call_attend_forward(dp, x, w, small, ids, wi, wf):
    length, width = x.shape
    s = jax.ShapeDtypeStruct
    big = s((length, width), BF)
    tall = s((width, length), BF)
    low = s((LAND, width), BF)
    wide = s((LAND, width), F32)
    steps = s((ITERS, LAND, width), F32)
    tn = w.shape[0]
    depth, units = wi.shape
    whole = s((tn, dp // 4, 2, 2, depth, units), BF)
    outs = (big, big, big, tall, tall, big, low, low, low, wide, wide, s((ITERS + 1, LAND, width), F32), steps, steps, steps,
            whole, whole)
    return pl.pallas_call(
        functools.partial(attend_forward, dp),
        out_shape=outs,
        in_specs=[VM] * 4 + [ANY] * 2,
        out_specs=tuple([VM] * 15 + [ANY] * 2),
        scratch_shapes=[pltpu.VMEM((256, length + 256), BF)] + sems(4 * gather_count(dp)) + [DMA((4,))],
        compiler_params=params(1, 56),
        name="attend_forward",
    )(x, w, small, ids, wi, wf)


ROOT_HALF = 0.7071067811865476
P_ERF = 0.3275911
C_ERF = (0.254829592, -0.284496736, 1.421413741, -1.453152027, 1.061405429)


def gelu_both(u):
    x = jnp.abs(u) * ROOT_HALF
    e = jnp.exp(-0.5 * u * u)
    t = 1.0 / (1.0 + P_ERF * x)
    poly = C_ERF[4]
    for c in (C_ERF[3], C_ERF[2], C_ERF[1], C_ERF[0]):
        poly = poly * t + c
    tail = 0.5 * poly * t * e
    phi = jnp.where(u < 0.0, tail, 1.0 - tail)
    return u * phi, phi + u * e * 0.3989422804014327


def norm_parts(r):
    n = r.shape[1]
    center = r - jnp.sum(r, axis=1, keepdims=True) * (1.0 / n)
    spread_ = jnp.sum(center * center, axis=1, keepdims=True) * (1.0 / n)
    rstd = lax.rsqrt(spread_ + 1e-05)
    return center * rstd, rstd


def norm_back(e, normed, rstd):
    n = e.shape[1]
    mean_e = jnp.sum(e, axis=1, keepdims=True) * (1.0 / n)
    mean_en = jnp.sum(e * normed, axis=1, keepdims=True) * (1.0 / n)
    return rstd * (e - mean_e - normed * mean_en)


def fold(a):
    return jnp.sum(a.reshape(a.shape[0] // 8, 8, a.shape[1]), axis=0)


def feed(dp, x_ref, ctx_ref, wo_ref, wi_ref, wf_ref, bo_in, g1_in, s1_in, bf_in, g2_in, s2_in, small_ref, cot_ref,
         gr1_ref, dc_ref, dwo_ref, dwi_ref, dwf_ref, vec_ref, bsum_ref, half_ref,
         act_ref, gi_ref, hid_ref, gr2_ref, turn_ref, n1_ref, n2_ref, rs1_ref, rs2_ref, out_ref, cots_ref,
         c_ss, c_rs, h_ss, h_rs, local):
    length, width = x_ref.shape
    tn = wo_ref.shape[0]
    cols = width // tn
    units = wi_ref.shape[2]
    size = 256
    chunk = 512
    part = length // dp
    per = size // part
    me = Place(dp, tn)
    greet(me)
    arriving = to_owner(me, cot_ref, cots_ref, c_ss, c_rs, local.at[0])
    leaving = to_home(me, out_ref, half_ref, h_ss, h_rs, local.at[1])
    start_all(arriving)
    bo, g1, s1, bf, g2, s2 = [r[...].astype(F32) for r in (bo_in, g1_in, s1_in, bf_in, g2_in, s2_in)]
    bi = [side_row(small_ref, t, ROWS_BI, units // 128) for t in range(tn)]
    vec_ref[...] = jnp.zeros_like(vec_ref)
    bsum_ref[...] = jnp.zeros_like(bsum_ref)

    def rows_at(i):
        return pl.ds(pl.multiple_of(i * size, size), size)

    def forward(i, carry):
        at = rows_at(i)
        attn = bo + x_ref[at, :].astype(F32)
        for t in range(tn):
            attn = attn + nt(ctx_ref[at, t * cols : (t + 1) * cols], wo_ref[t])
        n1, rstd1 = norm_parts(attn)
        n1_ref[at, :] = n1
        rs1_ref[at, :] = rstd1
        hidden = n1 * g1 + s1
        hid = hidden.astype(BF)
        hid_ref[at, :] = hid
        r2 = hidden + bf
        for t in range(tn):
            for c in range(0, units, chunk):
                own = slice(t * units + c, t * units + c + chunk)
                act, gp = gelu_both(nn(hid, wi_ref[t, :, c : c + chunk]) + bi[t][:, c : c + chunk])
                act_ref[at, own] = act.astype(BF)
                gi_ref[at, own] = gp.astype(BF)
        for t in range(tn):
            r2 = r2 + nt(act_ref[at, t * units : (t + 1) * units], wf_ref[t])
        n2, rstd2 = norm_parts(r2)
        n2_ref[at, :] = n2
        rs2_ref[at, :] = rstd2
        out_ref[pl.ds(i * per, per)] = (n2 * g2 + s2).reshape(per, part, width).astype(BF)
        return carry

    def backward(i, carry):
        at = rows_at(i)
        cot = cots_ref[pl.ds(i * per, per)].astype(F32).reshape(size, width)
        n2 = n2_ref[at, :]
        gr2 = norm_back(cot * g2, n2, rs2_ref[at, :])
        vec_ref[5] += fold(cot)
        vec_ref[4] += fold(cot * n2)
        vec_ref[3] += fold(gr2)
        low = gr2.astype(BF)
        gr2_ref[at, :] = low
        for t in range(tn):
            for c in range(0, units, chunk):
                own = slice(t * units + c, t * units + c + chunk)
                gi = nn(low, wf_ref[t, :, c : c + chunk]) * gi_ref[at, own].astype(F32)
                bsum_ref[:, own] += fold(gi)
                gi_ref[at, own] = gi.astype(BF)
        gh = gr2
        for t in range(tn):
            gh = gh + nt(gi_ref[at, t * units : (t + 1) * units], wi_ref[t])
        n1 = n1_ref[at, :]
        gr1 = norm_back(gh * g1, n1, rs1_ref[at, :])
        vec_ref[2] += fold(gh)
        vec_ref[1] += fold(gh * n1)
        vec_ref[0] += fold(gr1)
        low1 = gr1.astype(BF)
        gr1_ref[at, :] = low1
        for t in range(tn):
            dc_ref[at, t * cols : (t + 1) * cols] = nn(low1, wo_ref[t]).astype(BF)
        return carry

    lax.fori_loop(0, length // size, forward, 0)
    start_all(leaving)
    wait_all(arriving)
    lax.fori_loop(0, length // size, backward, 0)

    turn_ref[...] = turn(gr2_ref[...])
    for t in range(tn):
        for c in range(0, units, chunk):
            own = slice(t * units + c, t * units + c + chunk)
            dwf_ref[t, :, c : c + chunk] = nn(turn_ref[...], act_ref[:, own]).astype(BF)
    turn_ref[...] = turn(hid_ref[...])
    for t in range(tn):
        for c in range(0, units, chunk):
            own = slice(t * units + c, t * units + c + chunk)
            dwi_ref[t, :, c : c + chunk] = nn(turn_ref[...], gi_ref[:, own]).astype(BF)
    turn_ref[...] = turn(gr1_ref[...])
    for t in range(tn):
        dwo_ref[t] = nn(turn_ref[...], ctx_ref[:, t * cols : (t + 1) * cols]).astype(BF)
    wait_all(leaving)


def call_feed(dp, x, ctx, wo, wi, wf, vectors, small, cot):
    length, width = x.shape
    tn, _, cols = wo.shape
    units = wi.shape[2]
    s = jax.ShapeDtypeStruct
    big = s((length, width), BF)
    blocks = (dp,) + cot.shape[1:]
    outs = (big, big, s((tn, width, cols), BF), s((tn, width, units), BF), s((tn, width, units), BF),
            s((6, 8, width), F32), s((8, tn * units), F32), s(blocks, BF))
    vm = pltpu.VMEM
    return pl.pallas_call(
        functools.partial(feed, dp),
        out_shape=outs,
        in_specs=[VM] * 12 + [ANY],
        out_specs=tuple([VM] * 7 + [ANY]),
        scratch_shapes=[vm((length, tn * units), BF), vm((length, tn * units), BF), vm((length, width), BF),
                        vm((length, width), BF), vm((width, length), BF), vm((length, width), F32),
                        vm((length, width), F32), vm((length, 1), F32), vm((length, 1), F32), vm(blocks, BF),
                        vm(blocks, BF)] + sems(dp) + sems(dp) + [DMA((2,))],
        compiler_params=params(2, 62),
        name="feed_forward",
    )(x, ctx, wo, wi, wf, *vectors, small, cot)


def attend_backward(dp, x_ref, w_ref, ids_ref, small_ref, q_ref, k_ref, v_ref, near_ref, far_ref, lq_ref, lk_ref, mix_ref,
                    sum_ref, ker_ref, z_ref, a_ref, v2_ref, w2_ref, dc_ref, gr1_ref, dwo_in, dwi_in, dwf_in, half_ref,
                    gtok_ref, dw_ref, vecq_ref, vecv_ref, gtap_ref, go_ref, gi_ref, gf_ref, home_ref,
                    pre_ref, glq_ref, glk_ref, gsum_ref, gz_ref, gk_ref, padv_ref, padc_ref, xt_ref,
                    g_ss, g_rs, y_ss, y_rs, local, *bufs):
    length, width = x_ref.shape
    tn = w_ref.shape[0]
    cols = width // tn
    scale = LAND ** -0.25
    size = length // dp
    pairs = width // 128
    groups = width // 256
    me = Place(dp, tn)
    n = reduce_count(dp)
    half = dwi_in.shape[5] // 2
    plan = [(dwf_in, 0, half, gf_ref), (dwf_in, half, half, gf_ref), (dwi_in, 0, half, gi_ref), (dwi_in, half, half, gi_ref),
            (dwo_in, 0, cols, go_ref)]
    lanes = []
    for k, (src, lo, w, dst) in enumerate(plan):
        lanes.append(reduce_lane(me, src, lo, w, bufs[5 * k : 5 * k + 5], Sub(g_ss, k * n), Sub(g_rs, k * n), local.at[k],
                                 [(dst, lo, 0, w)]))
    quarter = dp // 4
    sides = []
    for k in range(4):
        here, there = pl.ds(k * quarter, quarter), pl.ds(me.t * dp + k * quarter, quarter)
        sides.append(remote(half_ref.at[here], home_ref.at[there], y_ss.at[k], y_rs.at[k], (me.i, 1 - me.t)))
    kept = pltpu.make_async_copy(half_ref, home_ref.at[pl.ds(me.t * dp, dp)], local.at[5])
    greet(me, False)
    for lane in lanes:
        lane[0]()
    kept.start()
    sides[0].start()
    sides[1].start()
    tick = Ticks([lanes[0][1], lanes[1][1], lanes[2][1], lanes[3][1], lanes[4][1], lanes[0][2], lanes[1][2], sides[2].start,
                  lanes[0][3], lanes[2][2], lanes[1][3], lanes[3][2], sides[3].start, lanes[4][2], lanes[2][3], lanes[3][3],
                  lanes[4][3]])
    ids = ids_ref[pl.ds(own_sequence(), 1), :]
    member = jnp.where(lax.broadcasted_iota(jnp.int32, (LAND, length), 0) == ids, 1.0, 0.0).astype(F32)
    count = jnp.sum(member, axis=1, keepdims=True)
    member = member.astype(BF)
    valid = ids < LAND
    eye = pair_eye()

    for g in range(groups):
        own = slice(g * 256, (g + 1) * 256)
        gsum_ref[:, own] = gather_diag(nn(near_ref[own, :], dc_ref[:, own]))
    for p in range(pairs):
        own = slice(p * 128, (p + 1) * 128)
        gmix = gsum_ref[:, own]
        gz_ref[:, own] = pair_nt(gmix, sum_ref[:, own])
        gsum_ref[:, own] = pair_nn(pair_turn(z_ref[ITERS, :, own]), gmix)

    tick(5)
    gk_ref[...] = jnp.zeros_like(gk_ref)

    def iterate(m, carry):
        n = ITERS - 1 - m
        for p in range(pairs):
            own = slice(p * 128, (p + 1) * 128)
            grad = 0.25 * gz_ref[:, own]
            kernel = ker_ref[:, own]
            z = z_ref[n, :, own]
            a = a_ref[n, :, own]
            v2 = v2_ref[n, :, own]
            w2 = w2_ref[n, :, own]
            dw2 = pair_nn(pair_turn(z), grad)
            at = pair_turn(a)
            dv2 = -pair_nn(at, dw2)
            da = -pair_nt(dw2, v2) - pair_nt(dv2, 7.0 * eye - a) + pair_nn(at, dv2)
            gk_ref[:, own] += pair_nt(da, z)
            gz_ref[:, own] = pair_nt(grad, w2) + pair_nn(pair_turn(kernel), da)
        return carry

    lax.fori_loop(0, ITERS // 2, iterate, 0)
    tick(1)
    lax.fori_loop(ITERS // 2, ITERS, iterate, 0)
    tick(2)

    for p in range(pairs):
        own = slice(p * 128, (p + 1) * 128)
        kernel = ker_ref[:, own]
        gz = gz_ref[:, own]
        total = jnp.sum(pair_sum(kernel * kernel), axis=0, keepdims=True)
        kt = pair_turn(kernel)
        back = jnp.sum(pair_sum(gz * kt), axis=0, keepdims=True)
        gk = gk_ref[:, own] + pair_turn(gz) / total - kernel * (2.0 * back / (total * total))
        mid = kernel * (gk - pair_sum(kernel * gk))
        glq_ref[:, own] = pair_nn(mid, lk_ref[:, own].astype(F32))
        glk_ref[:, own] = pair_nn(pair_turn(mid), lq_ref[:, own].astype(F32))

    flip = jnp.where(
        lax.broadcasted_iota(jnp.int32, (256, 256), 0) + lax.broadcasted_iota(jnp.int32, (256, 256), 1) == 255, 1.0, 0.0
    ).astype(BF)
    taps = [reversed_taps(tap_rows(small_ref, t)) for t in range(tn)]
    padv_ref[...] = jnp.zeros_like(padv_ref)
    padc_ref[...] = jnp.zeros_like(padc_ref)
    inner = slice(128, 128 + length)
    for g in range(groups):
        own = slice(g * 256, (g + 1) * 256)
        lk4 = spread(lk_ref[:, own])
        lq4 = spread(lq_ref[:, own])
        near = near_ref[own, :].astype(F32)
        gnear = nt(spread(mix_ref[:, own]), dc_ref[:, own])
        drop = jnp.sum((near * gnear).reshape(4, LAND, length), axis=1, keepdims=True)
        first = (near * (gnear.reshape(4, LAND, length) - drop).reshape(256, length)).astype(BF)
        glk_ref[:, own] += gather_diag(nn(first, q_ref[:, own]))
        gsum4 = spread(gsum_ref[:, own].astype(BF))
        far = far_ref[own, :].astype(F32)
        gfar = nt(gsum4, v_ref[:, own])
        drop = jnp.sum(far * gfar, axis=1, keepdims=True)
        third = (far * (gfar - drop)).astype(BF)
        glq_ref[:, own] += gather_diag(nn(third, k_ref[:, own]))
        glq = turn((glq_ref[:, own] / count).astype(BF))
        glk = turn((glk_ref[:, own] / count).astype(BF))
        dq = (nn(turn(lk4), first) + nn(glq, member)) * scale
        dk = (nn(turn(lq4), third) + nn(glk, member)) * scale
        dv = nn(turn(gsum4), far_ref[own, :])

        vt = turn(v_ref[:, own])
        padv_ref[:, inner] = jnp.where(valid, vt, jnp.zeros_like(vt))
        padc_ref[:, inner] = turn(dc_ref[:, own])
        parts = []
        for h in range(4):
            band = band_of(taps, 4 * g + h)
            parts.append(unblock(nt(blocks_of(padc_ref, h * LAND, 256), band), 256))
            plain = jnp.concatenate(
                [padc_ref[h * LAND : (h + 1) * LAND, 128 + at : 128 + at + 256] for at in range(0, length, 256)], axis=0
            )
            gram = nn(nt(flip, plain).astype(BF), blocks_of(padv_ref, h * LAND, 256))
            gram = pltpu.roll(gram, 0, 1, stride=1, stride_axis=0)
            gtap_ref[4 * g + h : 4 * g + h + 1, :] = jnp.sum(gram, axis=0, keepdims=True)
        dv = dv + jnp.where(valid, jnp.concatenate(parts, axis=0), 0.0)
        vecq_ref[own, :] = jnp.sum(dq, axis=1, keepdims=True)
        vecv_ref[own, :] = jnp.sum(dv, axis=1, keepdims=True)
        for lower in range(0, 256, 128):
            c = g * 256 + lower
            t, r = c // cols, c % cols
            pre_ref[t, r : r + 128, :] = dq[lower : lower + 128].astype(BF)
            pre_ref[t, cols + r : cols + r + 128, :] = dk[lower : lower + 128].astype(BF)
            pre_ref[t, 2 * cols + r : 2 * cols + r + 128, :] = dv[lower : lower + 128].astype(BF)
        tick(2)

    xt_ref[...] = turn(x_ref[...])
    tick(2)
    for t in range(tn):
        dw_ref[t] = nt(xt_ref[...], pre_ref[t]).astype(BF)
    tick(2)
    for at in range(0, length, 256):
        part = nn(w_ref[0], pre_ref[0, :, at : at + 256])
        for t in range(1, tn):
            part = part + nn(w_ref[t], pre_ref[t, :, at : at + 256])
        gtok_ref[at // size : (at + 256) // size] = (
            (gr1_ref[at : at + 256, :].astype(F32) + turn(part)).reshape(256 // size, size, width).astype(BF)
        )
    tick.rest()
    for lane in lanes:
        lane[4]()
    wait_all(sides)
    kept.wait()


def call_attend_backward(dp, x, w, ids, small, saved, dc, gr1, dwo, dwi, dwf, half):
    length, width = x.shape
    tn = w.shape[0]
    cols = width // tn
    s = jax.ShapeDtypeStruct
    depth, units = dwi.shape[4:]
    outs = (s(half.shape, BF), s((tn, width, 3 * cols), BF), s((width, 1), F32), s((width, 1), F32),
            s((width // LAND, 512), F32), s((depth, cols), F32), s((depth, units), F32), s((depth, units), F32),
            s((tn * dp,) + half.shape[1:], BF))
    args = (x, w, ids, small, *saved, dc, gr1, dwo, dwi, dwf, half)
    vm = pltpu.VMEM
    little = vm((LAND, width), F32)
    n = 5 * reduce_count(dp)
    scratch = [vm((tn, 3 * cols, length), BF)] + [little] * 5
    scratch += [vm((256, length + 256), BF), vm((256, length + 256), BF), vm((width, length), BF)]
    scratch += sems(n) + sems(4) + [DMA((6,))]
    for wide in (units // 2,) * 4 + (cols,):
        scratch += reduce_bufs(dp, tn, depth, wide)
    return pl.pallas_call(
        functools.partial(attend_backward, dp),
        out_shape=outs,
        in_specs=[VM] * (len(args) - 4) + [ANY] * 4,
        out_specs=tuple([VM] * 8 + [ANY]),
        scratch_shapes=scratch,
        compiler_params=params(3, 62),
        name="attend_backward",
    )(*args)


def local(tokens, cotangent, landmark_ids, w_query, w_key, w_value, b_query, b_value, conv_taps, w_out, b_out,
          first_gain, first_shift, w_inner, b_inner, w_outer, b_outer, second_gain, second_shift):
    dp = lax.axis_size("dp")
    tn = lax.axis_size("tensor")
    part, width = tokens.shape[1:]
    length = dp * part
    cols = w_query.shape[1]
    units = w_inner.shape[1]
    heads, taps = conv_taps.shape
    row = lambda v: v.reshape(1, -1)
    vectors = [row(v) for v in (b_out, first_gain, first_shift, b_outer, second_gain, second_shift)]

    def join(w):
        return w.reshape(tn, width, w.shape[-1])

    def cut(g):
        return g.reshape(tn, dp // 4, 2, 2, width // dp, g.shape[2])

    rows, wqkv, wout, small = call_bring(
        dp, tn, tokens, w_query, w_key, w_value, w_out, row(b_query), row(b_value), row(b_inner), conv_taps
    )
    rows = rows.reshape(length, width)
    wqkv, wout = join(wqkv), join(wout)
    q, k, v, near, far, ctx, *rest_saved, wi, wf = call_attend_forward(
        dp, rows, wqkv, small, landmark_ids, w_inner, w_outer
    )
    gr1, dc, dwo, dwi, dwf, vec, bsum, half = call_feed(
        dp, rows, ctx, wout, join(wi), join(wf), vectors, small, cotangent
    )
    grad_rows, dwqkv, gbq, gbv, gtap, go, gi, gf, out_home = call_attend_backward(
        dp, rows, wqkv, landmark_ids, small, (q, k, v, near, far, *rest_saved), dc, gr1, cut(dwo), cut(dwi), cut(dwf), half
    )
    share = width // dp
    norms = jnp.sum(vec, axis=1).reshape(6, dp, share).transpose(1, 0, 2).reshape(dp, 6 * share)
    norms = jnp.pad(norms, ((0, 0), (0, 1024 - 6 * share))).reshape(dp, 8, 128)
    rest = jnp.concatenate(
        [gbq.reshape(tn, cols), gbv.reshape(tn, cols), jnp.sum(bsum, axis=0).reshape(tn, units),
         gtap[:, FLIP_AT : FLIP_AT + taps].reshape(tn, heads * taps)], axis=1)
    rest = jnp.pad(rest, ((0, 0), (0, 24 * 128 - rest.shape[1]))).reshape(tn, 24, 128)
    grad_home, gq, gk, gv, nsum, rsum = call_carry_home(dp, tn, grad_rows, cut(dwqkv), norms, rest)
    n = nsum.reshape(-1)[: 6 * share].reshape(6, share)
    r = rsum.reshape(-1)
    at = 2 * cols + units
    return (out_home, grad_home, gq, gk, gv, r[:cols], r[cols : 2 * cols],
            r[at : at + heads * taps].reshape(heads, taps), go, n[0], n[1], n[2], gi, r[2 * cols : at], gf,
            n[3], n[4], n[5])


def solution(mesh):
    return jax.shard_map(
        local,
        mesh=mesh,
        in_specs=(
            P(None, "dp", None),
            P(None, "dp", None),
            P(),
            P("dp", "tensor"),
            P("dp", "tensor"),
            P("dp", "tensor"),
            P("tensor"),
            P("tensor"),
            P("tensor", None),
            P("dp", "tensor"),
            P(),
            P(),
            P(),
            P("dp", "tensor"),
            P("tensor"),
            P("dp", "tensor"),
            P(),
            P(),
            P(),
        ),
        out_specs=(
            P(None, "dp", None),
            P(None, "dp", None),
            P("dp", "tensor"),
            P("dp", "tensor"),
            P("dp", "tensor"),
            P("tensor"),
            P("tensor"),
            P("tensor", None),
            P("dp", "tensor"),
            P("dp"),
            P("dp"),
            P("dp"),
            P("dp", "tensor"),
            P("tensor"),
            P("dp", "tensor"),
            P("dp"),
            P("dp"),
            P("dp"),
        ),
        check_vma=False,
    )
```

time: 534 us -> 436 us (0.82)
  Pallas kernels: 492 us -> 390 us
  local copies, waits for them, and re-layouts: 28.8 us -> 34.3 us
    pallas_call x5, Pallas kernels: 492 us -> 390 us  [the longest x1 117 us: call_attend_backward(): pl.pallas_call(functools.partial(attend_backward, dp), out_shape=outs, in...]
    reshape x0 -> x9, local copies, waits for them, and re-layouts: none -> 9.63 us  [local(): row = lambda v: v.reshape(1, -1)]
    unnamed x36 -> x43, local copies, waits for them, and re-layouts: 15.7 us -> 21.2 us
where the time goes in v3:
time: 436 us; the launch traced here: 428 us
  Pallas kernels  390 us (89%)
  local copies, waits for them, and re-layouts  34.3 us (8%)
    pallas_call x1, Pallas kernels, call_attend_backward(): pl.pallas_call(functools.partial(attend_backward, dp), out_shape=outs, in...  117 us
    pallas_call x1, Pallas kernels, call_feed(): pl.pallas_call(functools.partial(feed, dp), out_shape=outs, in_specs=[VM]...  78 us
    pallas_call x1, Pallas kernels, call_attend_forward(): pl.pallas_call(functools.partial(attend_forward, dp), out_shape=outs, in_...  71.8 us
    pallas_call x1, Pallas kernels, call_carry_home(): pl.pallas_call(functools.partial(carry_home, dp, tn), out_shape=outs, in_...  68.4 us
    pallas_call x1, Pallas kernels, call_bring(): pl.pallas_call(functools.partial(bring, dp, tn), out_shape=outs, in_specs...  54.3 us
    unnamed x43, local copies, waits for them, and re-layouts  21.2 us
    reshape x9, local copies, waits for them, and re-layouts, local(): row = lambda v: v.reshape(1, -1)  9.63 us

profile of v3, /device:TPU:0, one launch (start us, length us, event | category | flops | bytes accessed | tf_op | source)
XLA Modules:
  0.0 428.0 jit_solution(14209061646654974831)
XLA Ops:
  0.7 0.7 reshape.139.bq
  1.3 0.7 reshape.140.bv
  2.0 1.3 reshape.147.bo_in
  3.3 1.3 reshape.148.g1_in
  4.5 1.3 reshape.149.s1_in
  5.8 1.3 reshape.150.bf_in
  7.1 1.3 reshape.151.g2_in
  8.3 1.3 reshape.152.s2_in
  9.6 0.7 reshape.141.bi
  10.3 1.9 copy-done.2
  12.2 0.8 copy-done.6
  12.9 0.8 copy-done.7
  13.7 0.8 copy-done.8
  14.5 0.8 copy-done.9
  15.3 0.7 copy-done.10
  15.9 54.3 %bring.1 = (bf16[16,64,768]{2,1,0:T(8,128)(2,1)S(1)}, bf16[2,4,2,2,48,1152]{5,4,3,2,1,0:T(8,128)(2,1)S(1)}, bf16[2,4,2,2,48,384]{5,4,3,2,1,0:T(8,128)(2,1)S(1)}, f32[2,32,128]{2,1,0:T(8,128)S(1)}) custom-call(bf16[32,64,768]{2,1,0:T(8,128)(2,1)S(1)} %copy-done.2, bf16[48,384]{1,0:T(8,128)(2,1)S(1)} %copy-done.6, bf16[48,384]{1,0:T(8,128)(2,1)S(1)} %copy-done.7, ...), custom_call_target="tpu_custom_call" | custom-call | tf_op jit(solution)/shard_map/bring/pallas_call | solution.py:260
  70.3 0.0 copy-start
  70.3 1.1 copy-done
  71.4 1.8 copy-done.1
  73.3 1.0 copy-done.4
  74.3 0.6 copy-done.5
  74.9 71.8 %attend_forward.1 = (bf16[1024,768]{1,0:T(8,128)(2,1)}, bf16[1024,768]{1,0:T(8,128)(2,1)}, bf16[1024,768]{1,0:T(8,128)(2,1)}, bf16[768,1024]{1,0:T(8,128)(2,1)},...) custom-call(bf16[1024,768]{1,0:T(8,128)(2,1)} %bitcast.26, ...), custom_call_target="tpu_custom_call" | custom-call | tf_op jit(solution)/shard_map/attend_forward/pallas_call | solution.py:623
  146.7 78.0 %feed_forward.1 = (bf16[1024,768]{1,0:T(8,128)(2,1)}, bf16[1024,768]{1,0:T(8,128)(2,1)}, bf16[2,768,384]{2,1,0:T(8,128)(2,1)}, bf16[2,768,1536]{2,1,0:T(8,128)(2...) custom-call(bf16[1024,768]{1,0:T(8,128)(2,1)} %bitcast.27, ...), custom_call_target="tpu_custom_call" | custom-call | tf_op jit(solution)/shard_map/feed_forward/pallas_call | solution.py:782
  224.7 0.0 copy-start.14
  224.7 0.0 copy-start.13
  224.7 117.4 %attend_backward.1 = (bf16[16,64,768]{2,1,0:T(8,128)(2,1)}, bf16[2,768,1152]{2,1,0:T(8,128)(2,1)}, f32[768,1]{1,0:T(8,128)}, f32[768,1]{1,0:T(8,128)}, f32[12,51...) custom-call(bf16[1024,768]{1,0:T(8,128)(2,1)} %bitcast.28, ...), custom_call_target="tpu_custom_call" | custom-call | tf_op jit(solution)/shard_map/attend_backward/pallas_call | solution.py:975
  342.1 1.2 reduce
  343.3 1.2 reduce.1
  344.5 0.8 slice.55
  345.3 0.1 reshape.163
  345.5 0.1 reshape.157
  345.6 0.1 reshape.158
  345.7 0.0 copy-start.3
  345.8 1.4 copy-done.3
  347.2 68.4 %carry_home.1 = (bf16[32,64,768]{2,1,0:T(8,128)(2,1)S(1)}, f32[48,384]{1,0:T(8,128)S(1)}, f32[48,384]{1,0:T(8,128)S(1)}, f32[48,384]{1,0:T(8,128)S(1)}, f32[8,128]{1,0:T(8,128)S(1)}, /*index=5*/f32[24,128]{1,0:T(8,128)S(1)}) custom-call(bf16[16,64,768]{2,1,0:T(8,128)(2,1)S(1)} %copy-done.3, bf16[2,4,2,2,48,1152]{5,4,3,2,1,0:T(8,128)(2,1)} %bitcast.40, ...), custom_call_target="tpu_custom_call" | custom-call | tf_op jit(solution)/shard_map/carry_home/pallas_call | solution.py:348
  415.6 0.7 reshape.166
  416.2 0.6 fusion.1
  416.8 0.6 slice_bitcast_fusion.1
  417.4 0.6 slice_bitcast_fusion
  418.0 3.9 copy.50
  421.9 1.7 copy.51
  423.6 0.6 copy.52
  424.2 0.6 copy.53
  424.8 0.6 copy.54
  425.5 0.6 copy.55
  426.1 0.7 copy.56
  426.8 0.0 copy-done.11
  426.8 0.7 copy.57
  (27 shorter events, 0.2 us)
Async XLA Ops:
  10.3 1.9 copy-start.2
  12.2 0.8 copy-start.6
  12.9 0.8 copy-start.7
  13.7 0.8 copy-start.8
  14.5 0.8 copy-start.9
  15.2 0.7 copy-start.10
  70.3 1.1 copy-start
  71.4 1.8 copy-start.1
  73.3 1.0 copy-start.4
  74.3 0.6 copy-start.5
  224.7 120.7 %copy-start.14 = (f32[8,3072]{1,0:T(8,128)S(1)}, f32[8,3072]{1,0:T(8,128)}, u32[]{:S(2)}) copy-start(f32[8,3072]{1,0:T(8,128)} %get-tuple-element.95) | copy-start | bytes 294916
  224.7 120.7 %copy-start.13 = (f32[6,8,768]{2,1,0:T(8,128)S(1)}, f32[6,8,768]{2,1,0:T(8,128)}, u32[]{:S(2)}) copy-start(f32[6,8,768]{2,1,0:T(8,128)} %get-tuple-element.92) | copy-start | bytes 442372
  345.7 1.4 copy-start.3
  421.9 3.6 copy-start.15
  421.9 4.2 copy-start.12
  421.9 4.9 %copy-start.11 = (f32[48,1536]{1,0:T(8,128)S(1)}, f32[48,1536]{1,0:T(8,128)}, u32[]{:S(2)}) copy-start(f32[48,1536]{1,0:T(8,128)} %get-tuple-element.146) | copy-start | bytes 884740

commit v4 on v3

--- a/solution.py
+++ b/solution.py
@@ -11,6 +11,7 @@
 BF = jnp.bfloat16
 MESH = pl.DeviceIdType.MESH
 ANY = pl.BlockSpec(memory_space=pl.ANY)
+TOP = 62
 VM = pl.BlockSpec(memory_space=pltpu.VMEM)
 DMA = pltpu.SemaphoreType.DMA
 SMALL_ROWS = 32
@@ -130,9 +131,9 @@
     return (a.astype(F32) + b.astype(F32)).astype(BF)
 
 
-def reduce_lane(me, src, lo, w, bufs, ss, rs, local, puts):
+def reduce_lane(me, src, lo, w, bufs, ss, rs, local, puts, north_first=False):
     t, z, x, c, n = me.t, me.z, me.x, me.c, me.nz
-    mine, rc, rx, ry, rz = bufs
+    mine, rc, r1, r2, rz = bufs
     cols = pl.ds(lo, w)
 
     def move(a, b, q, to):
@@ -140,12 +141,17 @@
 
     keep = pltpu.make_async_copy(src.at[:, :, :, c, :, cols], mine, local)
     core = move(src.at[:, :, :, 1 - c, :, cols], rc, 0, me.at(c=1 - c))
-    east = move(rc.at[:, :, 1 - x], rx, 1, me.at(x=1 - x))
-    north = move(rx.at[1 - t], ry, 2, me.at(t=1 - t))
+    px, py = me.at(x=1 - x), me.at(t=1 - t)
+    if north_first:
+        first = move(rc.at[1 - t], r1, 1, py)
+        second = move(r1.at[:, 1 - x], r2, 2, px)
+    else:
+        first = move(rc.at[:, :, 1 - x], r1, 1, px)
+        second = move(r1.at[1 - t], r2, 2, py)
     lines = []
     for q in range(1, n):
         to = lax.rem(z + q, n)
-        lines.append(move(ry.at[to], rz.at[q], 2 + q, me.at(z=to)))
+        lines.append(move(r2.at[to], rz.at[q], 2 + q, me.at(z=to)))
 
     def s0():
         keep.start()
@@ -155,37 +161,52 @@
         keep.wait()
         core.wait()
         rc[...] = add_low(rc[...], mine[...])
-        east.start()
+        first.start()
 
     def s2():
-        east.wait()
-        rx[...] = add_low(rx[...], rc[:, :, x])
-        north.start()
+        first.wait()
+        r1[...] = add_low(r1[...], rc[t] if north_first else rc[:, :, x])
+        second.start()
 
     def s3():
-        north.wait()
-        ry[...] = add_low(ry[...], rx[t])
+        second.wait()
+        r2[...] = add_low(r2[...], r1[:, x] if north_first else r1[t])
         start_all(lines)
 
     def s4():
-        total = ry[z].astype(F32)
+        total = r2[z].astype(F32)
         wait_all(lines)
         for q in range(1, n):
             total = total + rz[q].astype(F32)
-        for dst, at, first, width in puts:
-            dst[:, at : at + width] = total[:, first : first + width]
+        for dst, at, first_col, width in puts:
+            dst[:, at : at + width] = total[:, first_col : first_col + width]
 
     return [s0, s1, s2, s3, s4]
 
 
-def reduce_bufs(dp, tn, depth, w):
+def reduce_bufs(dp, tn, depth, w, north_first=False):
     nz = dp // 4
+    one = (nz, 2) if north_first else (tn, nz)
     return [pltpu.VMEM((tn, nz, 2, depth, w), BF), pltpu.VMEM((tn, nz, 2, depth, w), BF),
-            pltpu.VMEM((tn, nz, depth, w), BF), pltpu.VMEM((nz, depth, w), BF), pltpu.VMEM((nz, depth, w), BF)]
+            pltpu.VMEM(one + (depth, w), BF), pltpu.VMEM((nz, depth, w), BF), pltpu.VMEM((nz, depth, w), BF)]
 
 
 def reduce_count(dp):
     return dp // 4 + 2
+
+
+class Fetch:
+    def __init__(self, src, dst, sem):
+        self.copy, self.open = pltpu.make_async_copy(src, dst, sem), True
+
+    def start(self):
+        self.copy.start()
+        return self
+
+    def wait(self):
+        if self.open:
+            self.copy.wait()
+        self.open = False
 
 
 class Sub:
@@ -231,8 +252,9 @@
                                  Sub(g_ss, k * n), Sub(g_rs, k * n), local.at[k]))
     piece[...] = jnp.zeros_like(piece)
     for ref, first in ((bq, ROWS_BQ), (bv, ROWS_BV), (bi, ROWS_BI)):
-        for r in range(ref.shape[1] // 128):
-            piece[first + r : first + r + 1, :] = ref[:, r * 128 : (r + 1) * 128].astype(F32)
+        line = ref[...].astype(F32).reshape(1, ref.shape[0])
+        for r in range(ref.shape[0] // 128):
+            piece[first + r : first + r + 1, :] = line[:, r * 128 : (r + 1) * 128]
     heads, width = taps.shape
     tap = taps[...].astype(F32)
     piece[ROWS_TAPS : ROWS_TAPS + heads, :width] = tap
@@ -263,13 +285,14 @@
         in_specs=[ANY] * 5 + [VM] * 4,
         out_specs=(ANY, ANY, ANY, ANY),
         scratch_shapes=sems(dp) + sems(4 * gather_count(dp)) + [DMA((6,)), pltpu.VMEM((SMALL_ROWS, 128), F32)],
-        compiler_params=params(0, 16),
+        compiler_params=params(0, TOP),
         name="bring",
     )(tok, wq, wk, wv, wo, bq, bv, bi, taps)
 
 
-def carry_home(dp, tn, g_rows, dwqkv, norms, rest, g_home, gq, gk, gv, n_out, r_out,
-               r_ss, r_rs, v_ss, v_rs, g_ss, g_rs, local, nbuf, rbuf, nall, rall, nsum, rsum, *bufs):
+def carry_home(dp, tn, g_rows, dwqkv, vec, bsum, vecs, gtap, g_home, gq, gk, gv, gbq, gbv, gtaps, gbi, *refs):
+    n_outs, (r_ss, r_rs, v_ss, v_rs, g_ss, g_rs, local, norms, rest, nbuf, rbuf, nall, rall, nsum, rsum) = refs[:6], refs[6:21]
+    bufs = refs[21:]
     me = Place(dp, tn)
     cols = gq.shape[1]
     n = reduce_count(dp)
@@ -293,10 +316,25 @@
           remote(rest.at[1 - me.t], rbuf, v_ss.at[1], v_rs.at[1], partner)]
     for lane in lanes:
         lane[0]()
-    start_all(v1)
     start_all(first)
     own.start()
     second[0].start()
+    share = n_outs[0].shape[0]
+    six = jnp.sum(vec[...], axis=1)
+    norms[...] = jnp.zeros_like(norms)
+    rest[...] = jnp.zeros_like(rest)
+    for j in range(dp):
+        norms[j, 0:6, :share] = six[:, j * share : (j + 1) * share]
+    units = jnp.sum(bsum[...], axis=0, keepdims=True)
+    per, taps = gtaps.shape
+    for t in range(tn):
+        for line, first_row, size in ((vecs[0:1, :], ROWS_BQ, cols), (vecs[1:2, :], ROWS_BV, cols),
+                                      (units, ROWS_BI, gbi.shape[0])):
+            for r in range(size // 128):
+                lo = t * size + r * 128
+                rest[t, first_row + r : first_row + r + 1, :] = line[:, lo : lo + 128]
+        rest[t, ROWS_TAPS : ROWS_TAPS + per, :taps] = gtap[t * per : (t + 1) * per, FLIP_AT : FLIP_AT + taps]
+    start_all(v1)
     for lane in lanes:
         lane[1]()
     wait_all(v1)
@@ -325,35 +363,42 @@
     for k in range(1, dp):
         ntot = ntot + nall[k]
         rtot = rtot + rall[k]
-    n_out[...] = ntot
-    r_out[...] = rtot
+    for k in range(6):
+        n_outs[k][...] = ntot[k, :share]
+    for ref, first_row in ((gbq, ROWS_BQ), (gbv, ROWS_BV), (gbi, ROWS_BI)):
+        size = ref.shape[0]
+        ref[...] = jnp.concatenate([rtot[first_row + r : first_row + r + 1] for r in range(size // 128)], axis=1).reshape(size)
+    gtaps[...] = rtot[ROWS_TAPS : ROWS_TAPS + per, :taps]
     for lane in lanes:
         lane[4]()
     own.wait()
     wait_all(second)
 
 
-def call_carry_home(dp, tn, g_rows, dwqkv, norms, rest):
+def call_carry_home(dp, tn, g_rows, dwqkv, vec, bsum, vecs, gtap, taps):
     s = jax.ShapeDtypeStruct
     r, w = g_rows.shape[1:]
     depth, cols = dwqkv.shape[4], dwqkv.shape[5] // 3
     share = s((depth, cols), F32)
-    outs = (s((tn * dp, r, w), BF), share, share, share, s(norms.shape[1:], F32), s(rest.shape[1:], F32))
+    norms, rest = (dp, 8, 128), (tn, 24, 128)
+    outs = (s((tn * dp, r, w), BF), share, share, share, s((cols,), F32), s((cols,), F32), s(taps.shape, F32),
+            s((bsum.shape[1] // tn,), F32)) + (s((depth,), F32),) * 6
     scratch = sems(2 * dp) + sems(2 * dp) + sems(3 * reduce_count(dp)) + [DMA((4,))]
-    scratch += [pltpu.VMEM(norms.shape, F32), pltpu.VMEM(rest.shape[1:], F32),
-                pltpu.VMEM((dp,) + norms.shape[1:], F32), pltpu.VMEM((dp,) + rest.shape[1:], F32),
-                pltpu.VMEM(norms.shape, F32), pltpu.VMEM(rest.shape[1:], F32)]
+    scratch += [pltpu.VMEM(norms, F32), pltpu.VMEM(rest, F32),
+                pltpu.VMEM(norms, F32), pltpu.VMEM(rest[1:], F32),
+                pltpu.VMEM((dp,) + norms[1:], F32), pltpu.VMEM((dp,) + rest[1:], F32),
+                pltpu.VMEM(norms, F32), pltpu.VMEM(rest[1:], F32)]
     for _ in range(3):
         scratch += reduce_bufs(dp, tn, depth, cols)
     return pl.pallas_call(
         functools.partial(carry_home, dp, tn),
         out_shape=outs,
-        in_specs=[ANY, ANY, VM, VM],
-        out_specs=(ANY,) + (VM,) * 5,
+        in_specs=[ANY, ANY] + [VM] * 4,
+        out_specs=(ANY,) + (VM,) * 13,
         scratch_shapes=scratch,
-        compiler_params=params(4, 48),
+        compiler_params=params(4, TOP),
         name="carry_home",
-    )(g_rows, dwqkv, norms, rest)
+    )(g_rows, dwqkv, vec, bsum, vecs, gtap)
 
 
 F32 = jnp.float32
@@ -490,11 +535,17 @@
     return nn(rows.astype(BF), turned)
 
 
-def attend_forward(dp, x_ref, w_ref, small_ref, ids_ref, wi_ref, wf_ref,
-                   q_ref, k_ref, v_ref, near_ref, far_ref, ctx_ref, lq_ref, lk_ref, mix_ref, sum_ref, ker_ref,
-                   z_ref, a_ref, v2_ref, w2_ref, wi_all, wf_all, pad_ref, g_ss, g_rs, local):
+def attend_forward(dp, x_in, w_in, small_ref, ids_ref, wi_ref, wf_ref, cot_ref,
+                   q_out, k_out, v_out, near_out, far_out, ctx_out, lq_ref, lk_ref, mix_ref, sum_ref, ker_ref,
+                   z_out, a_out, v2_out, w2_out, wi_all, wf_all, cota_ref, pad_ref, x_ref, w_ref, q_ref, k_ref, v_ref,
+                   near_ref, far_ref, ctx_ref, z_ref, a_ref, v2_ref, w2_ref, g_ss, g_rs, c_ss, c_rs, local, move):
     length, width = x_ref.shape
     tn = w_ref.shape[0]
+    loads = [Fetch(x_in, x_ref, move.at[0]).start(), Fetch(w_in, w_ref, move.at[1]).start()]
+    q_w, k_w, v_w, near_w, far_w, ctx_w, z_w, a_w, v2_w, w2_w = writes = [
+        Fetch(a, b, move.at[2 + k]) for k, (a, b) in enumerate((
+            (q_ref, q_out), (k_ref, k_out), (v_ref, v_out), (near_ref, near_out), (far_ref, far_out), (ctx_ref, ctx_out),
+            (z_ref, z_out), (a_ref, a_out), (v2_ref, v2_out), (w2_ref, w2_out)))]
     cols = width // tn
     scale = LAND ** -0.25
     rows_at = 256
@@ -515,9 +566,14 @@
                 lane[s]()
         return run
 
-    greet(me, False)
+    greet(me)
     stage(0, 0)()
     stage(1, 0)()
+    arriving = []
+    for k in range(1, early_blocks(dp) + 1):
+        j = lax.rem(me.i + k, dp)
+        arriving.append(remote(cot_ref.at[me.t * dp + j], cota_ref.at[me.i], c_ss.at[k], c_rs.at[k], (j, me.t)))
+    start_all(arriving)
     tick = Ticks([stage(0, 1), stage(0, 2), stage(1, 1), stage(0, 3), stage(1, 2), stage(1, 3), stage(0, 4), stage(1, 4)])
     bq = [side_row(small_ref, t, ROWS_BQ, 3) for t in range(tn)]
     bv = [side_row(small_ref, t, ROWS_BV, 3) for t in range(tn)]
@@ -532,7 +588,9 @@
             v_ref[at, own] = (out[:, 2 * cols :] + bv[t]).astype(BF)
         return carry
 
+    wait_all(loads)
     lax.fori_loop(0, length // rows_at, project, 0)
+    start_all([q_w, k_w, v_w])
 
     ids = ids_ref[pl.ds(own_sequence(), 1), :]
     member = jnp.where(lax.broadcasted_iota(jnp.int32, (LAND, length), 0) == ids, 1.0, 0.0).astype(F32)
@@ -551,6 +609,7 @@
         left = lax.broadcasted_iota(jnp.int32, kernel.shape, 1) < LAND
         total = jnp.sum(pair_sum(kernel * kernel), axis=0, keepdims=True)
         z_ref[0, :, own] = pair_turn(kernel) / total
+    tick()
 
     for g in range(groups):
         own = slice(g * 256, (g + 1) * 256)
@@ -564,8 +623,8 @@
         scores = scores / jnp.sum(scores, axis=1, keepdims=True)
         far_ref[own, :] = scores.astype(BF)
         sum_ref[:, own] = gather_diag(nn(far_ref[own, :], v_ref[:, own]))
-        if g == 1:
-            tick()
+    tick()
+    start_all([near_w, far_w])
 
     def iterate(n, carry):
         for p in range(pairs):
@@ -583,7 +642,7 @@
     lax.fori_loop(0, ITERS // 2, iterate, 0)
     tick()
     lax.fori_loop(ITERS // 2, ITERS, iterate, 0)
-    tick(2)
+    start_all([z_w, a_w, v2_w, w2_w])
 
     for p in range(pairs):
         own = slice(p * 128, (p + 1) * 128)
@@ -602,12 +661,17 @@
             parts.append(unblock(nt(blocks_of(pad_ref, h * LAND, 256), band), 256))
         att = (att + jnp.concatenate(parts, axis=0)).astype(BF)
         ctx_ref[:, own] = turn(att)
-        if g == 0:
-            tick()
+    ctx_w.start()
     tick.rest()
-
-
-def call_attend_forward(dp, x, w, small, ids, wi, wf):
+    wait_all(arriving)
+    wait_all(writes)
+
+
+def early_blocks(dp):
+    return dp // 2
+
+
+def call_attend_forward(dp, x, w, small, ids, wi, wf, cot):
     length, width = x.shape
     s = jax.ShapeDtypeStruct
     big = s((length, width), BF)
@@ -619,16 +683,18 @@
     depth, units = wi.shape
     whole = s((tn, dp // 4, 2, 2, depth, units), BF)
     outs = (big, big, big, tall, tall, big, low, low, low, wide, wide, s((ITERS + 1, LAND, width), F32), steps, steps, steps,
-            whole, whole)
+            whole, whole, s((dp,) + cot.shape[1:], BF))
+    vm = pltpu.VMEM
     return pl.pallas_call(
         functools.partial(attend_forward, dp),
         out_shape=outs,
-        in_specs=[VM] * 4 + [ANY] * 2,
-        out_specs=tuple([VM] * 15 + [ANY] * 2),
-        scratch_shapes=[pltpu.VMEM((256, length + 256), BF)] + sems(4 * gather_count(dp)) + [DMA((4,))],
-        compiler_params=params(1, 56),
+        in_specs=[ANY] * 2 + [VM] * 2 + [ANY] * 3,
+        out_specs=tuple([ANY] * 6 + [VM] * 5 + [ANY] * 7),
+        scratch_shapes=[vm((256, length + 256), BF)] + [vm(o.shape, o.dtype) for o in (x, w) + outs[:6] + outs[11:15]]
+        + sems(4 * gather_count(dp)) + sems(dp) + [DMA((4,)), DMA((12,))],
+        compiler_params=params(1, TOP),
         name="attend_forward",
-    )(x, w, small, ids, wi, wf)
+    )(x, w, small, ids, wi, wf, cot)
 
 
 ROOT_HALF = 0.7071067811865476
@@ -667,10 +733,11 @@
     return jnp.sum(a.reshape(a.shape[0] // 8, 8, a.shape[1]), axis=0)
 
 
-def feed(dp, x_ref, ctx_ref, wo_ref, wi_ref, wf_ref, bo_in, g1_in, s1_in, bf_in, g2_in, s2_in, small_ref, cot_ref,
-         gr1_ref, dc_ref, dwo_ref, dwi_ref, dwf_ref, vec_ref, bsum_ref, half_ref,
+def feed(dp, x_in, ctx_in, wo_in, wi_in, wf_in, bo_in, g1_in, s1_in, bf_in, g2_in, s2_in, small_ref, cot_ref, cota_ref,
+         gr1_out, dc_out, dwo_out, dwi_out, dwf_out, vec_ref, bsum_ref, home_ref,
          act_ref, gi_ref, hid_ref, gr2_ref, turn_ref, n1_ref, n2_ref, rs1_ref, rs2_ref, out_ref, cots_ref,
-         c_ss, c_rs, h_ss, h_rs, local):
+         x_ref, ctx_ref, wo_ref, wi_ref, wf_ref, gr1_ref, dc_ref, dwo_ref, dwi_ref, dwf_ref,
+         c_ss, c_rs, h_ss, h_rs, f_ss, f_rs, local, move):
     length, width = x_ref.shape
     tn = wo_ref.shape[0]
     cols = width // tn
@@ -680,11 +747,29 @@
     part = length // dp
     per = size // part
     me = Place(dp, tn)
+    x_l, ctx_l, wo_l, wi_l, wf_l = loads = [
+        Fetch(a, b, move.at[k]).start() for k, (a, b) in enumerate((
+            (x_in, x_ref), (ctx_in, ctx_ref), (wo_in, wo_ref), (wi_in, wi_ref), (wf_in, wf_ref)))]
     greet(me)
-    arriving = to_owner(me, cot_ref, cots_ref, c_ss, c_rs, local.at[0])
-    leaving = to_home(me, out_ref, half_ref, h_ss, h_rs, local.at[1])
+    mine = me.t * dp
+    early = early_blocks(dp)
+    arriving = [pltpu.make_async_copy(cot_ref.at[mine + me.i], cots_ref.at[me.i], local.at[0])]
+    leaving, passing = [], []
+    partner = (me.i, 1 - me.t)
+    for k in range(1, dp):
+        j, back = lax.rem(me.i + k, dp), lax.rem(me.i + dp - k, dp)
+        if k <= early:
+            arriving.append(pltpu.make_async_copy(cota_ref.at[back], cots_ref.at[back], c_ss.at[k]))
+        else:
+            arriving.append(remote(cot_ref.at[mine + j], cots_ref.at[me.i], c_ss.at[k], c_rs.at[k], (j, me.t)))
+        leaving.append(remote(out_ref.at[j], home_ref.at[mine + me.i], h_ss.at[k], h_rs.at[k], (j, me.t)))
+        if k < late_blocks(dp):
+            passing.append(remote(home_ref.at[mine + back], home_ref.at[mine + back], f_ss.at[k], f_rs.at[k], partner))
+    kept = pltpu.make_async_copy(out_ref.at[me.i], home_ref.at[mine + me.i], local.at[1])
+    across = remote(out_ref.at[me.i], home_ref.at[mine + me.i], f_ss.at[0], f_rs.at[0], partner)
     start_all(arriving)
-    bo, g1, s1, bf, g2, s2 = [r[...].astype(F32) for r in (bo_in, g1_in, s1_in, bf_in, g2_in, s2_in)]
+    bo, g1, s1, bf, g2, s2 = [
+        r[...].astype(F32).reshape(1, width) for r in (bo_in, g1_in, s1_in, bf_in, g2_in, s2_in)]
     bi = [side_row(small_ref, t, ROWS_BI, units // 128) for t in range(tn)]
     vec_ref[...] = jnp.zeros_like(vec_ref)
     bsum_ref[...] = jnp.zeros_like(bsum_ref)
@@ -748,28 +833,51 @@
             dc_ref[at, t * cols : (t + 1) * cols] = nn(low1, wo_ref[t]).astype(BF)
         return carry
 
+    wait_all(loads)
     lax.fori_loop(0, length // size, forward, 0)
     start_all(leaving)
+    kept.start()
+    across.start()
     wait_all(arriving)
-    lax.fori_loop(0, length // size, backward, 0)
-
+    n_back = length // size
+    done = 0
+    for i in range(n_back):
+        backward(i, 0)
+        upto = len(passing) * (i + 1) // n_back
+        for k in range(done, upto):
+            leaving[k].wait()
+            passing[k].start()
+        done = upto
+
+    outs = [Fetch(gr1_ref, gr1_out, move.at[5]).start(), Fetch(dc_ref, dc_out, move.at[6]).start()]
     turn_ref[...] = turn(gr2_ref[...])
     for t in range(tn):
         for c in range(0, units, chunk):
             own = slice(t * units + c, t * units + c + chunk)
             dwf_ref[t, :, c : c + chunk] = nn(turn_ref[...], act_ref[:, own]).astype(BF)
+    outs.append(Fetch(dwf_ref, dwf_out, move.at[7]).start())
     turn_ref[...] = turn(hid_ref[...])
     for t in range(tn):
         for c in range(0, units, chunk):
             own = slice(t * units + c, t * units + c + chunk)
             dwi_ref[t, :, c : c + chunk] = nn(turn_ref[...], gi_ref[:, own]).astype(BF)
+    outs.append(Fetch(dwi_ref, dwi_out, move.at[8]).start())
     turn_ref[...] = turn(gr1_ref[...])
     for t in range(tn):
         dwo_ref[t] = nn(turn_ref[...], ctx_ref[:, t * cols : (t + 1) * cols]).astype(BF)
-    wait_all(leaving)
-
-
-def call_feed(dp, x, ctx, wo, wi, wf, vectors, small, cot):
+    outs.append(Fetch(dwo_ref, dwo_out, move.at[9]).start())
+    wait_all(leaving[done:])
+    kept.wait()
+    across.wait()
+    wait_all(passing)
+    wait_all(outs)
+
+
+def late_blocks(dp):
+    return dp // 2
+
+
+def call_feed(dp, x, ctx, wo, wi, wf, vectors, small, cot, cota):
     length, width = x.shape
     tn, _, cols = wo.shape
     units = wi.shape[2]
@@ -777,27 +885,41 @@
     big = s((length, width), BF)
     blocks = (dp,) + cot.shape[1:]
     outs = (big, big, s((tn, width, cols), BF), s((tn, width, units), BF), s((tn, width, units), BF),
-            s((6, 8, width), F32), s((8, tn * units), F32), s(blocks, BF))
+            s((6, 8, width), F32), s((8, tn * units), F32), s((tn * dp,) + blocks[1:], BF))
     vm = pltpu.VMEM
     return pl.pallas_call(
         functools.partial(feed, dp),
         out_shape=outs,
-        in_specs=[VM] * 12 + [ANY],
-        out_specs=tuple([VM] * 7 + [ANY]),
+        in_specs=[ANY] * 5 + [VM] * 7 + [ANY] * 2,
+        out_specs=tuple([ANY] * 5 + [VM] * 2 + [ANY]),
         scratch_shapes=[vm((length, tn * units), BF), vm((length, tn * units), BF), vm((length, width), BF),
                         vm((length, width), BF), vm((width, length), BF), vm((length, width), F32),
                         vm((length, width), F32), vm((length, 1), F32), vm((length, 1), F32), vm(blocks, BF),
-                        vm(blocks, BF)] + sems(dp) + sems(dp) + [DMA((2,))],
-        compiler_params=params(2, 62),
+                        vm(blocks, BF)] + [vm(o.shape, o.dtype) for o in (x, ctx, wo, wi, wf) + outs[:5]]
+        + sems(dp) * 3 + [DMA((2,)), DMA((10,))],
+        compiler_params=params(2, TOP),
         name="feed_forward",
-    )(x, ctx, wo, wi, wf, *vectors, small, cot)
-
-
-def attend_backward(dp, x_ref, w_ref, ids_ref, small_ref, q_ref, k_ref, v_ref, near_ref, far_ref, lq_ref, lk_ref, mix_ref,
-                    sum_ref, ker_ref, z_ref, a_ref, v2_ref, w2_ref, dc_ref, gr1_ref, dwo_in, dwi_in, dwf_in, half_ref,
-                    gtok_ref, dw_ref, vecq_ref, vecv_ref, gtap_ref, go_ref, gi_ref, gf_ref, home_ref,
+    )(x, ctx, wo, wi, wf, *vectors, small, cot, cota)
+
+
+NORTH_LANE = 3
+
+
+def row_of(column):
+    return turn(jnp.broadcast_to(column, (column.shape[0], 128)))[0:1, :]
+
+
+def attend_backward(dp, ids_ref, small_ref, lq_ref, lk_ref, mix_ref, sum_ref, ker_ref,
+                    x_in, w_in, q_in, k_in, v_in, near_in, far_in, z_in, a_in, v2_in, w2_in, dc_in, gr1_in,
+                    dwo_in, dwi_in, dwf_in, home_in,
+                    gtok_ref, dw_ref, vecs_ref, gtap_ref, go_ref, gi_ref, gf_ref, home_ref,
+                    x_ref, w_ref, q_ref, k_ref, v_ref, near_ref, far_ref, z_ref, a_ref, v2_ref, w2_ref, dc_ref, gr1_ref,
                     pre_ref, glq_ref, glk_ref, gsum_ref, gz_ref, gk_ref, padv_ref, padc_ref, xt_ref,
-                    g_ss, g_rs, y_ss, y_rs, local, *bufs):
+                    g_ss, g_rs, y_ss, y_rs, local, move, *bufs):
+    near_l, dc_l, z_l, a_l, v2_l, w2_l, far_l, q_l, k_l, v_l, x_l, w_l, gr1_l = [
+        Fetch(a, b, move.at[k]).start() for k, (a, b) in enumerate((
+            (near_in, near_ref), (dc_in, dc_ref), (z_in, z_ref), (a_in, a_ref), (v2_in, v2_ref), (w2_in, w2_ref),
+            (far_in, far_ref), (q_in, q_ref), (k_in, k_ref), (v_in, v_ref), (x_in, x_ref), (w_in, w_ref), (gr1_in, gr1_ref)))]
     length, width = x_ref.shape
     tn = w_ref.shape[0]
     cols = width // tn
@@ -813,22 +935,17 @@
     lanes = []
     for k, (src, lo, w, dst) in enumerate(plan):
         lanes.append(reduce_lane(me, src, lo, w, bufs[5 * k : 5 * k + 5], Sub(g_ss, k * n), Sub(g_rs, k * n), local.at[k],
-                                 [(dst, lo, 0, w)]))
-    quarter = dp // 4
+                                 [(dst, lo, 0, w)], k == NORTH_LANE))
     sides = []
-    for k in range(4):
-        here, there = pl.ds(k * quarter, quarter), pl.ds(me.t * dp + k * quarter, quarter)
-        sides.append(remote(half_ref.at[here], home_ref.at[there], y_ss.at[k], y_rs.at[k], (me.i, 1 - me.t)))
-    kept = pltpu.make_async_copy(half_ref, home_ref.at[pl.ds(me.t * dp, dp)], local.at[5])
+    for k in range(late_blocks(dp), dp):
+        j = me.t * dp + lax.rem(me.i + dp - k, dp)
+        sides.append(remote(home_ref.at[j], home_ref.at[j], y_ss.at[k], y_rs.at[k], (me.i, 1 - me.t)))
     greet(me, False)
-    for lane in lanes:
-        lane[0]()
-    kept.start()
-    sides[0].start()
-    sides[1].start()
-    tick = Ticks([lanes[0][1], lanes[1][1], lanes[2][1], lanes[3][1], lanes[4][1], lanes[0][2], lanes[1][2], sides[2].start,
-                  lanes[0][3], lanes[2][2], lanes[1][3], lanes[3][2], sides[3].start, lanes[4][2], lanes[2][3], lanes[3][3],
-                  lanes[4][3]])
+    for k in (3, 0, 1, 2, 4):
+        lanes[k][0]()
+    tick = Ticks([lanes[3][1], lanes[0][1], lanes[1][1], lanes[2][1], lanes[4][1]] + [c.start for c in sides]
+                 + [lanes[0][2], lanes[3][2], lanes[1][2], lanes[0][3], lanes[2][2], lanes[1][3], lanes[3][3], lanes[4][2],
+                    lanes[2][3], lanes[4][3]])
     ids = ids_ref[pl.ds(own_sequence(), 1), :]
     member = jnp.where(lax.broadcasted_iota(jnp.int32, (LAND, length), 0) == ids, 1.0, 0.0).astype(F32)
     count = jnp.sum(member, axis=1, keepdims=True)
@@ -836,16 +953,19 @@
     valid = ids < LAND
     eye = pair_eye()
 
+    near_l.wait()
+    dc_l.wait()
     for g in range(groups):
         own = slice(g * 256, (g + 1) * 256)
         gsum_ref[:, own] = gather_diag(nn(near_ref[own, :], dc_ref[:, own]))
+    tick(5 + len(sides))
+    wait_all([z_l, a_l, v2_l, w2_l])
     for p in range(pairs):
         own = slice(p * 128, (p + 1) * 128)
         gmix = gsum_ref[:, own]
         gz_ref[:, own] = pair_nt(gmix, sum_ref[:, own])
         gsum_ref[:, own] = pair_nn(pair_turn(z_ref[ITERS, :, own]), gmix)
 
-    tick(5)
     gk_ref[...] = jnp.zeros_like(gk_ref)
 
     def iterate(m, carry):
@@ -866,10 +986,9 @@
             gz_ref[:, own] = pair_nt(grad, w2) + pair_nn(pair_turn(kernel), da)
         return carry
 
-    lax.fori_loop(0, ITERS // 2, iterate, 0)
+    lax.fori_loop(0, ITERS, iterate, 0)
     tick(1)
-    lax.fori_loop(ITERS // 2, ITERS, iterate, 0)
-    tick(2)
+    wait_all([far_l, q_l, k_l, v_l])
 
     for p in range(pairs):
         own = slice(p * 128, (p + 1) * 128)
@@ -925,18 +1044,20 @@
             gram = pltpu.roll(gram, 0, 1, stride=1, stride_axis=0)
             gtap_ref[4 * g + h : 4 * g + h + 1, :] = jnp.sum(gram, axis=0, keepdims=True)
         dv = dv + jnp.where(valid, jnp.concatenate(parts, axis=0), 0.0)
-        vecq_ref[own, :] = jnp.sum(dq, axis=1, keepdims=True)
-        vecv_ref[own, :] = jnp.sum(dv, axis=1, keepdims=True)
+        vecs_ref[0:1, own] = row_of(jnp.sum(dq, axis=1, keepdims=True))
+        vecs_ref[1:2, own] = row_of(jnp.sum(dv, axis=1, keepdims=True))
         for lower in range(0, 256, 128):
             c = g * 256 + lower
             t, r = c // cols, c % cols
             pre_ref[t, r : r + 128, :] = dq[lower : lower + 128].astype(BF)
             pre_ref[t, cols + r : cols + r + 128, :] = dk[lower : lower + 128].astype(BF)
             pre_ref[t, 2 * cols + r : 2 * cols + r + 128, :] = dv[lower : lower + 128].astype(BF)
-        tick(2)
-
+        if g > 0:
+            tick(1)
+
+    wait_all([x_l, w_l, gr1_l])
     xt_ref[...] = turn(x_ref[...])
-    tick(2)
+    tick(1)
     for t in range(tn):
         dw_ref[t] = nt(xt_ref[...], pre_ref[t]).astype(BF)
     tick(2)
@@ -951,34 +1072,37 @@
     for lane in lanes:
         lane[4]()
     wait_all(sides)
-    kept.wait()
-
-
-def call_attend_backward(dp, x, w, ids, small, saved, dc, gr1, dwo, dwi, dwf, half):
+
+
+def call_attend_backward(dp, x, w, ids, small, saved, dc, gr1, dwo, dwi, dwf, home):
+    q, k, v, near, far, lq, lk, mix, summ, ker, z, a, v2, w2 = saved
     length, width = x.shape
     tn = w.shape[0]
     cols = width // tn
     s = jax.ShapeDtypeStruct
     depth, units = dwi.shape[4:]
-    outs = (s(half.shape, BF), s((tn, width, 3 * cols), BF), s((width, 1), F32), s((width, 1), F32),
+    outs = (s((dp,) + home.shape[1:], BF), s((tn, width, 3 * cols), BF), s((8, width), F32),
             s((width // LAND, 512), F32), s((depth, cols), F32), s((depth, units), F32), s((depth, units), F32),
-            s((tn * dp,) + half.shape[1:], BF))
-    args = (x, w, ids, small, *saved, dc, gr1, dwo, dwi, dwf, half)
+            s(home.shape, BF))
+    little = (ids, small, lq, lk, mix, summ, ker)
+    large = (x, w, q, k, v, near, far, z, a, v2, w2, dc, gr1)
+    args = little + large + (dwo, dwi, dwf, home)
     vm = pltpu.VMEM
-    little = vm((LAND, width), F32)
+    mini = vm((LAND, width), F32)
     n = 5 * reduce_count(dp)
-    scratch = [vm((tn, 3 * cols, length), BF)] + [little] * 5
+    scratch = [vm(b.shape, b.dtype) for b in large] + [vm((tn, 3 * cols, length), BF)] + [mini] * 5
     scratch += [vm((256, length + 256), BF), vm((256, length + 256), BF), vm((width, length), BF)]
-    scratch += sems(n) + sems(4) + [DMA((6,))]
-    for wide in (units // 2,) * 4 + (cols,):
-        scratch += reduce_bufs(dp, tn, depth, wide)
+    scratch += sems(n) + sems(dp) + [DMA((5,)), DMA((len(large),))]
+    for k, wide in enumerate((units // 2,) * 4 + (cols,)):
+        scratch += reduce_bufs(dp, tn, depth, wide, k == NORTH_LANE)
     return pl.pallas_call(
         functools.partial(attend_backward, dp),
         out_shape=outs,
-        in_specs=[VM] * (len(args) - 4) + [ANY] * 4,
-        out_specs=tuple([VM] * 8 + [ANY]),
+        in_specs=[VM] * len(little) + [ANY] * (len(args) - len(little)),
+        out_specs=tuple([VM] * 7 + [ANY]),
         scratch_shapes=scratch,
-        compiler_params=params(3, 62),
+        input_output_aliases={len(args) - 1: 7},
+        compiler_params=params(3, TOP),
         name="attend_backward",
     )(*args)
 
@@ -990,10 +1114,7 @@
     part, width = tokens.shape[1:]
     length = dp * part
     cols = w_query.shape[1]
-    units = w_inner.shape[1]
-    heads, taps = conv_taps.shape
-    row = lambda v: v.reshape(1, -1)
-    vectors = [row(v) for v in (b_out, first_gain, first_shift, b_outer, second_gain, second_shift)]
+    vectors = [b_out, first_gain, first_shift, b_outer, second_gain, second_shift]
 
     def join(w):
         return w.reshape(tn, width, w.shape[-1])
@@ -1002,33 +1123,23 @@
         return g.reshape(tn, dp // 4, 2, 2, width // dp, g.shape[2])
 
     rows, wqkv, wout, small = call_bring(
-        dp, tn, tokens, w_query, w_key, w_value, w_out, row(b_query), row(b_value), row(b_inner), conv_taps
+        dp, tn, tokens, w_query, w_key, w_value, w_out, b_query, b_value, b_inner, conv_taps
     )
     rows = rows.reshape(length, width)
     wqkv, wout = join(wqkv), join(wout)
-    q, k, v, near, far, ctx, *rest_saved, wi, wf = call_attend_forward(
-        dp, rows, wqkv, small, landmark_ids, w_inner, w_outer
+    q, k, v, near, far, ctx, *rest_saved, wi, wf, cota = call_attend_forward(
+        dp, rows, wqkv, small, landmark_ids, w_inner, w_outer, cotangent
     )
-    gr1, dc, dwo, dwi, dwf, vec, bsum, half = call_feed(
-        dp, rows, ctx, wout, join(wi), join(wf), vectors, small, cotangent
+    gr1, dc, dwo, dwi, dwf, vec, bsum, home = call_feed(
+        dp, rows, ctx, wout, join(wi), join(wf), vectors, small, cotangent, cota
     )
-    grad_rows, dwqkv, gbq, gbv, gtap, go, gi, gf, out_home = call_attend_backward(
-        dp, rows, wqkv, landmark_ids, small, (q, k, v, near, far, *rest_saved), dc, gr1, cut(dwo), cut(dwi), cut(dwf), half
+    grad_rows, dwqkv, vecs, gtap, go, gi, gf, out_home = call_attend_backward(
+        dp, rows, wqkv, landmark_ids, small, (q, k, v, near, far, *rest_saved), dc, gr1, cut(dwo), cut(dwi), cut(dwf), home
     )
-    share = width // dp
-    norms = jnp.sum(vec, axis=1).reshape(6, dp, share).transpose(1, 0, 2).reshape(dp, 6 * share)
-    norms = jnp.pad(norms, ((0, 0), (0, 1024 - 6 * share))).reshape(dp, 8, 128)
-    rest = jnp.concatenate(
-        [gbq.reshape(tn, cols), gbv.reshape(tn, cols), jnp.sum(bsum, axis=0).reshape(tn, units),
-         gtap[:, FLIP_AT : FLIP_AT + taps].reshape(tn, heads * taps)], axis=1)
-    rest = jnp.pad(rest, ((0, 0), (0, 24 * 128 - rest.shape[1]))).reshape(tn, 24, 128)
-    grad_home, gq, gk, gv, nsum, rsum = call_carry_home(dp, tn, grad_rows, cut(dwqkv), norms, rest)
-    n = nsum.reshape(-1)[: 6 * share].reshape(6, share)
-    r = rsum.reshape(-1)
-    at = 2 * cols + units
-    return (out_home, grad_home, gq, gk, gv, r[:cols], r[cols : 2 * cols],
-            r[at : at + heads * taps].reshape(heads, taps), go, n[0], n[1], n[2], gi, r[2 * cols : at], gf,
-            n[3], n[4], n[5])
+    grad_home, gq, gk, gv, gbq, gbv, gtaps, gbi, gbo, gg1, gs1, gbf, gg2, gs2 = call_carry_home(
+        dp, tn, grad_rows, cut(dwqkv), vec, bsum, vecs, gtap, conv_taps
+    )
+    return (out_home, grad_home, gq, gk, gv, gbq, gbv, gtaps, go, gbo, gg1, gs1, gi, gbi, gf, gbf, gg2, gs2)
 
 
 def solution(mesh):

time: 436 us -> 398 us (0.913)
  local copies, waits for them, and re-layouts: 34.3 us -> 15.1 us
  Pallas kernels: 390 us -> 374 us
    pallas_call x1, Pallas kernels: 117 us -> 90.6 us  [call_attend_backward(): pl.pallas_call(functools.partial(attend_backward, dp), out_shape=outs, in...]
    reshape x16 -> x0, local copies, waits for them, and re-layouts: 10.6 us -> none  [the longest x9 9.63 us: local(): row = lambda v: v.reshape(1, -1)]
    unnamed x43 -> x52, local copies, waits for them, and re-layouts: 21.2 us -> 15.1 us
    pallas_call x1, Pallas kernels: 71.8 us -> 76.5 us  [call_attend_forward(): pl.pallas_call(functools.partial(attend_forward, dp), out_shape=outs, in_...]
where the time goes in v4:
time: 398 us; the launch traced here: 390 us
  Pallas kernels  374 us (94%)
  local copies, waits for them, and re-layouts  15.1 us (4%)
    pallas_call x1, Pallas kernels, call_attend_backward(): pl.pallas_call(functools.partial(attend_backward, dp), out_shape=outs, in...  90.6 us
    pallas_call x1, Pallas kernels, call_feed(): pl.pallas_call(functools.partial(feed, dp), out_shape=outs, in_specs=[ANY...  77.4 us
    pallas_call x1, Pallas kernels, call_attend_forward(): pl.pallas_call(functools.partial(attend_forward, dp), out_shape=outs, in_...  76.5 us
    pallas_call x1, Pallas kernels, call_carry_home(): pl.pallas_call(functools.partial(carry_home, dp, tn), out_shape=outs, in_...  72.6 us
    pallas_call x1, Pallas kernels, call_bring(): pl.pallas_call(functools.partial(bring, dp, tn), out_shape=outs, in_specs...  56.4 us
    unnamed x52, local copies, waits for them, and re-layouts  15.1 us

profile of v4, /device:TPU:0, one launch (start us, length us, event | category | flops | bytes accessed | tf_op | source)
XLA Modules:
  0.0 389.9 jit_solution(11238935479995772103)
XLA Ops:
  0.7 56.4 %bring.1 = (bf16[16,64,768]{2,1,0:T(8,128)(2,1)}, bf16[2,4,2,2,48,1152]{5,4,3,2,1,0:T(8,128)(2,1)}, bf16[2,4,2,2,48,384]{5,4,3,2,1,0:T(8,128)(2,1)}, f32[2,32,128]{2,1,0:T(8,128)}) custom-call(bf16[32,64,768]{2,1,0:T(8,128)(2,1)} %tok.1, bf16[48,384]{1,0:T(8,128)(2,1)} %wq.1, bf16[48,384]{1,0:T(8,128)(2,1)} %wk.1, bf16[48,384]{1,0:T(8,128)(2,1)} %wv.1, ...), custom_call_target="tpu_custom_call" | custom-call | tf_op jit(solution)/shard_map/bring/pallas_call | solution.py:282
  57.1 76.5 %attend_forward.1 = (bf16[1024,768]{1,0:T(8,128)(2,1)}, bf16[1024,768]{1,0:T(8,128)(2,1)}, bf16[1024,768]{1,0:T(8,128)(2,1)}, bf16[768,1024]{1,0:T(8,128)(2,1)},...) custom-call(bf16[1024,768]{1,0:T(8,128)(2,1)} %bitcast.9, ...), custom_call_target="tpu_custom_call" | custom-call | tf_op jit(solution)/shard_map/attend_forward/pallas_call | solution.py:688
  133.7 77.4 %feed_forward.1 = (bf16[1024,768]{1,0:T(8,128)(2,1)}, bf16[1024,768]{1,0:T(8,128)(2,1)}, bf16[2,768,384]{2,1,0:T(8,128)(2,1)}, bf16[2,768,1536]{2,1,0:T(8,128)(2...) custom-call(bf16[1024,768]{1,0:T(8,128)(2,1)} %bitcast.10, ...), custom_call_target="tpu_custom_call" | custom-call | tf_op jit(solution)/shard_map/feed_forward/pallas_call | solution.py:890
  211.0 90.6 %attend_backward.1 = (bf16[16,64,768]{2,1,0:T(8,128)(2,1)}, bf16[2,768,1152]{2,1,0:T(8,128)(2,1)}, f32[8,768]{1,0:T(8,128)}, f32[12,512]{1,0:T(8,128)}, f32[48,3...) custom-call(s32[32,1024]{1,0:T(8,128)} %ids_ref.3, ...), custom_call_target="tpu_custom_call", output_to_operand_aliasing={{7}: (23, {})} | custom-call | tf_op jit(solution)/shard_map/attend_backward/pallas_call | solution.py:1098
  301.6 72.6 %carry_home.1 = (bf16[32,64,768]{2,1,0:T(8,128)(2,1)}, f32[48,384]{1,0:T(8,128)}, f32[48,384]{1,0:T(8,128)}, f32[48,384]{1,0:T(8,128)}, f32[384]{0:T(512)}, /*in...) custom-call(bf16[16,64,768]{2,1,0:T(8,128)(2,1)} %get-tuple-element., ...), custom_call_target="tpu_custom_call" | custom-call | tf_op jit(solution)/shard_map/carry_home/pallas_call | solution.py:393
  374.2 0.0 copy-start
  374.2 4.0 %copy.57 = bf16[32,64,768]{2,1,0:T(8,128)(2,1)} copy(bf16[32,64,768]{2,1,0:T(8,128)(2,1)} %get-tuple-element.140) | data formatting | bytes 6291456
  378.3 0.0 copy-done
  378.3 0.0 copy-start.10
  378.3 0.0 copy-start.9
  378.3 0.0 copy-start.8
  378.3 0.0 copy-start.3
  378.3 0.0 copy-start.16
  378.3 0.0 copy-start.15
  378.4 0.0 copy-start.14
  378.4 0.0 copy-start.2
  378.4 0.0 copy-start.7
  378.4 0.0 copy-start.1
  378.4 1.7 copy.58
  380.1 0.0 copy-done.6
  380.1 0.6 copy.59
  380.7 0.0 copy-done.5
  380.7 0.6 copy.60
  381.3 0.0 copy-done.4
  381.3 0.6 copy.61
  382.0 0.0 copy-done.10
  382.0 0.6 copy.62
  382.6 0.0 copy-done.9
  382.6 0.6 copy.63
  383.1 0.0 copy-done.8
  383.1 0.6 copy.64
  383.7 0.0 copy-done.3
  383.7 0.6 copy.65
  384.4 0.0 copy-done.16
  384.4 0.5 copy.66
  384.9 0.0 copy-done.15
  384.9 0.5 copy.67
  385.4 0.0 copy-done.14
  385.4 0.5 copy.68
  385.9 0.0 copy-done.2
  385.9 0.7 copy.69
  386.6 0.0 copy-done.7
  386.6 0.6 copy.70
  387.2 0.0 copy-done.1
  387.2 0.7 copy.71
  388.0 0.5 copy.72
  388.5 0.5 copy.73
  389.0 0.5 copy.74
  (9 shorter events, 0.0 us)
Async XLA Ops:
  374.2 4.0 %copy-start = (bf16[32,64,768]{2,1,0:T(8,128)(2,1)S(1)}, bf16[32,64,768]{2,1,0:T(8,128)(2,1)}, u32[]{:S(2)}) copy-start(bf16[32,64,768]{2,1,0:T(8,128)(2,1)} %get-tuple-element.141) | copy-start | bytes 9437188
  378.3 1.8 copy-start.6
  378.3 2.4 copy-start.5
  378.3 3.1 copy-start.4
  378.3 3.7 copy-start.10
  378.3 4.3 %copy-start.9 = (f32[384]{0:T(512)S(1)}, f32[384]{0:T(512)}, u32[]{:S(2)}) copy-start(f32[384]{0:T(512)} %get-tuple-element.146) | copy-start | bytes 4612
  378.3 4.8 %copy-start.8 = (f32[6,33]{1,0:T(8,128)S(1)}, f32[6,33]{1,0:T(8,128)}, u32[]{:S(2)}) copy-start(f32[6,33]{1,0:T(8,128)} %get-tuple-element.147) | copy-start | bytes 2380
  378.3 5.4 %copy-start.3 = (f32[48,384]{1,0:T(8,128)S(1)}, f32[48,384]{1,0:T(8,128)}, u32[]{:S(2)}) copy-start(f32[48,384]{1,0:T(8,128)} %get-tuple-element.148) | copy-start | bytes 221188
  378.3 6.0 %copy-start.16 = (f32[48]{0:T(128)S(1)}, f32[48]{0:T(128)}, u32[]{:S(2)}) copy-start(f32[48]{0:T(128)} %get-tuple-element.149) | copy-start | bytes 580
  378.3 6.5 %copy-start.15 = (f32[48]{0:T(128)S(1)}, f32[48]{0:T(128)}, u32[]{:S(2)}) copy-start(f32[48]{0:T(128)} %get-tuple-element.150) | copy-start | bytes 580
  378.4 7.1 %copy-start.14 = (f32[48]{0:T(128)S(1)}, f32[48]{0:T(128)}, u32[]{:S(2)}) copy-start(f32[48]{0:T(128)} %get-tuple-element.151) | copy-start | bytes 580
  378.4 7.6 %copy-start.2 = (f32[48,1536]{1,0:T(8,128)S(1)}, f32[48,1536]{1,0:T(8,128)}, u32[]{:S(2)}) copy-start(f32[48,1536]{1,0:T(8,128)} %get-tuple-element.152) | copy-start | bytes 884740
  378.4 8.3 %copy-start.7 = (f32[1536]{0:T(1024)S(1)}, f32[1536]{0:T(1024)}, u32[]{:S(2)}) copy-start(f32[1536]{0:T(1024)} %get-tuple-element.153) | copy-start | bytes 18436
  378.4 8.9 %copy-start.1 = (f32[48,1536]{1,0:T(8,128)S(1)}, f32[48,1536]{1,0:T(8,128)}, u32[]{:S(2)}) copy-start(f32[48,1536]{1,0:T(8,128)} %get-tuple-element.154) | copy-start | bytes 884740
  380.1 7.9 %copy-start.13 = (f32[48]{0:T(128)S(1)}, f32[48]{0:T(128)}, u32[]{:S(2)}) copy-start(f32[48]{0:T(128)} %get-tuple-element.155) | copy-start | bytes 580
  380.1 8.4 %copy-start.12 = (f32[48]{0:T(128)S(1)}, f32[48]{0:T(128)}, u32[]{:S(2)}) copy-start(f32[48]{0:T(128)} %get-tuple-element.156) | copy-start | bytes 580
  380.1 8.9 %copy-start.11 = (f32[48]{0:T(128)S(1)}, f32[48]{0:T(128)}, u32[]{:S(2)}) copy-start(f32[48]{0:T(128)} %get-tuple-element.157) | copy-start | bytes 580
